TPU v7x, 768 devices: a whole 4x8x12 slice. The times are simulated.
768 devices in a mesh: slide: 8 (over x, core), gy: 12 (over z), gx: 8 (over y).
Axes of the slice: x: 4, y: 8, z: 12, core: 2. Of those that a mesh axis runs over, the one named last changes fastest.
Arguments:
- features: bfloat16 [8, 192, 512, 256], P('slide', 'gy', 'gx'), may hold values from -6 to 6
- depth_weight: bfloat16 [3, 3, 256], replicated, may hold values from -2 to 2
- point_weight: bfloat16 [256, 256], replicated, may hold values from -0.375 to 0.375
- classifier: float32 [2, 256, 256], replicated
- valid_count: int32 [8, 12, 8], P('slide', 'gy', 'gx'), may hold values from 512 to 1024, as said below
- labels: int32 [8], P('slide'), may hold values from 0 to 1
Outputs:
- loss_value: float32 [], replicated
- depth_gradient: float32 [3, 3, 256], replicated
- point_gradient: float32 [256, 256], replicated
- classifier_gradient: float32 [2, 256, 256], replicated
- feature_gradient: bfloat16 [8, 192, 512, 256], P('slide', 'gy', 'gx')
Inputs may be any that keep to these rules, and one draw needn't show every extreme that they name: `valid_count`: every tile holds 512 or more valid pixels, and tile 0 of every slide holds exactly 1024.
All inputs are finite; a program needn't handle non-finite values.
Results may differ from a plain program's by a relative error of at most 0.0064.
The roundings to bfloat16 on the way count: a program that leaves them out, or rounds other values in their place, can miss the bound.
Values may be sent and summed in bfloat16 or wider, within the bound.
No kernel may reach another device: no remote copies, remote signals or barrier semaphores. Data moves between devices by JAX's collectives and lax.ppermute only.
A program may use at most 32 MiB of HBM per device.

v0:
```python
import jax
import jax.numpy as jnp
from jax import lax
from jax.sharding import PartitionSpec as P

ITERS = 5


def extended(block, sides, width):
    for axis, dim in sides:
        count = lax.axis_size(axis)
        forward = [(i, i + 1) for i in range(count - 1)]
        backward = [(target, source) for source, target in forward]
        low = lax.ppermute(
            lax.slice_in_dim(block, block.shape[dim] - width, None, axis=dim), axis, forward
        )
        high = lax.ppermute(lax.slice_in_dim(block, 0, width, axis=dim), axis, backward)
        block = jnp.concatenate([low, block, high], axis=dim)
    return block


def matmul_high(left, right):
    return jnp.dot(left, right, precision=lax.Precision.HIGHEST)


def cov_root(second_in, first_in, pixel_count):
    identity = jnp.eye(second_in.shape[0], dtype=second_in.dtype)
    mean_vec = first_in / pixel_count
    sigma = second_in / pixel_count - jnp.outer(mean_vec, mean_vec)
    trace_val = jnp.trace(sigma)
    ymat = sigma / trace_val
    zmat = identity
    for step_index in range(ITERS):
        middle = 0.5 * (3.0 * identity - matmul_high(zmat, ymat))
        ymat = matmul_high(ymat, middle)
        zmat = matmul_high(middle, zmat)
    return jnp.sqrt(trace_val) * ymat


def depthwise(padded, weights, height, width):
    result = jnp.zeros((height, width, padded.shape[2]), jnp.float32)
    for offset_row in range(3):
        for offset_col in range(3):
            result = result + padded[
                offset_row : offset_row + height, offset_col : offset_col + width
            ].astype(jnp.float32) * weights[offset_row, offset_col].astype(jnp.float32)
    return result


def per_device(features, depth_weight, point_weight, classifier, valid_count, labels):
    slides = lax.axis_size("slide")
    tile_block = features[0]
    height, width, channels = tile_block.shape
    padded = extended(tile_block, (("gy", 0), ("gx", 1)), 1)
    hidden = depthwise(padded, depth_weight, height, width).astype(jnp.bfloat16)
    flat_hidden = hidden.reshape(height * width, channels)
    point_out = jnp.dot(flat_hidden, point_weight, preferred_element_type=jnp.float32).astype(
        jnp.bfloat16
    )
    position = (
        lax.broadcasted_iota(jnp.int32, (height, width), 0) * width
        + lax.broadcasted_iota(jnp.int32, (height, width), 1)
    ).reshape(-1)
    pixel_mask = (position < valid_count[0, 0, 0]).astype(jnp.float32)
    masked = point_out * pixel_mask[:, None].astype(jnp.bfloat16)
    second_part = lax.dot_general(
        masked, point_out, (((0,), (0,)), ((), ())), preferred_element_type=jnp.float32
    )
    first_part = jnp.sum(masked.astype(jnp.float32), axis=0)
    count_part = jnp.sum(pixel_mask)
    second_sum, first_sum, pixel_count = lax.psum(
        (second_part, first_part, count_part), ("gy", "gx")
    )
    pooled, pullback = jax.vjp(
        lambda second_in, first_in: cov_root(second_in, first_in, pixel_count),
        second_sum,
        first_sum,
    )
    logits = jnp.tensordot(
        classifier, pooled, axes=([1, 2], [0, 1]), precision=lax.Precision.HIGHEST
    )
    log_peak = jnp.max(logits)
    log_total = log_peak + jnp.log(jnp.sum(jnp.exp(logits - log_peak)))
    class_probs = jnp.exp(logits - log_total)
    onehot = (jnp.arange(classifier.shape[0], dtype=jnp.int32) == labels[0]).astype(jnp.float32)
    loss_term = jnp.sum(onehot * (log_total - logits)) / slides
    logit_slope = (class_probs - onehot) / slides
    class_term = pooled[None] * logit_slope[:, None, None]
    back_pooled = jnp.tensordot(
        logit_slope, classifier, axes=(0, 0), precision=lax.Precision.HIGHEST
    )
    back_second, back_first = pullback(back_pooled)
    symmetric = back_second + back_second.T
    back_mapped = (
        pixel_mask[:, None]
        * (matmul_high(point_out.astype(jnp.float32), symmetric) + back_first[None, :])
    ).astype(jnp.bfloat16)
    back_hidden = jnp.dot(back_mapped, point_weight.T, preferred_element_type=jnp.float32).astype(
        jnp.bfloat16
    )
    point_term = lax.dot_general(
        flat_hidden, back_mapped, (((0,), (0,)), ((), ())), preferred_element_type=jnp.float32
    )
    back_grid = back_hidden.reshape(height, width, channels)
    rows_list = []
    for offset_row in range(3):
        cols_list = []
        for offset_col in range(3):
            cols_list.append(
                jnp.sum(
                    padded[
                        offset_row : offset_row + height, offset_col : offset_col + width
                    ].astype(jnp.float32)
                    * back_grid.astype(jnp.float32),
                    axis=(0, 1),
                )
            )
        rows_list.append(jnp.stack(cols_list))
    depth_term = jnp.stack(rows_list)
    back_pad = extended(back_grid, (("gy", 0), ("gx", 1)), 1)
    feature_sum = jnp.zeros((height, width, channels), jnp.float32)
    for offset_row in range(3):
        for offset_col in range(3):
            feature_sum = feature_sum + back_pad[
                2 - offset_row : 2 - offset_row + height, 2 - offset_col : 2 - offset_col + width
            ].astype(jnp.float32) * depth_weight[offset_row, offset_col].astype(jnp.float32)
    feature_gradient = feature_sum.astype(jnp.bfloat16)[None]
    class_total, loss_total = lax.psum((class_term, loss_term), "slide")
    point_total, depth_total = lax.psum((point_term, depth_term), ("slide", "gy", "gx"))
    return (loss_total, depth_total, point_total, class_total, feature_gradient)


def solution(mesh):
    placed = (P("slide", "gy", "gx", None), P(), P(), P(), P("slide", "gy", "gx"), P("slide"))
    return jax.shard_map(
        per_device,
        mesh=mesh,
        in_specs=placed,
        out_specs=(P(), P(), P(), P(), P("slide", "gy", "gx", None)),
        check_vma=False,
    )
```

profile of v0, /device:TPU:1, one launch (start us, length us, event | category | flops | bytes accessed | tf_op | source)
XLA Modules:
  0.0 868.5 jit_solution(6589940961632411110)
XLA Ops:
  8.1 4.8 collective-permute-start
  12.9 1.3 collective-permute-start.1
  15.8 2.4 collective-permute-done.1
  19.1 3.2 collective-permute-start.2
  25.1 1.8 collective-permute-done.3
  30.2 178.0 %all-reduce = (f32[256]{0:T(256)S(1)}, f32[]{:T(128)}) all-reduce(f32[256]{0:T(256)S(1)} %get-tuple-element.48, f32[]{:T(128)} %fusion.65), channel_id=1, replica_groups=mesh['slide'=8,'gy'=12,'gx'=8] {'gy','gx'}, use_global_device_ids=true, to_apply=%region_4.0 | all-reduce | flops 257 | bytes 2056 | tf_op jit(solution)/shard_map/psum | solution.py:71
  209.1 47.7 %all-reduce.5.cloned.1.call-done = f32[256,256]{1,0:T(8,128)} async-done(((f32[256,256]{1,0:T(8,128)}), f32[256,256]{1,0:T(8,128)}) %all-reduce.5.cloned.1.call-update) | async-done | bytes 262160 | tf_op jit(solution)/shard_map/psum | solution.py:71
  256.9 1.6 divide_subtract_fusion
  270.4 5.5 fusion.72
  275.8 1.3 exponential_reduce_fusion
  279.2 2.3 fusion.43
  291.5 19.5 %psum.52 = f32[]{:T(128)} all-reduce(f32[]{:T(128)S(6)} %div.59), channel_id=1, replica_groups=mesh['slide'=8,'gy'=12,'gx'=8] {'slide'}, use_global_device_ids=true, to_apply=%region_9.10 | all-reduce | flops 1 | bytes 8 | tf_op jit(solution)/shard_map/psum | solution.py:128
  311.0 1.7 fusion.49
  318.0 1.5 multiply_reduce_fusion.2
  321.8 1.4 fusion.1
  325.2 2.5 fusion.25
  327.7 2.5 collective-permute-start.4
  332.5 2.4 collective-permute-done.5
  336.2 4.0 collective-permute-start.7
  340.2 108.2 %psum.53 = f32[3,3,256]{2,1,0:T(4,128)} all-reduce(f32[3,3,256]{2,1,0:T(4,128)S(1)} %pad_maximum_fusion.12), channel_id=1, replica_groups=mesh['slide'=8,'gy'=12,'gx'=8] {'slide','gy','gx'}, use_global_device_ids=true, to_apply=%region_23.24 | all-reduce | flops 2304 | bytes 18432 | tf_op jit(solution)/shard_map/psum | solution.py:129
  448.8 1.6 fusion.42
  450.5 332.1 %all-reduce.7.cloned.1.call-done = f32[256,256]{1,0:T(8,128)} async-done(((f32[256,256]{1,0:T(8,128)}), f32[256,256]{1,0:T(8,128)}) %all-reduce.7.cloned.1.call-update) | async-done | bytes 262160 | tf_op jit(solution)/shard_map/psum | solution.py:129
  782.5 76.9 %all-reduce.9.cloned.1.call-done = f32[2,256,256]{2,1,0:T(8,128)} async-done(((f32[2,256,256]{2,1,0:T(8,128)}), f32[2,256,256]{2,1,0:T(8,128)}) %all-reduce.9.cloned.1.call-update) | async-done | bytes 524304 | tf_op jit(solution)/shard_map/psum | solution.py:128
  859.4 1.7 copy.82
  (151 shorter events, 41.6 us)
Async XLA Ops:
  7.2 263.2 %copy-start = (f32[2,256,256]{2,1,0:T(8,128)S(1)}, f32[2,256,256]{2,1,0:T(8,128)}, u32[]{:S(2)}) copy-start(f32[2,256,256]{2,1,0:T(8,128)} %param.9) | copy-start | bytes 1572868
  7.2 19.7 %copy-start.7 = (bf16[1,16,64,256]{3,2,1,0:T(8,128)(2,1)S(1)}, bf16[1,16,64,256]{3,2,1,0:T(8,128)(2,1)}, u32[]{:S(2)}) copy-start(bf16[1,16,64,256]{3,2,1,0:T(8,128)(2,1)} %param.6) | copy-start | bytes 1572868
  7.2 249.7 %all-reduce.5.cloned.1.call-start = ((), (), s32[]{:S(2)}) async-start(), calls=%async_computation | async-start | bytes 524288 | tf_op jit(solution)/shard_map/psum | solution.py:71
  8.1 7.7 collective-permute-start
  12.9 5.3 collective-permute-start.1
  19.1 5.9 collective-permute-start.2
  22.4 4.5 collective-permute-start.3
  30.2 752.3 %all-reduce.7.cloned.1.call-start = ((), (), s32[]{:S(2)}) async-start(), calls=%async_computation.1 | async-start | bytes 524288 | tf_op jit(solution)/shard_map/psum | solution.py:129
  258.5 3.9 copy-start.24
  268.6 1.8 copy-start.11
  270.3 5.5 copy-start.26
  278.6 2.9 copy-start.16
  279.2 2.7 copy-start.6
  288.7 1.7 copy-start.17
  289.3 21.7 %copy-start.14 = (f32[1,256,256]{2,0,1:T(1,128)S(1)}, f32[1,256,256]{2,0,1:T(1,128)}, u32[]{:S(2)}) copy-start(f32[1,256,256]{2,0,1:T(1,128)} %copy-done.13) | copy-start | bytes 786436
  319.5 2.3 copy-start.33
  321.8 2.2 copy-start.20
  325.1 6.4 copy-start.27
  325.1 534.3 %all-reduce.9.cloned.1.call-start = ((), (), s32[]{:S(2)}) async-start(), calls=%async_computation.2 | async-start | bytes 1048576 | tf_op jit(solution)/shard_map/psum | solution.py:128
  327.7 4.8 collective-permute-start.4
  330.2 4.7 collective-permute-start.5
  334.9 113.5 %collective-permute-start.6 = (bf16[18,1,256]{2,1,0:T(2,128)(2,1)S(1)}, bf16[18,1,256]{2,1,0:T(2,128)(2,1)S(1)}, u32[]{:S(2)}, u32[]{:S(2)}) collective-permute-start(bf16[18,1,256]{2,1,0:T(2,128)(2,1)S(1)} %get-tuple-element.25), channel_id=1, source_target_pairs={{1,0},{2,1},{3,2},{4,3},{5,4},{6,5},{7,6},{9,8},{10,9},{11,10},{12... | collective-permute-start | bytes 27656 | tf_op jit(solution)/shard_map/ppermute | solution.py:17
  336.2 112.2 %collective-permute-start.7 = (bf16[18,1,256]{2,1,0:T(2,128)(2,1)S(1)}, bf16[18,1,256]{2,1,0:T(2,128)(2,1)S(1)}, u32[]{:S(2)}, u32[]{:S(2)}) collective-permute-start(bf16[18,1,256]{2,1,0:T(2,128)(2,1)S(1)} %get-tuple-element.26), channel_id=1, source_target_pairs={{0,1},{1,2},{2,3},{3,4},{4,5},{5,6},{6,7},{8,9},{9,10},{10,11},{11... | collective-permute-start | bytes 27656 | tf_op jit(solution)/shard_map/ppermute | solution.py:14
  859.4 1.7 copy-start.28
  (21 other events, 22.1 us)
Sparse Core Ops, SparseCore 0:
  30.3 226.5 all-reduce.4
  325.2 457.2 all-reduce.6
  785.4 73.9 all-reduce.8
where the time goes:
time: 869 us; the launch traced here: 868 us
  waiting for transfers between devices  463 us (53%)
  blocking collectives  306 us (35%)
  matrix products  38.3 us (4%)
  between operations  21 us (2%)
  starting transfers between devices  19.8 us (2%)
  other arithmetic  14.2 us (2%)
    psum x1, waiting for transfers between devices, per_device(): lax.psum((point_term, depth_term), ('slide', 'gy', 'gx'))  332 us
    psum x1, blocking collectives, per_device(): lax.psum((second_part, first_part, count_part), ('gy', 'gx'))  178 us
    psum x1, blocking collectives, per_device(): lax.psum((point_term, depth_term), ('slide', 'gy', 'gx'))  108 us
    psum x1, waiting for transfers between devices, per_device(): class_total, loss_total = lax.psum((class_term, loss_term), 'slide')  76.9 us
    psum x1, waiting for transfers between devices, per_device(): lax.psum((second_part, first_part, count_part), ('gy', 'gx'))  47.7 us
    dot_general x41, matrix products, matmul_high(): return jnp.dot(left, right, precision=lax.Precision.HIGHEST)  25.3 us
    psum x1, blocking collectives, per_device(): class_total, loss_total = lax.psum((class_term, loss_term), 'slide')  19.5 us
  transfers between devices with their start and end apart: 11, of which 6 were waited for; matrix products, arithmetic and copies ran while one was open for 1% of the time, Pallas kernels for 0%

commit v1 on v0

v1 whole, which is shorter than its diff:
```python
import functools

import jax
import jax.numpy as jnp
from jax import lax
from jax.experimental import pallas as pl
from jax.experimental.pallas import tpu as pltpu
from jax.sharding import PartitionSpec as P

ITERS = 5
RIM = 2
LEFT = 8
LANES = 128
F32 = jnp.float32
BF16 = jnp.bfloat16
VMEM = pl.BlockSpec(memory_space=pltpu.VMEM)
SMEM = pl.BlockSpec(memory_space=pltpu.SMEM)
PARAMS = pltpu.CompilerParams(vmem_limit_bytes=40 * 1024 * 1024)


def iota(shape, dim):
    return lax.broadcasted_iota(jnp.int32, shape, dim)


def total(x):
    return jnp.sum(jnp.sum(x, axis=1, keepdims=True), axis=0, keepdims=True)


def dot(left, right):
    return jnp.dot(left, right, preferred_element_type=F32)


def split(x):
    high = x.astype(BF16)
    return high, (x - high.astype(F32)).astype(BF16)


def mm(left, right):
    lhs = jnp.concatenate([left[0], left[1], left[0]], axis=1)
    rhs = jnp.concatenate([right[0], right[0], right[1]], axis=0)
    return dot(lhs, rhs)


def stack(*pairs):
    return tuple(jnp.concatenate([pair[i] for pair in pairs], axis=0) for i in range(2))


def shifted(x, step):
    return pltpu.roll(x, step % x.shape[0], 0)


def tri_pack(full):
    half = full.shape[0] // 2
    row, col = iota((half, half), 0), iota((half, half), 1)
    first, upper, second = full[:half, :half], full[:half, half:], full[half:, half:]
    both = jnp.where(row <= col, first, second)
    diag = jnp.sum(jnp.where(row == col, second, 0.0), axis=0, keepdims=True)
    return upper, both, diag


def tri_unpack(upper, both, diag):
    half = both.shape[0]
    row, col = iota((half, half), 0), iota((half, half), 1)
    turned = both.T
    first = jnp.where(row <= col, both, turned)
    second = jnp.where(row > col, both, jnp.where(row == col, diag, turned))
    return jnp.concatenate(
        [jnp.concatenate([first, upper], axis=1), jnp.concatenate([upper.T, second], axis=1)],
        axis=0,
    )


def assemble(ext, tile, up, down, left, right):
    height, width, channels = tile.shape
    rows = height + 2 * RIM
    ext[:, 0:LEFT, :] = jnp.zeros((rows, LEFT, channels), F32)
    ext[:, LEFT + width : 2 * LEFT + width, :] = jnp.zeros((rows, LEFT, channels), F32)
    ext[RIM : RIM + height, LEFT : LEFT + width, :] = tile[...].astype(F32)
    ext[0:RIM, LEFT : LEFT + width, :] = up[...].astype(F32)
    ext[RIM + height : rows, LEFT : LEFT + width, :] = down[...].astype(F32)
    ext[:, LEFT - RIM : LEFT, :] = left[...].astype(F32)
    ext[:, LEFT + width : LEFT + width + RIM, :] = right[...].astype(F32)


def forward_kernel(
    planes, count, tile, up, down, left, right, weights, point, mapped, packed, ext, hidden, inner
):
    height, width, channels = tile.shape
    wide = ext.shape[1]
    assemble(ext, tile, up, down, left, right)
    valid = count[0]

    for lane in range(0, channels, LANES):
        part = slice(lane, lane + LANES)
        taps = [weights[k : k + 1, part] for k in range(9)]

        def body(r, carry, part=part, taps=taps):
            rows = [ext[r + a, :, part] for a in range(3)]
            cols = [sum(rows[a] * taps[3 * a + b] for a in range(3)) for b in range(3)]
            value = cols[1] + shifted(cols[0], 1) + shifted(cols[2], -1)
            hidden[pl.ds(pl.multiple_of(r * wide, 16), wide), part] = value.astype(BF16)

            @pl.when((r >= 1) & (r <= height))
            def _():
                raster = (r - 1) * width + iota((width, LANES), 0)
                kept = jnp.where(raster < valid, value[LEFT : LEFT + width], 0.0)
                start = pl.multiple_of((r - 1) * width, 16)
                inner[pl.ds(start, width), part] = kept.astype(BF16)

            return carry

        lax.fori_loop(0, height + 2, body, 0)

    mapped[...] = dot(hidden[...], point[...]).astype(BF16)
    kept = inner[...]
    gram = lax.dot_general(kept, kept, (((0,), (0,)), ((), ())), preferred_element_type=F32)
    sums = jnp.sum(kept.astype(F32), axis=0, keepdims=True)
    upper, both, diag = tri_pack(gram)
    chunks = packed.shape[1] // LANES
    spare = chunks * planes - 2 * LANES - 3
    flat = jnp.concatenate(
        [upper, both, diag, sums[:, :LANES], sums[:, LANES:], jnp.zeros((spare, LANES), F32)],
        axis=0,
    )
    for q in range(chunks):
        packed[:, q * LANES : (q + 1) * LANES] = flat[q * planes : (q + 1) * planes]


def plane_sum_kernel(count, terms, out):
    planes, lanes = terms.shape
    summed = jnp.sum(terms[...], axis=0, keepdims=True)
    out[:, :lanes] = jnp.broadcast_to(summed, (planes, lanes))
    out[:, lanes:] = jnp.full((planes, LANES), count[0].astype(F32))


def cov_kernel(
    grid_y, grid_x, slides, place, label, gathered, tile, up, down, left, right, weights, point,
    point_turned, classifier, mapped, gradient, sent, ext, back,
):
    height, width, channels = tile.shape
    planes = grid_y * grid_x
    wide = ext.shape[1]
    half = channels // 2
    chunks = gathered.shape[1] // LANES - 1
    pixels = (height + 2) * wide

    flat = jnp.concatenate(
        [gathered[:, q * LANES : (q + 1) * LANES] for q in range(chunks)], axis=0
    )
    counts = gathered[:, chunks * LANES : (chunks + 1) * LANES]
    inverse = 1.0 / jnp.sum(counts, axis=0, keepdims=True)[:, 0:1]
    gram = tri_unpack(flat[:half], flat[half : 2 * half], flat[2 * half : 2 * half + 1])
    sums = jnp.concatenate(
        [flat[2 * half + 1 : 2 * half + 2], flat[2 * half + 2 : 2 * half + 3]], axis=1
    )
    center = sums * inverse
    spread = jnp.broadcast_to(center, (channels, channels))
    moment = gram * inverse - spread * spread.T

    mixing, mixing_turned = point[...], point_turned[...]
    high, low = split(moment)
    moved = dot(
        jnp.concatenate([high, low], axis=1), jnp.concatenate([mixing, mixing], axis=0)
    )
    moved_pair = split(moved)
    sigma = dot(
        jnp.concatenate([mixing_turned, mixing_turned], axis=1),
        jnp.concatenate(moved_pair, axis=0),
    )
    sigma = 0.5 * (sigma + sigma.T)
    eye = iota((channels, channels), 0) == iota((channels, channels), 1)
    trace = total(jnp.where(eye, sigma, 0.0))
    start = sigma * (1.0 / trace)

    toward = classifier[0] - classifier[1]
    toward = toward + toward.T
    wmat, ymat, dw, dy = start, start, toward, toward
    for step in range(ITERS):
        w_pair, dw_pair = split(wmat), split(dw)
        if step == 0:
            square = mm(w_pair, w_pair)
            cross = mm(w_pair, dw_pair)
            yw, dyw = square, cross + cross.T
        else:
            first = mm(stack(w_pair, split(ymat), split(dy)), w_pair)
            second = mm(stack(w_pair, split(ymat)), dw_pair)
            square, yw = first[:channels], first[channels : 2 * channels]
            cross = second[:channels]
            dyw = first[2 * channels :] + second[channels:]
        ymat = 1.5 * ymat - 0.5 * yw
        dy = 1.5 * dy - 0.5 * dyw
        if step + 1 < ITERS:
            dsquare = cross + cross.T
            square_pair = split(square)
            third = mm(stack(square_pair, split(dsquare)), w_pair)
            cube = third[:channels]
            dcube = third[channels:] + mm(square_pair, dw_pair)
            wmat = 2.25 * wmat - 1.5 * square + 0.25 * cube
            dw = 2.25 * dw - 1.5 * dsquare + 0.25 * dcube

    root = jnp.sqrt(trace)
    pooled = root * ymat
    logit0 = total(classifier[0] * pooled)
    logit1 = total(classifier[1] * pooled)
    peak = jnp.maximum(logit0, logit1)
    lse = peak + jnp.log(jnp.exp(logit0 - peak) + jnp.exp(logit1 - peak))
    is_zero = label[0] == 0
    slope = jnp.where(is_zero, -jnp.exp(logit1 - lse), jnp.exp(logit0 - lse)) * (1.0 / slides)
    loss = (lse - jnp.where(is_zero, logit0, logit1)) * (1.0 / slides)

    level = 0.5 * total(toward * ymat) - total(dy * start)
    slant = (dy + jnp.where(eye, level, 0.0)) * (slope / root)
    slant = 0.5 * (slant + slant.T)
    point_term = mm(moved_pair, split(slant))
    class_term = slope * pooled
    class_term = 0.5 * (class_term + class_term.T)

    symmetric = slant * inverse
    sym_pair = split(symmetric)
    center_pair = split(jnp.broadcast_to(center, (8, channels)))
    mean = dot(
        jnp.concatenate(center_pair, axis=1), jnp.concatenate([mixing, mixing], axis=0)
    )
    offset = -mm(split(mean), sym_pair)[0:1]

    row_id = iota((planes, LANES), 0)
    spots = []
    for dy_ in (-1, 0, 1):
        for dx_ in (-1, 0, 1):
            near_y, near_x = place[0] + dy_, place[1] + dx_
            inside = (near_y >= 0) & (near_y < grid_y) & (near_x >= 0) & (near_x < grid_x)
            spot = jnp.where(inside, near_y * grid_x + near_x, -1)
            near = jnp.sum(jnp.where(row_id == spot, counts, 0.0), axis=0, keepdims=True)
            spots.append(near[:, 0:1])

    both = dot(mapped[...], sym_pair[0]) + dot(mapped[...], sym_pair[1]) + offset
    lane_col = iota((wide, channels), 0) - LEFT
    inner_col = jnp.where(lane_col < 0, lane_col + width, jnp.where(lane_col >= width, lane_col - width, lane_col))
    seen = (lane_col >= -1) & (lane_col <= width)
    limits = []
    for k in range(3):
        limit = jnp.where(
            lane_col < 0, spots[3 * k], jnp.where(lane_col >= width, spots[3 * k + 2], spots[3 * k + 1])
        )
        limits.append(jnp.where(seen, limit, -1.0))
    pieces = []
    for r in range(height + 2):
        tile_row = (r - 1) % height
        limit = limits[0 if r == 0 else (2 if r == height + 1 else 1)]
        raster = (tile_row * width + inner_col).astype(F32)
        pieces.append(jnp.where(raster < limit, both[r * wide : (r + 1) * wide], 0.0).astype(BF16))
    back_mapped = jnp.concatenate(pieces, axis=0)
    back_hidden = dot(back_mapped, mixing_turned).astype(BF16)
    back[...] = back_hidden.astype(F32).reshape(height + 2, wide, channels)

    assemble(ext, tile, up, down, left, right)
    depth = []
    for lane in range(0, channels, LANES):
        part = slice(lane, lane + LANES)
        taps = [weights[k : k + 1, part] for k in range(9)]
        column = iota((wide, LANES), 0)
        within = (column >= LEFT) & (column < LEFT + width)

        def body(i, sums, part=part, taps=taps, within=within):
            rows = [back[i + a, :, part] for a in range(3)]
            cols = [sum(rows[2 - a] * taps[3 * a + b] for a in range(3)) for b in range(3)]
            value = cols[1] + shifted(cols[0], -1) + shifted(cols[2], 1)
            gradient[i, :, part] = value[LEFT : LEFT + width].astype(BF16)
            own = jnp.where(within, rows[1], 0.0)
            moved_own = [shifted(own, -1), own, shifted(own, 1)]
            feats = [ext[i + 1 + a, :, part] for a in range(3)]
            out = []
            for a in range(3):
                for b in range(3):
                    product = (feats[a] * moved_own[b]).reshape(wide // 8, 8, LANES)
                    out.append(sums[3 * a + b] + jnp.sum(product, axis=0))
            return tuple(out)

        sums = lax.fori_loop(
            0, height, body, tuple(jnp.zeros((8, LANES), F32) for _ in range(9))
        )
        depth.append(
            jnp.concatenate([jnp.sum(s, axis=0, keepdims=True) for s in sums], axis=0)
        )
    depth = jnp.concatenate(depth, axis=1)

    upper, tri, diag = tri_pack(class_term)
    class_flat = jnp.concatenate([upper, tri], axis=0)
    scale = 1.0 / planes
    extra = jnp.concatenate([diag, jnp.broadcast_to(loss, (1, half))], axis=1) * scale
    small = jnp.concatenate([depth, extra, jnp.zeros((6, channels), F32)], axis=0)
    rp, rc, rd = channels // slides, channels // slides // 2, 16 // slides
    for k in range(slides):
        sent[k, 0:rp, :] = point_term[k * rp : (k + 1) * rp]
        sent[k, rp : rp + rc, 0:half] = class_flat[k * rp : k * rp + rc]
        sent[k, rp : rp + rc, half:channels] = class_flat[k * rp + rc : (k + 1) * rp]
        sent[k, rp + rc : rp + rc + 8, :] = jnp.concatenate(
            [small[k * rd : (k + 1) * rd], jnp.zeros((8 - rd, channels), F32)], axis=0
        ) if rd < 8 else small[k * rd : (k + 1) * rd]


def slide_sum_kernel(rd, terms, shares, spread):
    planes = spread.shape[0]
    slides, rows, channels = terms.shape
    summed = terms[0]
    for k in range(1, slides):
        summed = summed + terms[k]
    shares[...] = summed[: rows - 8]
    tail = summed[rows - 8 : rows]
    for q in range(rd):
        spread[:, q * channels : (q + 1) * channels] = jnp.broadcast_to(
            tail[q : q + 1], (planes, channels)
        )


def join_kernel(shares, spread, out):
    slides, rows, channels = out.shape
    rd = spread.shape[1] // channels
    summed = jnp.sum(spread[...], axis=0, keepdims=True)
    tail = [summed[:, q * channels : (q + 1) * channels] for q in range(rd)]
    if rd < 8:
        tail.append(jnp.zeros((8 - rd, channels), F32))
    tail = jnp.concatenate(tail, axis=0)
    for k in range(slides):
        out[k, 0 : rows - 8, :] = shares[...]
        out[k, rows - 8 : rows, :] = tail


def finish_kernel(terms, loss, depth, point, classes):
    slides, rows, channels = terms.shape
    half = channels // 2
    rp, rc, rd = channels // slides, channels // slides // 2, 16 // slides
    flat, small = [], []
    for k in range(slides):
        point[k * rp : (k + 1) * rp, :] = terms[k, 0:rp, :]
        flat += [terms[k, rp : rp + rc, 0:half], terms[k, rp : rp + rc, half:channels]]
        small.append(terms[k, rp + rc : rp + rc + rd, :])
    flat = jnp.concatenate(flat, axis=0)
    small = jnp.concatenate(small, axis=0)
    full = tri_unpack(flat[:half], flat[half:], small[9:10, :half])
    classes[0] = full
    classes[1] = -full
    for a in range(3):
        depth[a] = small[3 * a : 3 * a + 3]
    loss[...] = small[9:10, half : half + 1]


def per_device(features, depth_weight, point_weight, classifier, valid_count, labels):
    slides, grid_y, grid_x = (lax.axis_size(axis) for axis in ("slide", "gy", "gx"))
    planes = grid_y * grid_x
    tile = features[0]
    height, width, channels = tile.shape
    wide = width + 2 * LEFT

    def edges(low_part, high_part, axis):
        forward = [(i, i + 1) for i in range(lax.axis_size(axis) - 1)]
        backward = [(target, source) for source, target in forward]
        return lax.ppermute(high_part, axis, forward), lax.ppermute(low_part, axis, backward)

    up, down = edges(tile[:RIM], tile[height - RIM :], "gy")

    def strip(start):
        return jnp.concatenate([part[:, start : start + RIM] for part in (up, tile, down)], axis=0)

    left, right = edges(strip(0), strip(width - RIM), "gx")

    weights = depth_weight.reshape(9, channels).astype(F32)
    point_turned = point_weight.T
    count = valid_count.reshape(1)
    place = jnp.stack([lax.axis_index("gy"), lax.axis_index("gx")]).astype(jnp.int32)
    halo = (tile, up, down, left, right)
    chunks = -(-(channels + 3) // planes)

    mapped, packed = pl.pallas_call(
        functools.partial(forward_kernel, planes),
        out_shape=(
            jax.ShapeDtypeStruct(((height + 2) * wide, channels), BF16),
            jax.ShapeDtypeStruct((planes, chunks * LANES), F32),
        ),
        in_specs=[SMEM] + [VMEM] * 7,
        out_specs=(VMEM, VMEM),
        scratch_shapes=[
            pltpu.VMEM((height + 2 * RIM, wide, channels), F32),
            pltpu.VMEM(((height + 2) * wide, channels), BF16),
            pltpu.VMEM((height * width, channels), BF16),
        ],
        compiler_params=PARAMS,
        name="forward",
    )(count, *halo, weights, point_weight)

    packed = lax.all_to_all(packed, ("gy", "gx"), 0, 0)
    packed = pl.pallas_call(
        plane_sum_kernel,
        out_shape=jax.ShapeDtypeStruct((planes, (chunks + 1) * LANES), F32),
        in_specs=[SMEM, VMEM],
        out_specs=VMEM,
        name="plane_sum",
    )(count, packed)
    gathered = lax.all_to_all(packed, ("gy", "gx"), 0, 0)

    rp, rd = channels // slides, 16 // slides
    rows = rp + rp // 2 + 8
    gradient, sent = pl.pallas_call(
        functools.partial(cov_kernel, grid_y, grid_x, slides),
        out_shape=(
            jax.ShapeDtypeStruct((height, width, channels), BF16),
            jax.ShapeDtypeStruct((slides, rows, channels), F32),
        ),
        in_specs=[SMEM, SMEM] + [VMEM] * 11,
        out_specs=(VMEM, VMEM),
        scratch_shapes=[
            pltpu.VMEM((height + 2 * RIM, wide, channels), F32),
            pltpu.VMEM((height + 2, wide, channels), F32),
        ],
        compiler_params=PARAMS,
        name="covariance",
    )(place, labels, gathered, *halo, weights, point_weight, point_turned, classifier, mapped)

    received = lax.all_to_all(sent, "slide", 0, 0)
    shares, spread = pl.pallas_call(
        functools.partial(slide_sum_kernel, rd),
        out_shape=(
            jax.ShapeDtypeStruct((rows - 8, channels), F32),
            jax.ShapeDtypeStruct((planes, rd * channels), F32),
        ),
        in_specs=[VMEM],
        out_specs=(VMEM, VMEM),
        name="slide_sum",
    )(received)
    spread = lax.all_to_all(spread, ("gy", "gx"), 0, 0)
    joined = pl.pallas_call(
        join_kernel,
        out_shape=jax.ShapeDtypeStruct((slides, rows, channels), F32),
        in_specs=[VMEM, VMEM],
        out_specs=VMEM,
        name="join",
    )(shares, spread)
    joined = lax.all_to_all(joined, "slide", 0, 0)
    loss, depth, point, classes = pl.pallas_call(
        finish_kernel,
        out_shape=(
            jax.ShapeDtypeStruct((1, 1), F32),
            jax.ShapeDtypeStruct((3, 3, channels), F32),
            jax.ShapeDtypeStruct((channels, channels), F32),
            jax.ShapeDtypeStruct(classifier.shape, F32),
        ),
        in_specs=[VMEM],
        out_specs=(VMEM, VMEM, VMEM, VMEM),
        name="finish",
    )(joined)
    return loss.reshape(()), depth, point, classes, gradient[None]


def solution(mesh):
    placed = (P("slide", "gy", "gx", None), P(), P(), P(), P("slide", "gy", "gx"), P("slide"))
    return jax.shard_map(
        per_device,
        mesh=mesh,
        in_specs=placed,
        out_specs=(P(), P(), P(), P(), P("slide", "gy", "gx", None)),
        check_vma=False,
    )
```

time: 869 us -> 160 us (0.18)
  waiting for transfers between devices: 463 us -> 17.2 us
  blocking collectives: 306 us -> 92.7 us
  matrix products: 38.3 us -> 0 us
  Pallas kernels: 0 us -> 22 us
  between operations: 21 us -> 2.1 us
  other arithmetic: 14.2 us -> 0.15 us
    psum x3 -> x0, waiting for transfers between devices: 457 us -> none  [the longest x1 332 us: per_device(): lax.psum((point_term, depth_term), ('slide', 'gy', 'gx'))]
    psum x3 -> x0, blocking collectives: 306 us -> none  [the longest x1 178 us: per_device(): lax.psum((second_part, first_part, count_part), ('gy', 'gx'))]
    all_to_all x0 -> x4, blocking collectives: none -> 92.7 us  [the longest x1 36.8 us: per_device(): packed = lax.all_to_all(packed, ('gy', 'gx'), 0, 0)]
    dot_general x47 -> x0, matrix products: 38.3 us -> none  [the longest x41 25.3 us: matmul_high(): return jnp.dot(left, right, precision=lax.Precision.HIGHEST)]
    pallas_call x0 -> x6, Pallas kernels: none -> 22 us  [the longest x1 12.7 us: per_device(): pl.pallas_call(functools.partial(cov_kernel, grid_y, grid_x, slides), out...]
    all_to_all x0 -> x1, waiting for transfers between devices: none -> 14 us  [per_device(): gathered = lax.all_to_all(packed, ('gy', 'gx'), 0, 0)]
    ppermute x8 -> x4, starting transfers between devices: 19.7 us -> 11.4 us  [the longest x2 8.66 us: edges(): lax.ppermute(high_part, axis, forward)]
  transfers between devices with their start and end apart: 11 -> 5, of which waited for: 6 -> 3; matrix products, arithmetic and copies ran while one was open for 1% -> 1% of each run, Pallas kernels for 0% -> 0%
where the time goes in v1:
time: 160 us; the launch traced here: 159 us
  blocking collectives  92.7 us (58%)
  Pallas kernels  22 us (14%)
  starting transfers between devices  17.4 us (11%)
  waiting for transfers between devices  17.2 us (11%)
  local copies, waits for them, and re-layouts  7.44 us (5%)
  between operations  2.1 us (1%)
    all_to_all x1, blocking collectives, per_device(): packed = lax.all_to_all(packed, ('gy', 'gx'), 0, 0)  36.8 us
    all_to_all x1, blocking collectives, per_device(): spread = lax.all_to_all(spread, ('gy', 'gx'), 0, 0)  21.1 us
    all_to_all x1, blocking collectives, per_device(): received = lax.all_to_all(sent, 'slide', 0, 0)  19 us
    all_to_all x1, blocking collectives, per_device(): joined = lax.all_to_all(joined, 'slide', 0, 0)  15.8 us
    all_to_all x1, waiting for transfers between devices, per_device(): gathered = lax.all_to_all(packed, ('gy', 'gx'), 0, 0)  14 us
    pallas_call x1, Pallas kernels, per_device(): pl.pallas_call(functools.partial(cov_kernel, grid_y, grid_x, slides), out...  12.7 us
    ppermute x2, starting transfers between devices, edges(): lax.ppermute(high_part, axis, forward)  8.66 us
    all_to_all x1, starting transfers between devices, per_device(): gathered = lax.all_to_all(packed, ('gy', 'gx'), 0, 0)  6.07 us
  transfers between devices with their start and end apart: 5, of which 3 were waited for; matrix products, arithmetic and copies ran while one was open for 1% of the time, Pallas kernels for 0%

profile of v1, /device:TPU:1, one launch (start us, length us, event | category | flops | bytes accessed | tf_op | source)
XLA Modules:
  0.0 159.0 jit_solution(11170254450900564361)
XLA Ops:
  0.6 0.9 slice_bitcast_fusion
  1.5 1.4 collective-permute-start.1
  3.0 5.5 %collective-permute-start = (bf16[2,64,256]{2,1,0:T(8,128)(2,1)S(1)}, bf16[2,64,256]{2,1,0:T(8,128)(2,1)S(1)}, u32[]{:S(2)}, u32[]{:S(2)}) collective-permute-start(bf16[2,64,256]{2,1,0:T(8,128)(2,1)S(1)} %get-tuple-element.28), channel_id=1, source_target_pairs={{0,8},{8,16},{16,24},{24,32},{32,40},{40,48},{48,56},{56,64},{64,7... | collective-permute-start | bytes 196616 | tf_op jit(solution)/shard_map/ppermute | solution.py:358
  8.4 0.9 fusion
  9.8 3.2 %collective-permute-start.2 = (bf16[20,2,256]{2,1,0:T(2,128)(2,1)S(1)}, bf16[20,2,256]{2,1,0:T(2,128)(2,1)S(1)}, u32[]{:S(2)}, u32[]{:S(2)}) collective-permute-start(bf16[20,2,256]{2,1,0:T(2,128)(2,1)S(1)} %pad_maximum_fusion), channel_id=1, source_target_pairs={{0,1},{1,2},{2,3},{3,4},{4,5},{5,6},{6,7},{8,9},{9,10},{10,11},{11... | collective-permute-start | bytes 61448 | tf_op jit(solution)/shard_map/ppermute | solution.py:358
  13.0 1.3 collective-permute-start.3
  15.0 2.8 %collective-permute-done.3.right = bf16[20,2,256]{2,1,0:T(2,128)(2,1)S(1)} collective-permute-done((bf16[20,2,256]{2,1,0:T(2,128)(2,1)S(1)}, bf16[20,2,256]{2,1,0:T(2,128)(2,1)S(1)}, u32[]{:S(2)}, u32[]{:S(2)}) %collective-permute-start.3) | collective-permute-done | bytes 20512 | tf_op jit(solution)/shard_map/ppermute | solution.py:358
  17.9 1.0 copy-done
  18.9 2.2 %forward.1 = (bf16[1440,256]{1,0:T(8,128)(2,1)S(1)}, f32[96,384]{1,0:T(8,128)S(1)}) custom-call(s32[1]{0:T(128)} %bitcast.23.count, bf16[16,64,256]{2,1,0:T(8,128)(2,1)S(1)} %bitcast.26, bf16[2,64,256]{2,1,0:T(8,128)(2,1)S(1)} %collective-permute-done.up, bf16[2,64,256]{2,1,0:T(8,128)(2,1)S(1)} %collective-permute-done.1.down, ...), custom_call_target="tpu_custom_call" | custom-call | tf_op jit(solution)/shard_map/forward/pallas_call | solution.py:374
  21.3 36.8 %all_to_all.43 = f32[96,1,384]{2,1,0:T(1,128)S(1)} all-to-all(f32[96,1,384]{2,1,0:T(1,128)S(1)} %copy.12), channel_id=1, replica_groups=mesh['slide'=8,'gy'=12,'gx'=8] {'gy','gx'}, dimensions={0} | all-to-all | bytes 294912 | tf_op jit(solution)/shard_map/all_to_all | solution.py:391
  58.1 0.7 copy.24
  58.8 1.6 %plane_sum.1 = f32[96,512]{1,0:T(8,128)} custom-call(s32[1]{0:T(128)} %bitcast.24.count, f32[96,384]{1,0:T(8,128)} %bitcast.33), custom_call_target="tpu_custom_call" | custom-call | tf_op jit(solution)/shard_map/plane_sum/pallas_call | solution.py:392
  60.4 1.8 %copy.13 = f32[96,1,512]{2,1,0:T(1,128)} copy(f32[96,1,512]{2,0,1:T(8,128)} %bitcast.32) | data formatting | bytes 393216 | tf_op jit(solution)/shard_map/all_to_all | solution.py:399
  62.2 6.1 %all-to-all-start.1 = ((f32[96,1,512]{2,1,0:T(1,128)}), f32[96,1,512]{2,1,0:T(1,128)S(1)}, u32[]{:S(2)}, u32[]{:S(2)}) async-start(f32[96,1,512]{2,1,0:T(1,128)} %copy.13), calls=%async_computation.1 | async-start | bytes 393216 | tf_op jit(solution)/shard_map/all_to_all | solution.py:399
  69.2 14.0 %all-to-all-done.1 = f32[96,1,512]{2,1,0:T(1,128)S(1)} async-done(((f32[96,1,512]{2,1,0:T(1,128)}), f32[96,1,512]{2,1,0:T(1,128)S(1)}, u32[]{:S(2)}, u32[]{:S(2)}) %all-to-all-start.1) | async-done | bytes 196640 | tf_op jit(solution)/shard_map/all_to_all | solution.py:399
  83.2 12.7 %covariance.1 = (bf16[16,64,256]{2,1,0:T(8,128)(2,1)}, f32[8,56,256]{2,1,0:T(8,128)S(1)}) custom-call(s32[2]{0:T(128)S(1)} %pad_add_fusion.place, s32[1]{0:T(128)S(6)} %copy.26.label, f32[96,512]{1,0:T(8,128)S(1)} %bitcast.28, bf16[16,64,256]{2,1,0:T(8,128)(2,1)S(1)} %bitcast.27, bf16[2,64,256]{2,1,0:T(8,128)(2,1)S(1)} %collective-permute-done.up, ...), custom_call_target="tpu_custom_call" | custom-call | tf_op jit(solution)/shard_map/covariance/pallas_call | solution.py:403
  95.9 19.0 %all_to_all.44.terms = f32[8,56,256]{2,1,0:T(8,128)} all-to-all(f32[8,56,256]{2,1,0:T(8,128)S(1)} %get-tuple-element.17), channel_id=1, replica_groups=mesh['slide'=8,'gy'=12,'gx'=8] {'slide'}, dimensions={0} | all-to-all | bytes 917504 | tf_op jit(solution)/shard_map/all_to_all | solution.py:419
  114.9 1.7 %slide_sum.1 = (f32[48,256]{1,0:T(8,128)}, f32[96,512]{1,0:T(8,128)}) custom-call(f32[8,56,256]{2,1,0:T(8,128)} %all_to_all.44.terms), custom_call_target="tpu_custom_call" | custom-call | tf_op jit(solution)/shard_map/slide_sum/pallas_call | solution.py:420
  116.6 1.1 copy.15
  117.8 21.1 %all_to_all.45 = f32[96,1,512]{2,1,0:T(1,128)S(1)} all-to-all(f32[96,1,512]{2,1,0:T(1,128)S(1)} %copy.15), channel_id=1, replica_groups=mesh['slide'=8,'gy'=12,'gx'=8] {'gy','gx'}, dimensions={0} | all-to-all | bytes 393216 | tf_op jit(solution)/shard_map/all_to_all | solution.py:430
  138.8 0.7 copy.22
  139.5 1.8 %join.1 = f32[8,56,256]{2,1,0:T(8,128)} custom-call(f32[48,256]{1,0:T(8,128)} %get-tuple-element.18.shares, f32[96,512]{1,0:T(8,128)} %bitcast.31), custom_call_target="tpu_custom_call" | custom-call | tf_op jit(solution)/shard_map/join/pallas_call | solution.py:431
  141.3 15.8 %all_to_all.46.terms = f32[8,56,256]{2,1,0:T(8,128)} all-to-all(f32[8,56,256]{2,1,0:T(8,128)} %join.1), channel_id=1, replica_groups=mesh['slide'=8,'gy'=12,'gx'=8] {'slide'}, dimensions={0} | all-to-all | bytes 917504 | tf_op jit(solution)/shard_map/all_to_all | solution.py:438
  157.1 1.9 %finish.1 = (f32[1,1]{1,0:T(1,128)}, f32[3,3,256]{2,1,0:T(4,128)}, f32[256,256]{1,0:T(8,128)}, f32[2,256,256]{2,1,0:T(8,128)}) custom-call(f32[8,56,256]{2,1,0:T(8,128)} %all_to_all.46.terms), custom_call_target="tpu_custom_call" | custom-call | tf_op jit(solution)/shard_map/finish/pallas_call | solution.py:439
  (21 shorter events, 0.8 us)
Async XLA Ops:
  1.5 16.4 %copy-start.2 = (bf16[256,256]{1,0:T(8,128)(2,1)S(1)}, bf16[256,256]{1,0:T(8,128)(2,1)}, u32[]{:S(2)}) copy-start(bf16[256,256]{1,0:T(8,128)(2,1)} %point.3) | copy-start | bytes 393220
  1.5 7.8 %collective-permute-start.1 = (bf16[2,64,256]{2,1,0:T(8,128)(2,1)S(1)}, bf16[2,64,256]{2,1,0:T(8,128)(2,1)S(1)}, u32[]{:S(2)}, u32[]{:S(2)}) collective-permute-start(bf16[2,64,256]{2,1,0:T(8,128)(2,1)S(1)} %get-tuple-element.27), channel_id=1, source_target_pairs={{8,0},{16,8},{24,16},{32,24},{40,32},{48,40},{56,48},{64,56},{72,6... | collective-permute-start | bytes 196616 | tf_op jit(solution)/shard_map/ppermute | solution.py:358
  3.0 6.8 %collective-permute-start = (bf16[2,64,256]{2,1,0:T(8,128)(2,1)S(1)}, bf16[2,64,256]{2,1,0:T(8,128)(2,1)S(1)}, u32[]{:S(2)}, u32[]{:S(2)}) collective-permute-start(bf16[2,64,256]{2,1,0:T(8,128)(2,1)S(1)} %get-tuple-element.28), channel_id=1, source_target_pairs={{0,8},{8,16},{16,24},{24,32},{32,40},{40,48},{48,56},{56,64},{64,7... | collective-permute-start | bytes 196616 | tf_op jit(solution)/shard_map/ppermute | solution.py:358
  9.8 5.2 %collective-permute-start.2 = (bf16[20,2,256]{2,1,0:T(2,128)(2,1)S(1)}, bf16[20,2,256]{2,1,0:T(2,128)(2,1)S(1)}, u32[]{:S(2)}, u32[]{:S(2)}) collective-permute-start(bf16[20,2,256]{2,1,0:T(2,128)(2,1)S(1)} %pad_maximum_fusion), channel_id=1, source_target_pairs={{0,1},{1,2},{2,3},{3,4},{4,5},{5,6},{6,7},{8,9},{9,10},{10,11},{11... | collective-permute-start | bytes 61448 | tf_op jit(solution)/shard_map/ppermute | solution.py:358
  13.0 2.0 %copy-start.4 = (bf16[3,3,256]{2,1,0:T(4,128)(2,1)S(1)}, bf16[3,3,256]{2,1,0:T(4,128)(2,1)}, u32[]{:S(2)}) copy-start(bf16[3,3,256]{2,1,0:T(4,128)(2,1)} %param.7) | copy-start | bytes 13828
  13.0 4.8 %collective-permute-start.3 = (bf16[20,2,256]{2,1,0:T(2,128)(2,1)S(1)}, bf16[20,2,256]{2,1,0:T(2,128)(2,1)S(1)}, u32[]{:S(2)}, u32[]{:S(2)}) collective-permute-start(bf16[20,2,256]{2,1,0:T(2,128)(2,1)S(1)} %pad_maximum_fusion.1), channel_id=1, source_target_pairs={{1,0},{2,1},{3,2},{4,3},{5,4},{6,5},{7,6},{9,8},{10,9},{11,10},{12... | collective-permute-start | bytes 61448 | tf_op jit(solution)/shard_map/ppermute | solution.py:358
  17.9 1.0 copy-start
  62.2 21.0 %copy-start.1 = (bf16[1,16,64,256]{3,2,1,0:T(8,128)(2,1)S(1)}, bf16[1,16,64,256]{3,2,1,0:T(8,128)(2,1)}, u32[]{:S(2)}) copy-start(bf16[1,16,64,256]{3,2,1,0:T(8,128)(2,1)} %param.6) | copy-start | bytes 1572868
  62.2 21.0 %copy-start.3 = (f32[2,256,256]{2,1,0:T(8,128)S(1)}, f32[2,256,256]{2,1,0:T(8,128)}, u32[]{:S(2)}) copy-start(f32[2,256,256]{2,1,0:T(8,128)} %classifier.1) | copy-start | bytes 1572868
  62.2 20.9 %all-to-all-start.1 = ((f32[96,1,512]{2,1,0:T(1,128)}), f32[96,1,512]{2,1,0:T(1,128)S(1)}, u32[]{:S(2)}, u32[]{:S(2)}) async-start(f32[96,1,512]{2,1,0:T(1,128)} %copy.13), calls=%async_computation.1 | async-start | bytes 393216 | tf_op jit(solution)/shard_map/all_to_all | solution.py:399

commit v2 on v1

--- a/solution.py
+++ b/solution.py
@@ -15,7 +15,7 @@
 BF16 = jnp.bfloat16
 VMEM = pl.BlockSpec(memory_space=pltpu.VMEM)
 SMEM = pl.BlockSpec(memory_space=pltpu.SMEM)
-PARAMS = pltpu.CompilerParams(vmem_limit_bytes=40 * 1024 * 1024)
+PARAMS = pltpu.CompilerParams(vmem_limit_bytes=24 * 1024 * 1024)
 
 
 def iota(shape, dim):
@@ -83,7 +83,7 @@
 
 
 def forward_kernel(
-    planes, count, tile, up, down, left, right, weights, point, mapped, packed, ext, hidden, inner
+    planes, count, tile, up, down, left, right, weights, hidden, packed, ext, inner
 ):
     height, width, channels = tile.shape
     wide = ext.shape[1]
@@ -111,43 +111,50 @@
 
         lax.fori_loop(0, height + 2, body, 0)
 
-    mapped[...] = dot(hidden[...], point[...]).astype(BF16)
     kept = inner[...]
     gram = lax.dot_general(kept, kept, (((0,), (0,)), ((), ())), preferred_element_type=F32)
     sums = jnp.sum(kept.astype(F32), axis=0, keepdims=True)
     upper, both, diag = tri_pack(gram)
-    chunks = packed.shape[1] // LANES
+    chunks = packed.shape[1] - 1
     spare = chunks * planes - 2 * LANES - 3
     flat = jnp.concatenate(
         [upper, both, diag, sums[:, :LANES], sums[:, LANES:], jnp.zeros((spare, LANES), F32)],
         axis=0,
     )
     for q in range(chunks):
-        packed[:, q * LANES : (q + 1) * LANES] = flat[q * planes : (q + 1) * planes]
+        packed[:, q, :] = flat[q * planes : (q + 1) * planes]
+    packed[:, chunks, :] = jnp.zeros((planes, LANES), F32)
 
 
 def plane_sum_kernel(count, terms, out):
-    planes, lanes = terms.shape
-    summed = jnp.sum(terms[...], axis=0, keepdims=True)
-    out[:, :lanes] = jnp.broadcast_to(summed, (planes, lanes))
-    out[:, lanes:] = jnp.full((planes, LANES), count[0].astype(F32))
+    planes, rows, lanes = terms.shape
+    summed = jnp.sum(terms[...], axis=0)
+    valid = jnp.full((rows, lanes), count[0].astype(F32))
+    summed = jnp.where(iota((rows, lanes), 0) == rows - 1, valid, summed)
+    out[...] = jnp.broadcast_to(summed[None], out.shape)
+
+
+def prepare_kernel(
+    hidden, point, tile, up, down, left, right, classifier, mapped, ext, toward
+):
+    mapped[...] = dot(hidden[...], point[...]).astype(BF16)
+    assemble(ext, tile, up, down, left, right)
+    gap = classifier[0] - classifier[1]
+    toward[...] = gap + gap.T
 
 
 def cov_kernel(
-    grid_y, grid_x, slides, place, label, gathered, tile, up, down, left, right, weights, point,
-    point_turned, classifier, mapped, gradient, sent, ext, back,
+    grid_y, grid_x, slides, place, label, gathered, ext, mapped, toward_ref, point, point_turned,
+    classifier, back, sent,
 ):
-    height, width, channels = tile.shape
     planes = grid_y * grid_x
-    wide = ext.shape[1]
+    wide, channels = ext.shape[1:]
+    height, width = ext.shape[0] - 2 * RIM, wide - 2 * LEFT
     half = channels // 2
-    chunks = gathered.shape[1] // LANES - 1
-    pixels = (height + 2) * wide
-
-    flat = jnp.concatenate(
-        [gathered[:, q * LANES : (q + 1) * LANES] for q in range(chunks)], axis=0
-    )
-    counts = gathered[:, chunks * LANES : (chunks + 1) * LANES]
+    chunks = gathered.shape[1] - 1
+
+    flat = jnp.concatenate([gathered[:, q, :] for q in range(chunks)], axis=0)
+    counts = gathered[:, chunks, :]
     inverse = 1.0 / jnp.sum(counts, axis=0, keepdims=True)[:, 0:1]
     gram = tri_unpack(flat[:half], flat[half : 2 * half], flat[2 * half : 2 * half + 1])
     sums = jnp.concatenate(
@@ -172,8 +179,7 @@
     trace = total(jnp.where(eye, sigma, 0.0))
     start = sigma * (1.0 / trace)
 
-    toward = classifier[0] - classifier[1]
-    toward = toward + toward.T
+    toward = toward_ref[...]
     wmat, ymat, dw, dy = start, start, toward, toward
     for step in range(ITERS):
         w_pair, dw_pair = split(wmat), split(dw)
@@ -253,20 +259,14 @@
     back_hidden = dot(back_mapped, mixing_turned).astype(BF16)
     back[...] = back_hidden.astype(F32).reshape(height + 2, wide, channels)
 
-    assemble(ext, tile, up, down, left, right)
     depth = []
     for lane in range(0, channels, LANES):
         part = slice(lane, lane + LANES)
-        taps = [weights[k : k + 1, part] for k in range(9)]
         column = iota((wide, LANES), 0)
         within = (column >= LEFT) & (column < LEFT + width)
 
-        def body(i, sums, part=part, taps=taps, within=within):
-            rows = [back[i + a, :, part] for a in range(3)]
-            cols = [sum(rows[2 - a] * taps[3 * a + b] for a in range(3)) for b in range(3)]
-            value = cols[1] + shifted(cols[0], -1) + shifted(cols[2], 1)
-            gradient[i, :, part] = value[LEFT : LEFT + width].astype(BF16)
-            own = jnp.where(within, rows[1], 0.0)
+        def body(i, sums, part=part, within=within):
+            own = jnp.where(within, back[i + 1, :, part], 0.0)
             moved_own = [shifted(own, -1), own, shifted(own, 1)]
             feats = [ext[i + 1 + a, :, part] for a in range(3)]
             out = []
@@ -290,40 +290,64 @@
     extra = jnp.concatenate([diag, jnp.broadcast_to(loss, (1, half))], axis=1) * scale
     small = jnp.concatenate([depth, extra, jnp.zeros((6, channels), F32)], axis=0)
     rp, rc, rd = channels // slides, channels // slides // 2, 16 // slides
+    pad = [jnp.zeros((8 - rd, channels), F32)] if rd < 8 else []
     for k in range(slides):
         sent[k, 0:rp, :] = point_term[k * rp : (k + 1) * rp]
         sent[k, rp : rp + rc, 0:half] = class_flat[k * rp : k * rp + rc]
         sent[k, rp : rp + rc, half:channels] = class_flat[k * rp + rc : (k + 1) * rp]
         sent[k, rp + rc : rp + rc + 8, :] = jnp.concatenate(
-            [small[k * rd : (k + 1) * rd], jnp.zeros((8 - rd, channels), F32)], axis=0
-        ) if rd < 8 else small[k * rd : (k + 1) * rd]
+            [small[k * rd : (k + 1) * rd]] + pad, axis=0
+        )
+
+
+def spread_kernel(back, weights, gradient):
+    height, width, channels = gradient.shape
+    for lane in range(0, channels, LANES):
+        part = slice(lane, lane + LANES)
+        taps = [weights[k : k + 1, part] for k in range(9)]
+
+        def body(i, carry, part=part, taps=taps):
+            rows = [back[i + a, :, part] for a in range(3)]
+            cols = [sum(rows[2 - a] * taps[3 * a + b] for a in range(3)) for b in range(3)]
+            value = cols[1] + shifted(cols[0], -1) + shifted(cols[2], 1)
+            gradient[i, :, part] = value[LEFT : LEFT + width].astype(BF16)
+            return carry
+
+        lax.fori_loop(0, height, body, 0)
 
 
 def slide_sum_kernel(rd, terms, shares, spread):
-    planes = spread.shape[0]
     slides, rows, channels = terms.shape
+    main = rows - 8
     summed = terms[0]
     for k in range(1, slides):
         summed = summed + terms[k]
-    shares[...] = summed[: rows - 8]
-    tail = summed[rows - 8 : rows]
-    for q in range(rd):
-        spread[:, q * channels : (q + 1) * channels] = jnp.broadcast_to(
-            tail[q : q + 1], (planes, channels)
-        )
+    shares[...] = summed[:main].astype(BF16)
+    tail = summed[main : main + rd]
+    lines = jnp.concatenate(
+        [tail[q : q + 1, p : p + LANES] for q in range(rd) for p in range(0, channels, LANES)],
+        axis=0,
+    )
+    spread[...] = jnp.broadcast_to(lines[None], spread.shape)
 
 
 def join_kernel(shares, spread, out):
     slides, rows, channels = out.shape
-    rd = spread.shape[1] // channels
-    summed = jnp.sum(spread[...], axis=0, keepdims=True)
-    tail = [summed[:, q * channels : (q + 1) * channels] for q in range(rd)]
-    if rd < 8:
-        tail.append(jnp.zeros((8 - rd, channels), F32))
-    tail = jnp.concatenate(tail, axis=0)
+    summed = jnp.sum(spread[...], axis=0)
+    per = channels // LANES
+    rd = summed.shape[0] // per
+    tail = jnp.concatenate(
+        [
+            jnp.concatenate([summed[per * q + p : per * q + p + 1] for p in range(per)], axis=1)
+            for q in range(rd)
+        ],
+        axis=0,
+    )
+    high, low = split(tail)
+    tail = jnp.concatenate([high, low, jnp.zeros((16 - 2 * rd, channels), BF16)], axis=0)
     for k in range(slides):
-        out[k, 0 : rows - 8, :] = shares[...]
-        out[k, rows - 8 : rows, :] = tail
+        out[k, 0 : rows - 16, :] = shares[...]
+        out[k, rows - 16 : rows, :] = tail
 
 
 def finish_kernel(terms, loss, depth, point, classes):
@@ -332,9 +356,11 @@
     rp, rc, rd = channels // slides, channels // slides // 2, 16 // slides
     flat, small = [], []
     for k in range(slides):
-        point[k * rp : (k + 1) * rp, :] = terms[k, 0:rp, :]
-        flat += [terms[k, rp : rp + rc, 0:half], terms[k, rp : rp + rc, half:channels]]
-        small.append(terms[k, rp + rc : rp + rc + rd, :])
+        piece = terms[k].astype(F32)
+        point[k * rp : (k + 1) * rp, :] = piece[:rp]
+        flat += [piece[rp : rp + rc, :half], piece[rp : rp + rc, half:]]
+        tail = piece[rp + rc :]
+        small.append(tail[:rd] + tail[rd : 2 * rd])
     flat = jnp.concatenate(flat, axis=0)
     small = jnp.concatenate(small, axis=0)
     full = tri_unpack(flat[:half], flat[half:], small[9:10, :half])
@@ -371,27 +397,43 @@
     halo = (tile, up, down, left, right)
     chunks = -(-(channels + 3) // planes)
 
-    mapped, packed = pl.pallas_call(
+    pixels = (height + 2) * wide
+    ext_shape = (height + 2 * RIM, wide, channels)
+
+    hidden, packed = pl.pallas_call(
         functools.partial(forward_kernel, planes),
         out_shape=(
-            jax.ShapeDtypeStruct(((height + 2) * wide, channels), BF16),
-            jax.ShapeDtypeStruct((planes, chunks * LANES), F32),
-        ),
-        in_specs=[SMEM] + [VMEM] * 7,
+            jax.ShapeDtypeStruct((pixels, channels), BF16),
+            jax.ShapeDtypeStruct((planes, chunks + 1, LANES), F32),
+        ),
+        in_specs=[SMEM] + [VMEM] * 6,
         out_specs=(VMEM, VMEM),
-        scratch_shapes=[
-            pltpu.VMEM((height + 2 * RIM, wide, channels), F32),
-            pltpu.VMEM(((height + 2) * wide, channels), BF16),
-            pltpu.VMEM((height * width, channels), BF16),
-        ],
+        scratch_shapes=[pltpu.VMEM(ext_shape, F32), pltpu.VMEM((height * width, channels), BF16)],
         compiler_params=PARAMS,
         name="forward",
-    )(count, *halo, weights, point_weight)
+    )(count, *halo, weights)
 
     packed = lax.all_to_all(packed, ("gy", "gx"), 0, 0)
+
+    mapped, ext, toward = pl.pallas_call(
+        prepare_kernel,
+        out_shape=(
+            jax.ShapeDtypeStruct((pixels, channels), BF16),
+            jax.ShapeDtypeStruct(ext_shape, F32),
+            jax.ShapeDtypeStruct((channels, channels), F32),
+        ),
+        in_specs=[VMEM] * 8,
+        out_specs=(VMEM, VMEM, VMEM),
+        compiler_params=PARAMS,
+        cost_estimate=pl.CostEstimate(
+            flops=2 * pixels * channels * channels, bytes_accessed=5 << 20, transcendentals=0
+        ),
+        name="prepare",
+    )(hidden, point_weight, *halo, classifier)
+
     packed = pl.pallas_call(
         plane_sum_kernel,
-        out_shape=jax.ShapeDtypeStruct((planes, (chunks + 1) * LANES), F32),
+        out_shape=jax.ShapeDtypeStruct((planes, chunks + 1, LANES), F32),
         in_specs=[SMEM, VMEM],
         out_specs=VMEM,
         name="plane_sum",
@@ -399,29 +441,36 @@
     gathered = lax.all_to_all(packed, ("gy", "gx"), 0, 0)
 
     rp, rd = channels // slides, 16 // slides
-    rows = rp + rp // 2 + 8
-    gradient, sent = pl.pallas_call(
+    main = rp + rp // 2
+    back, sent = pl.pallas_call(
         functools.partial(cov_kernel, grid_y, grid_x, slides),
         out_shape=(
-            jax.ShapeDtypeStruct((height, width, channels), BF16),
-            jax.ShapeDtypeStruct((slides, rows, channels), F32),
-        ),
-        in_specs=[SMEM, SMEM] + [VMEM] * 11,
+            jax.ShapeDtypeStruct((height + 2, wide, channels), F32),
+            jax.ShapeDtypeStruct((slides, main + 8, channels), F32),
+        ),
+        in_specs=[SMEM, SMEM] + [VMEM] * 7,
         out_specs=(VMEM, VMEM),
-        scratch_shapes=[
-            pltpu.VMEM((height + 2 * RIM, wide, channels), F32),
-            pltpu.VMEM((height + 2, wide, channels), F32),
-        ],
         compiler_params=PARAMS,
         name="covariance",
-    )(place, labels, gathered, *halo, weights, point_weight, point_turned, classifier, mapped)
+    )(place, labels, gathered, ext, mapped, toward, point_weight, point_turned, classifier)
 
     received = lax.all_to_all(sent, "slide", 0, 0)
+    gradient = pl.pallas_call(
+        spread_kernel,
+        out_shape=jax.ShapeDtypeStruct((height, width, channels), BF16),
+        in_specs=[VMEM, VMEM],
+        out_specs=VMEM,
+        compiler_params=PARAMS,
+        cost_estimate=pl.CostEstimate(
+            flops=20 * pixels * channels, bytes_accessed=4 << 20, transcendentals=0
+        ),
+        name="spread",
+    )(back, weights)
     shares, spread = pl.pallas_call(
         functools.partial(slide_sum_kernel, rd),
         out_shape=(
-            jax.ShapeDtypeStruct((rows - 8, channels), F32),
-            jax.ShapeDtypeStruct((planes, rd * channels), F32),
+            jax.ShapeDtypeStruct((main, channels), BF16),
+            jax.ShapeDtypeStruct((planes, rd * channels // LANES, LANES), F32),
         ),
         in_specs=[VMEM],
         out_specs=(VMEM, VMEM),
@@ -430,7 +479,7 @@
     spread = lax.all_to_all(spread, ("gy", "gx"), 0, 0)
     joined = pl.pallas_call(
         join_kernel,
-        out_shape=jax.ShapeDtypeStruct((slides, rows, channels), F32),
+        out_shape=jax.ShapeDtypeStruct((slides, main + 16, channels), BF16),
         in_specs=[VMEM, VMEM],
         out_specs=VMEM,
         name="join",

time: 160 us -> 157 us (0.981)
  blocking collectives: 92.7 us -> 79.2 us
  starting transfers between devices: 17.4 us -> 23.4 us
  local copies, waits for them, and re-layouts: 7.44 us -> 11.6 us
    all_to_all x1 -> x0, blocking collectives: 15.8 us -> none  [per_device(): joined = lax.all_to_all(joined, 'slide', 0, 0)]
    unnamed x14 -> x33, local copies, waits for them, and re-layouts: 2.54 us -> 9.04 us
    all_to_all x0 -> x1, starting transfers between devices: none -> 6.26 us  [per_device(): joined = lax.all_to_all(joined, 'slide', 0, 0)]
    all_to_all x0 -> x1, waiting for transfers between devices: none -> 4.7 us  [per_device(): joined = lax.all_to_all(joined, 'slide', 0, 0)]
    all_to_all x1, waiting for transfers between devices: 14 us -> 9.57 us  [per_device(): gathered = lax.all_to_all(packed, ('gy', 'gx'), 0, 0)]
    all_to_all x3 -> x0, local copies, waits for them, and re-layouts: 3.09 us -> none  [the longest x1 1.8 us: per_device(): gathered = lax.all_to_all(packed, ('gy', 'gx'), 0, 0)]
    pallas_call x1 -> x3, Pallas kernels: 1.76 us -> 4.03 us  [the longest x1 1.82 us: per_device(): pl.pallas_call(spread_kernel, out_shape=jax.ShapeDtypeStruct((height, wid...]
    pallas_call x1, Pallas kernels: 12.7 us -> 11.1 us  [per_device(): pl.pallas_call(functools.partial(cov_kernel, grid_y, grid_x, slides), out...]
  transfers between devices with their start and end apart: 5 -> 6, of which waited for: 3 -> 4; matrix products, arithmetic and copies ran while one was open for 1% -> 1% of each run, Pallas kernels for 0% -> 1%
where the time goes in v2:
time: 157 us; the launch traced here: 156 us
  blocking collectives  79.2 us (50%)
  starting transfers between devices  23.4 us (15%)
  Pallas kernels  22.6 us (14%)
  waiting for transfers between devices  16.8 us (11%)
  local copies, waits for them, and re-layouts  11.6 us (7%)
  between operations  2.11 us (1%)
    all_to_all x1, blocking collectives, per_device(): packed = lax.all_to_all(packed, ('gy', 'gx'), 0, 0)  37.5 us
    all_to_all x1, blocking collectives, per_device(): spread = lax.all_to_all(spread, ('gy', 'gx'), 0, 0)  22.6 us
    all_to_all x1, blocking collectives, per_device(): received = lax.all_to_all(sent, 'slide', 0, 0)  19 us
    pallas_call x1, Pallas kernels, per_device(): pl.pallas_call(functools.partial(cov_kernel, grid_y, grid_x, slides), out...  11.1 us
    all_to_all x1, waiting for transfers between devices, per_device(): gathered = lax.all_to_all(packed, ('gy', 'gx'), 0, 0)  9.57 us
    unnamed x33, local copies, waits for them, and re-layouts  9.04 us
    ppermute x2, starting transfers between devices, edges(): lax.ppermute(high_part, axis, forward)  8.66 us
    all_to_all x1, starting transfers between devices, per_device(): joined = lax.all_to_all(joined, 'slide', 0, 0)  6.26 us
  transfers between devices with their start and end apart: 6, of which 4 were waited for; matrix products, arithmetic and copies ran while one was open for 1% of the time, Pallas kernels for 1%

profile of v2, /device:TPU:1, one launch (start us, length us, event | category | flops | bytes accessed | tf_op | source)
XLA Modules:
  0.0 156.4 jit_solution(4433365919419119217)
XLA Ops:
  0.6 0.9 slice_bitcast_fusion
  1.6 1.3 collective-permute-start.1
  2.9 5.5 %collective-permute-start = (bf16[2,64,256]{2,1,0:T(8,128)(2,1)S(1)}, bf16[2,64,256]{2,1,0:T(8,128)(2,1)S(1)}, u32[]{:S(2)}, u32[]{:S(2)}) collective-permute-start(bf16[2,64,256]{2,1,0:T(8,128)(2,1)S(1)} %get-tuple-element.34), channel_id=1, source_target_pairs={{0,8},{8,16},{16,24},{24,32},{32,40},{40,48},{48,56},{56,64},{64,7... | collective-permute-start | bytes 196616 | tf_op jit(solution)/shard_map/ppermute | solution.py:384
  9.7 3.2 %collective-permute-start.2 = (bf16[20,2,256]{2,1,0:T(2,128)(2,1)S(1)}, bf16[20,2,256]{2,1,0:T(2,128)(2,1)S(1)}, u32[]{:S(2)}, u32[]{:S(2)}) collective-permute-start(bf16[20,2,256]{2,1,0:T(2,128)(2,1)S(1)} %pad_maximum_fusion), channel_id=1, source_target_pairs={{0,1},{1,2},{2,3},{3,4},{4,5},{5,6},{6,7},{8,9},{9,10},{10,11},{11... | collective-permute-start | bytes 61448 | tf_op jit(solution)/shard_map/ppermute | solution.py:384
  12.9 1.3 collective-permute-start.3
  15.6 2.2 %collective-permute-done.3.right = bf16[20,2,256]{2,1,0:T(2,128)(2,1)S(1)} collective-permute-done((bf16[20,2,256]{2,1,0:T(2,128)(2,1)S(1)}, bf16[20,2,256]{2,1,0:T(2,128)(2,1)S(1)}, u32[]{:S(2)}, u32[]{:S(2)}) %collective-permute-start.3) | collective-permute-done | bytes 20512 | tf_op jit(solution)/shard_map/ppermute | solution.py:384
  17.8 1.0 copy-done
  18.8 2.1 %forward.1 = (bf16[1440,256]{1,0:T(8,128)(2,1)S(1)}, f32[96,4,128]{2,1,0:T(4,128)S(1)}) custom-call(s32[1]{0:T(128)} %bitcast.11.count, bf16[16,64,256]{2,1,0:T(8,128)(2,1)S(1)} %bitcast.14, bf16[2,64,256]{2,1,0:T(8,128)(2,1)S(1)} %collective-permute-done.up, bf16[2,64,256]{2,1,0:T(8,128)(2,1)S(1)} %collective-permute-done.1.down, ...), custom_call_target="tpu_custom_call" | custom-call | tf_op jit(solution)/shard_map/forward/pallas_call | solution.py:403
  21.8 37.5 %all_to_all.25.terms = f32[96,4,128]{2,1,0:T(4,128)} all-to-all(f32[96,4,128]{2,1,0:T(4,128)S(1)} %get-tuple-element.18), channel_id=1, replica_groups=mesh['slide'=8,'gy'=12,'gx'=8] {'gy','gx'}, dimensions={0} | all-to-all | bytes 393216 | tf_op jit(solution)/shard_map/all_to_all | solution.py:416
  59.3 1.7 %plane_sum.1 = f32[96,4,128]{2,1,0:T(4,128)} custom-call(s32[1]{0:T(128)} %bitcast.12.count, f32[96,4,128]{2,1,0:T(4,128)} %all_to_all.25.terms), custom_call_target="tpu_custom_call" | custom-call | tf_op jit(solution)/shard_map/plane_sum/pallas_call | solution.py:434
  61.1 5.9 %all-to-all-start.1 = ((f32[96,4,128]{2,1,0:T(4,128)}), f32[96,4,128]{2,1,0:T(4,128)S(1)}, u32[]{:S(2)}, u32[]{:S(2)}) async-start(f32[96,4,128]{2,1,0:T(4,128)} %plane_sum.1), calls=%async_computation.1 | async-start | bytes 393216 | tf_op jit(solution)/shard_map/all_to_all | solution.py:441
  68.4 1.1 copy-done.7
  72.3 9.6 %all-to-all-done.1.gathered = f32[96,4,128]{2,1,0:T(4,128)S(1)} async-done(((f32[96,4,128]{2,1,0:T(4,128)}), f32[96,4,128]{2,1,0:T(4,128)S(1)}, u32[]{:S(2)}, u32[]{:S(2)}) %all-to-all-start.1) | async-done | bytes 196640 | tf_op jit(solution)/shard_map/all_to_all | solution.py:441
  81.9 1.1 copy-done.9
  83.6 11.1 %covariance.1 = (f32[18,80,256]{2,1,0:T(8,128)S(1)}, f32[8,56,256]{2,1,0:T(8,128)S(1)}) custom-call(s32[2]{0:T(128)S(1)} %copy-done.14, s32[1]{0:T(128)S(6)} %copy.13.label, f32[96,4,128]{2,1,0:T(4,128)S(1)} %all-to-all-done.1.gathered, f32[20,80,256]{2,1,0:T(8,128)S(1)} %get-tuple-element.20.ext, bf16[1440,256]{1,0:T(8,128)(2,1)S(1)} %copy-done.9, ...), custom_call_target="tpu_custom_call" | custom-call | tf_op jit(solution)/shard_map/covariance/pallas_call | solution.py:445
  94.7 1.1 copy-done.3
  95.8 19.0 %all_to_all.26.terms = f32[8,56,256]{2,1,0:T(8,128)} all-to-all(f32[8,56,256]{2,1,0:T(8,128)S(1)} %get-tuple-element.23), channel_id=1, replica_groups=mesh['slide'=8,'gy'=12,'gx'=8] {'slide'}, dimensions={0} | all-to-all | bytes 917504 | tf_op jit(solution)/shard_map/all_to_all | solution.py:457
  114.9 1.7 %slide_sum.1 = (bf16[48,256]{1,0:T(8,128)(2,1)}, f32[96,4,128]{2,1,0:T(4,128)}) custom-call(f32[8,56,256]{2,1,0:T(8,128)} %all_to_all.26.terms), custom_call_target="tpu_custom_call" | custom-call | tf_op jit(solution)/shard_map/slide_sum/pallas_call | solution.py:469
  116.6 22.6 %all_to_all.27.spread = f32[96,4,128]{2,1,0:T(4,128)} all-to-all(f32[96,4,128]{2,1,0:T(4,128)} %get-tuple-element.25), channel_id=1, replica_groups=mesh['slide'=8,'gy'=12,'gx'=8] {'gy','gx'}, dimensions={0} | all-to-all | bytes 393216 | tf_op jit(solution)/shard_map/all_to_all | solution.py:479
  139.2 1.8 %join.1 = bf16[8,64,256]{2,1,0:T(8,128)(2,1)} custom-call(bf16[48,256]{1,0:T(8,128)(2,1)} %get-tuple-element.24.shares, f32[96,4,128]{2,1,0:T(4,128)} %all_to_all.27.spread), custom_call_target="tpu_custom_call" | custom-call | tf_op jit(solution)/shard_map/join/pallas_call | solution.py:480
  141.0 6.3 %all-to-all-start.4 = ((bf16[8,64,256]{2,1,0:T(8,128)(2,1)}), bf16[8,64,256]{2,1,0:T(8,128)(2,1)S(1)}, u32[]{:S(2)}, u32[]{:S(2)}) async-start(bf16[8,64,256]{2,1,0:T(8,128)(2,1)} %join.1), calls=%async_computation.4 | async-start | bytes 524288 | tf_op jit(solution)/shard_map/all_to_all | solution.py:487
  147.3 1.8 %spread.1 = bf16[16,64,256]{2,1,0:T(8,128)(2,1)} custom-call(f32[18,80,256]{2,1,0:T(8,128)S(1)} %copy-done.4, f32[9,256]{1,0:T(8,128)S(1)} %reshape.23.weights), custom_call_target="tpu_custom_call" | custom-call | flops 7372800 | bytes 4194304 | tf_op jit(solution)/shard_map/spread/pallas_call | solution.py:458
  149.1 4.7 %all-to-all-done.4.terms = bf16[8,64,256]{2,1,0:T(8,128)(2,1)S(1)} async-done(((bf16[8,64,256]{2,1,0:T(8,128)(2,1)}), bf16[8,64,256]{2,1,0:T(8,128)(2,1)S(1)}, u32[]{:S(2)}, u32[]{:S(2)}) %all-to-all-start.4) | async-done | bytes 262176 | tf_op jit(solution)/shard_map/all_to_all | solution.py:487
  154.5 1.9 %finish.1 = (f32[1,1]{1,0:T(1,128)}, f32[3,3,256]{2,1,0:T(4,128)}, f32[256,256]{1,0:T(8,128)}, f32[2,256,256]{2,1,0:T(8,128)}) custom-call(bf16[8,64,256]{2,1,0:T(8,128)(2,1)} %copy-done.15), custom_call_target="tpu_custom_call" | custom-call | tf_op jit(solution)/shard_map/finish/pallas_call | solution.py:488
  (40 shorter events, 7.7 us)
Async XLA Ops:
  0.6 67.1 %copy-start.5 = (bf16[256,256]{1,0:T(8,128)(2,1)S(1)}, bf16[256,256]{1,0:T(8,128)(2,1)}, u32[]{:S(2)}) copy-start(bf16[256,256]{1,0:T(8,128)(2,1)} %point.3) | copy-start | bytes 393220
  1.6 7.7 %collective-permute-start.1 = (bf16[2,64,256]{2,1,0:T(8,128)(2,1)S(1)}, bf16[2,64,256]{2,1,0:T(8,128)(2,1)S(1)}, u32[]{:S(2)}, u32[]{:S(2)}) collective-permute-start(bf16[2,64,256]{2,1,0:T(8,128)(2,1)S(1)} %get-tuple-element.33), channel_id=1, source_target_pairs={{8,0},{16,8},{24,16},{32,24},{40,32},{48,40},{56,48},{64,56},{72,6... | collective-permute-start | bytes 196616 | tf_op jit(solution)/shard_map/ppermute | solution.py:384
  2.9 6.8 %collective-permute-start = (bf16[2,64,256]{2,1,0:T(8,128)(2,1)S(1)}, bf16[2,64,256]{2,1,0:T(8,128)(2,1)S(1)}, u32[]{:S(2)}, u32[]{:S(2)}) collective-permute-start(bf16[2,64,256]{2,1,0:T(8,128)(2,1)S(1)} %get-tuple-element.34), channel_id=1, source_target_pairs={{0,8},{8,16},{16,24},{24,32},{32,40},{40,48},{48,56},{56,64},{64,7... | collective-permute-start | bytes 196616 | tf_op jit(solution)/shard_map/ppermute | solution.py:384
  9.7 5.9 %collective-permute-start.2 = (bf16[20,2,256]{2,1,0:T(2,128)(2,1)S(1)}, bf16[20,2,256]{2,1,0:T(2,128)(2,1)S(1)}, u32[]{:S(2)}, u32[]{:S(2)}) collective-permute-start(bf16[20,2,256]{2,1,0:T(2,128)(2,1)S(1)} %pad_maximum_fusion), channel_id=1, source_target_pairs={{0,1},{1,2},{2,3},{3,4},{4,5},{5,6},{6,7},{8,9},{9,10},{10,11},{11... | collective-permute-start | bytes 61448 | tf_op jit(solution)/shard_map/ppermute | solution.py:384
  12.9 4.8 %collective-permute-start.3 = (bf16[20,2,256]{2,1,0:T(2,128)(2,1)S(1)}, bf16[20,2,256]{2,1,0:T(2,128)(2,1)S(1)}, u32[]{:S(2)}, u32[]{:S(2)}) collective-permute-start(bf16[20,2,256]{2,1,0:T(2,128)(2,1)S(1)} %pad_maximum_fusion.1), channel_id=1, source_target_pairs={{1,0},{2,1},{3,2},{4,3},{5,4},{6,5},{7,6},{9,8},{10,9},{11,10},{12... | collective-permute-start | bytes 61448 | tf_op jit(solution)/shard_map/ppermute | solution.py:384
  15.6 51.4 %copy-start.10 = (bf16[20,2,256]{2,1,0:T(2,128)(2,1)}, bf16[20,2,256]{2,1,0:T(2,128)(2,1)S(1)}, u32[]{:S(2)}) copy-start(bf16[20,2,256]{2,1,0:T(2,128)(2,1)S(1)} %collective-permute-done.2.left) | copy-start | bytes 61444
  17.8 49.3 %copy-start.12 = (bf16[20,2,256]{2,1,0:T(2,128)(2,1)}, bf16[20,2,256]{2,1,0:T(2,128)(2,1)S(1)}, u32[]{:S(2)}) copy-start(bf16[20,2,256]{2,1,0:T(2,128)(2,1)S(1)} %collective-permute-done.3.right) | copy-start | bytes 61444
  17.8 1.1 copy-start
  18.8 49.6 %copy-start.1 = (bf16[1,16,64,256]{3,2,1,0:T(8,128)(2,1)S(1)}, bf16[1,16,64,256]{3,2,1,0:T(8,128)(2,1)}, u32[]{:S(2)}) copy-start(bf16[1,16,64,256]{3,2,1,0:T(8,128)(2,1)} %param.6) | copy-start | bytes 1572868
  18.8 49.6 %copy-start.2 = (f32[2,256,256]{2,1,0:T(8,128)S(1)}, f32[2,256,256]{2,1,0:T(8,128)}, u32[]{:S(2)}) copy-start(f32[2,256,256]{2,1,0:T(8,128)} %classifier.3) | copy-start | bytes 1572868
  20.9 0.9 copy-start.6
  61.1 20.8 %all-to-all-start.1 = ((f32[96,4,128]{2,1,0:T(4,128)}), f32[96,4,128]{2,1,0:T(4,128)S(1)}, u32[]{:S(2)}, u32[]{:S(2)}) async-start(f32[96,4,128]{2,1,0:T(4,128)} %plane_sum.1), calls=%async_computation.1 | async-start | bytes 393216 | tf_op jit(solution)/shard_map/all_to_all | solution.py:441
  68.4 1.1 copy-start.7
  69.5 0.7 copy-start.11
  70.2 0.7 copy-start.13
  71.4 0.9 copy-start.8
  81.9 1.1 copy-start.9
  83.0 0.6 copy-start.14
  94.7 1.2 copy-start.3
  95.8 51.4 %copy-start.4 = (f32[18,80,256]{2,1,0:T(8,128)S(1)}, f32[18,80,256]{2,1,0:T(8,128)}, u32[]{:S(2)}) copy-start(f32[18,80,256]{2,1,0:T(8,128)} %copy-done.3) | copy-start | bytes 4423684
  141.0 12.8 %all-to-all-start.4 = ((bf16[8,64,256]{2,1,0:T(8,128)(2,1)}), bf16[8,64,256]{2,1,0:T(8,128)(2,1)S(1)}, u32[]{:S(2)}, u32[]{:S(2)}) async-start(bf16[8,64,256]{2,1,0:T(8,128)(2,1)} %join.1), calls=%async_computation.4 | async-start | bytes 524288 | tf_op jit(solution)/shard_map/all_to_all | solution.py:487
  153.8 0.7 copy-start.15

commit v3 on v2

--- a/solution.py
+++ b/solution.py
@@ -15,7 +15,8 @@
 BF16 = jnp.bfloat16
 VMEM = pl.BlockSpec(memory_space=pltpu.VMEM)
 SMEM = pl.BlockSpec(memory_space=pltpu.SMEM)
-PARAMS = pltpu.CompilerParams(vmem_limit_bytes=24 * 1024 * 1024)
+PARAMS = pltpu.CompilerParams(vmem_limit_bytes=16 * 1024 * 1024)
+SMALL = pltpu.CompilerParams(vmem_limit_bytes=4 * 1024 * 1024)
 
 
 def iota(shape, dim):
@@ -92,7 +93,7 @@
 
     for lane in range(0, channels, LANES):
         part = slice(lane, lane + LANES)
-        taps = [weights[k : k + 1, part] for k in range(9)]
+        taps = [weights[k // 3, k % 3 : k % 3 + 1, part].astype(F32) for k in range(9)]
 
         def body(r, carry, part=part, taps=taps):
             rows = [ext[r + a, :, part] for a in range(3)]
@@ -304,7 +305,7 @@
     height, width, channels = gradient.shape
     for lane in range(0, channels, LANES):
         part = slice(lane, lane + LANES)
-        taps = [weights[k : k + 1, part] for k in range(9)]
+        taps = [weights[k // 3, k % 3 : k % 3 + 1, part].astype(F32) for k in range(9)]
 
         def body(i, carry, part=part, taps=taps):
             rows = [back[i + a, :, part] for a in range(3)]
@@ -390,7 +391,6 @@
 
     left, right = edges(strip(0), strip(width - RIM), "gx")
 
-    weights = depth_weight.reshape(9, channels).astype(F32)
     point_turned = point_weight.T
     count = valid_count.reshape(1)
     place = jnp.stack([lax.axis_index("gy"), lax.axis_index("gx")]).astype(jnp.int32)
@@ -411,7 +411,7 @@
         scratch_shapes=[pltpu.VMEM(ext_shape, F32), pltpu.VMEM((height * width, channels), BF16)],
         compiler_params=PARAMS,
         name="forward",
-    )(count, *halo, weights)
+    )(count, *halo, depth_weight)
 
     packed = lax.all_to_all(packed, ("gy", "gx"), 0, 0)
 
@@ -436,6 +436,7 @@
         out_shape=jax.ShapeDtypeStruct((planes, chunks + 1, LANES), F32),
         in_specs=[SMEM, VMEM],
         out_specs=VMEM,
+        compiler_params=SMALL,
         name="plane_sum",
     )(count, packed)
     gathered = lax.all_to_all(packed, ("gy", "gx"), 0, 0)
@@ -465,7 +466,7 @@
             flops=20 * pixels * channels, bytes_accessed=4 << 20, transcendentals=0
         ),
         name="spread",
-    )(back, weights)
+    )(back, depth_weight)
     shares, spread = pl.pallas_call(
         functools.partial(slide_sum_kernel, rd),
         out_shape=(
@@ -474,6 +475,7 @@
         ),
         in_specs=[VMEM],
         out_specs=(VMEM, VMEM),
+        compiler_params=SMALL,
         name="slide_sum",
     )(received)
     spread = lax.all_to_all(spread, ("gy", "gx"), 0, 0)
@@ -482,6 +484,7 @@
         out_shape=jax.ShapeDtypeStruct((slides, main + 16, channels), BF16),
         in_specs=[VMEM, VMEM],
         out_specs=VMEM,
+        compiler_params=SMALL,
         name="join",
     )(shares, spread)
     joined = lax.all_to_all(joined, "slide", 0, 0)
@@ -495,6 +498,7 @@
         ),
         in_specs=[VMEM],
         out_specs=(VMEM, VMEM, VMEM, VMEM),
+        compiler_params=SMALL,
         name="finish",
     )(joined)
     return loss.reshape(()), depth, point, classes, gradient[None]

time: 157 us -> 150 us (0.955)
  Pallas kernels: 22.6 us -> 18 us
  blocking collectives: 79.2 us -> 77.5 us
    pallas_call x1, Pallas kernels: 1.75 us -> 0.05 us  [per_device(): pl.pallas_call(functools.partial(slide_sum_kernel, rd), out_shape=(jax.Sh...]
  transfers between devices with their start and end apart: 6 -> 6, of which waited for: 4 -> 4; matrix products, arithmetic and copies ran while one was open for 1% -> 1% of each run, Pallas kernels for 1% -> 2%
where the time goes in v3:
time: 150 us
  blocking collectives  77.5 us (52%)
  starting transfers between devices  23.4 us (16%)
  waiting for transfers between devices  18 us (12%)
  Pallas kernels  18 us (12%)
  local copies, waits for them, and re-layouts  10.3 us (7%)
  between operations  2.11 us (1%)
    all_to_all x1, blocking collectives, per_device(): packed = lax.all_to_all(packed, ('gy', 'gx'), 0, 0)  37.4 us
    all_to_all x1, blocking collectives, per_device(): spread = lax.all_to_all(spread, ('gy', 'gx'), 0, 0)  21.1 us
    all_to_all x1, blocking collectives, per_device(): received = lax.all_to_all(sent, 'slide', 0, 0)  18.9 us
    pallas_call x1, Pallas kernels, per_device(): pl.pallas_call(functools.partial(cov_kernel, grid_y, grid_x, slides), out...  11.1 us
    all_to_all x1, waiting for transfers between devices, per_device(): gathered = lax.all_to_all(packed, ('gy', 'gx'), 0, 0)  10.1 us
    ppermute x2, starting transfers between devices, edges(): lax.ppermute(high_part, axis, forward)  8.66 us
    unnamed x33, local copies, waits for them, and re-layouts  8.45 us
    all_to_all x1, starting transfers between devices, per_device(): joined = lax.all_to_all(joined, 'slide', 0, 0)  6.26 us
  transfers between devices with their start and end apart: 6, of which 4 were waited for; matrix products, arithmetic and copies ran while one was open for 1% of the time, Pallas kernels for 2%

profile of v3, /device:TPU:1, one launch (start us, length us, event | category | flops | bytes accessed | tf_op | source)
XLA Modules:
  0.0 149.5 jit_solution(5989116134075465307)
XLA Ops:
  0.6 0.9 slice_bitcast_fusion
  1.6 1.3 collective-permute-start.1
  2.9 5.5 %collective-permute-start = (bf16[2,64,256]{2,1,0:T(8,128)(2,1)S(1)}, bf16[2,64,256]{2,1,0:T(8,128)(2,1)S(1)}, u32[]{:S(2)}, u32[]{:S(2)}) collective-permute-start(bf16[2,64,256]{2,1,0:T(8,128)(2,1)S(1)} %get-tuple-element.34), channel_id=1, source_target_pairs={{0,8},{8,16},{16,24},{24,32},{32,40},{40,48},{48,56},{56,64},{64,7... | collective-permute-start | bytes 196616 | tf_op jit(solution)/shard_map/ppermute | solution.py:385
  8.3 0.9 fusion
  9.7 3.2 %collective-permute-start.2 = (bf16[20,2,256]{2,1,0:T(2,128)(2,1)S(1)}, bf16[20,2,256]{2,1,0:T(2,128)(2,1)S(1)}, u32[]{:S(2)}, u32[]{:S(2)}) collective-permute-start(bf16[20,2,256]{2,1,0:T(2,128)(2,1)S(1)} %pad_maximum_fusion), channel_id=1, source_target_pairs={{0,1},{1,2},{2,3},{3,4},{4,5},{5,6},{6,7},{8,9},{9,10},{10,11},{11... | collective-permute-start | bytes 61448 | tf_op jit(solution)/shard_map/ppermute | solution.py:385
  12.9 1.3 collective-permute-start.3
  14.9 2.9 %collective-permute-done.3.right = bf16[20,2,256]{2,1,0:T(2,128)(2,1)S(1)} collective-permute-done((bf16[20,2,256]{2,1,0:T(2,128)(2,1)S(1)}, bf16[20,2,256]{2,1,0:T(2,128)(2,1)S(1)}, u32[]{:S(2)}, u32[]{:S(2)}) %collective-permute-start.3) | collective-permute-done | bytes 20512 | tf_op jit(solution)/shard_map/ppermute | solution.py:385
  17.8 1.0 copy-done
  19.5 2.1 %forward.1 = (bf16[1440,256]{1,0:T(8,128)(2,1)S(1)}, f32[96,4,128]{2,1,0:T(4,128)S(1)}) custom-call(s32[1]{0:T(128)} %bitcast.11.count, bf16[16,64,256]{2,1,0:T(8,128)(2,1)S(1)} %bitcast.14, bf16[2,64,256]{2,1,0:T(8,128)(2,1)S(1)} %collective-permute-done.up, bf16[2,64,256]{2,1,0:T(8,128)(2,1)S(1)} %collective-permute-done.1.down, ...), custom_call_target="tpu_custom_call" | custom-call | tf_op jit(solution)/shard_map/forward/pallas_call | solution.py:403
  21.6 0.9 copy-done.6
  22.5 37.4 %all_to_all.25.terms = f32[96,4,128]{2,1,0:T(4,128)S(1)} all-to-all(f32[96,4,128]{2,1,0:T(4,128)S(1)} %get-tuple-element.18), channel_id=1, replica_groups=mesh['slide'=8,'gy'=12,'gx'=8] {'gy','gx'}, dimensions={0} | all-to-all | bytes 393216 | tf_op jit(solution)/shard_map/all_to_all | solution.py:416
  60.7 5.9 %all-to-all-start.1 = ((f32[96,4,128]{2,1,0:T(4,128)}), f32[96,4,128]{2,1,0:T(4,128)S(1)}, u32[]{:S(2)}, u32[]{:S(2)}) async-start(f32[96,4,128]{2,1,0:T(4,128)} %plane_sum.1), calls=%async_computation.1 | async-start | bytes 393216 | tf_op jit(solution)/shard_map/all_to_all | solution.py:442
  67.5 1.1 copy-done.7
  70.6 0.9 copy-done.8
  71.4 10.1 %all-to-all-done.1.gathered = f32[96,4,128]{2,1,0:T(4,128)S(1)} async-done(((f32[96,4,128]{2,1,0:T(4,128)}), f32[96,4,128]{2,1,0:T(4,128)S(1)}, u32[]{:S(2)}, u32[]{:S(2)}) %all-to-all-start.1) | async-done | bytes 196640 | tf_op jit(solution)/shard_map/all_to_all | solution.py:442
  81.5 1.1 copy-done.9
  82.7 11.1 %covariance.1 = (f32[18,80,256]{2,1,0:T(8,128)S(1)}, f32[8,56,256]{2,1,0:T(8,128)S(1)}) custom-call(s32[2]{0:T(128)S(1)} %pad_add_fusion.place, s32[1]{0:T(128)S(6)} %copy.13.label, f32[96,4,128]{2,1,0:T(4,128)S(1)} %all-to-all-done.1.gathered, f32[20,80,256]{2,1,0:T(8,128)S(1)} %get-tuple-element.20.ext, bf16[1440,256]{1,0:T(8,128)(2,1)S(1)} %copy-done.9, ...), custom_call_target="tpu_custom_call" | custom-call | tf_op jit(solution)/shard_map/covariance/pallas_call | solution.py:446
  93.7 1.1 copy-done.3
  94.9 18.9 %all_to_all.26.terms = f32[8,56,256]{2,1,0:T(8,128)S(1)} all-to-all(f32[8,56,256]{2,1,0:T(8,128)S(1)} %get-tuple-element.23), channel_id=1, replica_groups=mesh['slide'=8,'gy'=12,'gx'=8] {'slide'}, dimensions={0} | all-to-all | bytes 917504 | tf_op jit(solution)/shard_map/all_to_all | solution.py:458
  113.9 21.1 %all_to_all.27.spread = f32[96,4,128]{2,1,0:T(4,128)S(1)} all-to-all(f32[96,4,128]{2,1,0:T(4,128)S(1)} %get-tuple-element.25), channel_id=1, replica_groups=mesh['slide'=8,'gy'=12,'gx'=8] {'gy','gx'}, dimensions={0} | all-to-all | bytes 393216 | tf_op jit(solution)/shard_map/all_to_all | solution.py:481
  135.8 6.3 %all-to-all-start.4 = ((bf16[8,64,256]{2,1,0:T(8,128)(2,1)}), bf16[8,64,256]{2,1,0:T(8,128)(2,1)S(1)}, u32[]{:S(2)}, u32[]{:S(2)}) async-start(bf16[8,64,256]{2,1,0:T(8,128)(2,1)} %join.1), calls=%async_computation.4 | async-start | bytes 524288 | tf_op jit(solution)/shard_map/all_to_all | solution.py:490
  142.1 1.8 %spread.1 = bf16[16,64,256]{2,1,0:T(8,128)(2,1)} custom-call(f32[18,80,256]{2,1,0:T(8,128)S(1)} %copy-done.4, bf16[3,3,256]{2,1,0:T(4,128)(2,1)S(1)} %copy-done.15), custom_call_target="tpu_custom_call" | custom-call | flops 7372800 | bytes 4194304 | tf_op jit(solution)/shard_map/spread/pallas_call | solution.py:459
  143.9 4.7 %all-to-all-done.4.terms = bf16[8,64,256]{2,1,0:T(8,128)(2,1)S(1)} async-done(((bf16[8,64,256]{2,1,0:T(8,128)(2,1)}), bf16[8,64,256]{2,1,0:T(8,128)(2,1)S(1)}, u32[]{:S(2)}, u32[]{:S(2)}) %all-to-all-start.4) | async-done | bytes 262176 | tf_op jit(solution)/shard_map/all_to_all | solution.py:490
  148.6 0.9 finish.1
  (39 shorter events, 5.0 us)
Async XLA Ops:
  0.6 66.7 %copy-start.5 = (bf16[256,256]{1,0:T(8,128)(2,1)S(1)}, bf16[256,256]{1,0:T(8,128)(2,1)}, u32[]{:S(2)}) copy-start(bf16[256,256]{1,0:T(8,128)(2,1)} %point.3) | copy-start | bytes 393220
  1.6 7.7 %collective-permute-start.1 = (bf16[2,64,256]{2,1,0:T(8,128)(2,1)S(1)}, bf16[2,64,256]{2,1,0:T(8,128)(2,1)S(1)}, u32[]{:S(2)}, u32[]{:S(2)}) collective-permute-start(bf16[2,64,256]{2,1,0:T(8,128)(2,1)S(1)} %get-tuple-element.33), channel_id=1, source_target_pairs={{8,0},{16,8},{24,16},{32,24},{40,32},{48,40},{56,48},{64,56},{72,6... | collective-permute-start | bytes 196616 | tf_op jit(solution)/shard_map/ppermute | solution.py:385
  2.9 6.8 %collective-permute-start = (bf16[2,64,256]{2,1,0:T(8,128)(2,1)S(1)}, bf16[2,64,256]{2,1,0:T(8,128)(2,1)S(1)}, u32[]{:S(2)}, u32[]{:S(2)}) collective-permute-start(bf16[2,64,256]{2,1,0:T(8,128)(2,1)S(1)} %get-tuple-element.34), channel_id=1, source_target_pairs={{0,8},{8,16},{16,24},{24,32},{32,40},{40,48},{48,56},{56,64},{64,7... | collective-permute-start | bytes 196616 | tf_op jit(solution)/shard_map/ppermute | solution.py:385
  9.7 5.2 %collective-permute-start.2 = (bf16[20,2,256]{2,1,0:T(2,128)(2,1)S(1)}, bf16[20,2,256]{2,1,0:T(2,128)(2,1)S(1)}, u32[]{:S(2)}, u32[]{:S(2)}) collective-permute-start(bf16[20,2,256]{2,1,0:T(2,128)(2,1)S(1)} %pad_maximum_fusion), channel_id=1, source_target_pairs={{0,1},{1,2},{2,3},{3,4},{4,5},{5,6},{6,7},{8,9},{9,10},{10,11},{11... | collective-permute-start | bytes 61448 | tf_op jit(solution)/shard_map/ppermute | solution.py:385
  12.9 4.8 %collective-permute-start.3 = (bf16[20,2,256]{2,1,0:T(2,128)(2,1)S(1)}, bf16[20,2,256]{2,1,0:T(2,128)(2,1)S(1)}, u32[]{:S(2)}, u32[]{:S(2)}) collective-permute-start(bf16[20,2,256]{2,1,0:T(2,128)(2,1)S(1)} %pad_maximum_fusion.1), channel_id=1, source_target_pairs={{1,0},{2,1},{3,2},{4,3},{5,4},{6,5},{7,6},{9,8},{10,9},{11,10},{12... | collective-permute-start | bytes 61448 | tf_op jit(solution)/shard_map/ppermute | solution.py:385
  14.9 45.0 %copy-start.10 = (bf16[20,2,256]{2,1,0:T(2,128)(2,1)}, bf16[20,2,256]{2,1,0:T(2,128)(2,1)S(1)}, u32[]{:S(2)}) copy-start(bf16[20,2,256]{2,1,0:T(2,128)(2,1)S(1)} %collective-permute-done.2.left) | copy-start | bytes 61444
  17.8 42.2 %copy-start.12 = (bf16[20,2,256]{2,1,0:T(2,128)(2,1)}, bf16[20,2,256]{2,1,0:T(2,128)(2,1)S(1)}, u32[]{:S(2)}) copy-start(bf16[20,2,256]{2,1,0:T(2,128)(2,1)S(1)} %collective-permute-done.3.right) | copy-start | bytes 61444
  17.8 1.1 copy-start
  18.8 0.7 copy-start.14
  19.5 48.0 %copy-start.1 = (bf16[1,16,64,256]{3,2,1,0:T(8,128)(2,1)S(1)}, bf16[1,16,64,256]{3,2,1,0:T(8,128)(2,1)}, u32[]{:S(2)}) copy-start(bf16[1,16,64,256]{3,2,1,0:T(8,128)(2,1)} %param.6) | copy-start | bytes 1572868
  19.5 48.0 %copy-start.2 = (f32[2,256,256]{2,1,0:T(8,128)S(1)}, f32[2,256,256]{2,1,0:T(8,128)}, u32[]{:S(2)}) copy-start(f32[2,256,256]{2,1,0:T(8,128)} %classifier.3) | copy-start | bytes 1572868
  21.6 0.9 copy-start.6
  60.7 20.8 %all-to-all-start.1 = ((f32[96,4,128]{2,1,0:T(4,128)}), f32[96,4,128]{2,1,0:T(4,128)S(1)}, u32[]{:S(2)}, u32[]{:S(2)}) async-start(f32[96,4,128]{2,1,0:T(4,128)} %plane_sum.1), calls=%async_computation.1 | async-start | bytes 393216 | tf_op jit(solution)/shard_map/all_to_all | solution.py:442
  67.5 1.1 copy-start.7
  68.7 0.7 copy-start.11
  69.4 0.7 copy-start.13
  70.6 0.9 copy-start.8
  81.5 1.1 copy-start.9
  93.7 1.2 copy-start.3
  94.9 47.2 %copy-start.15 = (bf16[3,3,256]{2,1,0:T(4,128)(2,1)S(1)}, bf16[3,3,256]{2,1,0:T(4,128)(2,1)}, u32[]{:S(2)}) copy-start(bf16[3,3,256]{2,1,0:T(4,128)(2,1)} %weights.3) | copy-start | bytes 13828
  94.9 47.2 %copy-start.4 = (f32[18,80,256]{2,1,0:T(8,128)S(1)}, f32[18,80,256]{2,1,0:T(8,128)}, u32[]{:S(2)}) copy-start(f32[18,80,256]{2,1,0:T(8,128)} %copy-done.3) | copy-start | bytes 4423684
  135.8 12.8 %all-to-all-start.4 = ((bf16[8,64,256]{2,1,0:T(8,128)(2,1)}), bf16[8,64,256]{2,1,0:T(8,128)(2,1)S(1)}, u32[]{:S(2)}, u32[]{:S(2)}) async-start(bf16[8,64,256]{2,1,0:T(8,128)(2,1)} %join.1), calls=%async_computation.4 | async-start | bytes 524288 | tf_op jit(solution)/shard_map/all_to_all | solution.py:490

commit v4 on v3

--- a/solution.py
+++ b/solution.py
@@ -46,6 +46,10 @@
     return tuple(jnp.concatenate([pair[i] for pair in pairs], axis=0) for i in range(2))
 
 
+def beside(*pairs):
+    return tuple(jnp.concatenate([pair[i] for pair in pairs], axis=1) for i in range(2))
+
+
 def shifted(x, step):
     return pltpu.roll(x, step % x.shape[0], 0)
 
@@ -83,8 +87,21 @@
     ext[:, LEFT + width : LEFT + width + RIM, :] = right[...].astype(F32)
 
 
+def load_kernel(
+    tile, weights, point, classifier, tile_out, low, high, taps, turned, toward
+):
+    width = tile.shape[1]
+    tile_out[...] = tile[...]
+    low[...] = tile[:, :RIM, :]
+    high[...] = tile[:, width - RIM :, :]
+    taps[...] = jnp.concatenate([weights[a].astype(F32) for a in range(3)], axis=0)
+    turned[...] = point[...].astype(F32).T.astype(BF16)
+    gap = classifier[0] - classifier[1]
+    toward[...] = gap + gap.T
+
+
 def forward_kernel(
-    planes, count, tile, up, down, left, right, weights, hidden, packed, ext, inner
+    planes, count, tile, up, down, left, right, weights, point, mapped, packed, ext, hidden, inner
 ):
     height, width, channels = tile.shape
     wide = ext.shape[1]
@@ -93,7 +110,7 @@
 
     for lane in range(0, channels, LANES):
         part = slice(lane, lane + LANES)
-        taps = [weights[k // 3, k % 3 : k % 3 + 1, part].astype(F32) for k in range(9)]
+        taps = [weights[k : k + 1, part] for k in range(9)]
 
         def body(r, carry, part=part, taps=taps):
             rows = [ext[r + a, :, part] for a in range(3)]
@@ -114,6 +131,7 @@
 
     kept = inner[...]
     gram = lax.dot_general(kept, kept, (((0,), (0,)), ((), ())), preferred_element_type=F32)
+    mapped[...] = dot(hidden[...], point[...]).astype(BF16)
     sums = jnp.sum(kept.astype(F32), axis=0, keepdims=True)
     upper, both, diag = tri_pack(gram)
     chunks = packed.shape[1] - 1
@@ -135,18 +153,9 @@
     out[...] = jnp.broadcast_to(summed[None], out.shape)
 
 
-def prepare_kernel(
-    hidden, point, tile, up, down, left, right, classifier, mapped, ext, toward
-):
-    mapped[...] = dot(hidden[...], point[...]).astype(BF16)
-    assemble(ext, tile, up, down, left, right)
-    gap = classifier[0] - classifier[1]
-    toward[...] = gap + gap.T
-
-
 def cov_kernel(
     grid_y, grid_x, slides, place, label, gathered, ext, mapped, toward_ref, point, point_turned,
-    classifier, back, sent,
+    classifier, back_out, sent, back, sem,
 ):
     planes = grid_y * grid_x
     wide, channels = ext.shape[1:]
@@ -184,25 +193,27 @@
     wmat, ymat, dw, dy = start, start, toward, toward
     for step in range(ITERS):
         w_pair, dw_pair = split(wmat), split(dw)
+        both = beside(w_pair, dw_pair)
         if step == 0:
-            square = mm(w_pair, w_pair)
-            cross = mm(w_pair, dw_pair)
+            first = mm(w_pair, both)
+            square, cross = first[:, :channels], first[:, channels:]
             yw, dyw = square, cross + cross.T
+        elif step + 1 < ITERS:
+            first = mm(stack(w_pair, split(ymat)), both)
+            square, cross = first[:channels, :channels], first[:channels, channels:]
+            yw = first[channels:, :channels]
+            dyw = first[channels:, channels:] + mm(split(dy), w_pair)
         else:
-            first = mm(stack(w_pair, split(ymat), split(dy)), w_pair)
-            second = mm(stack(w_pair, split(ymat)), dw_pair)
-            square, yw = first[:channels], first[channels : 2 * channels]
-            cross = second[:channels]
-            dyw = first[2 * channels :] + second[channels:]
+            first = mm(split(ymat), both)
+            yw = first[:, :channels]
+            dyw = first[:, channels:] + mm(split(dy), w_pair)
         ymat = 1.5 * ymat - 0.5 * yw
         dy = 1.5 * dy - 0.5 * dyw
         if step + 1 < ITERS:
             dsquare = cross + cross.T
-            square_pair = split(square)
-            third = mm(stack(square_pair, split(dsquare)), w_pair)
-            cube = third[:channels]
-            dcube = third[channels:] + mm(square_pair, dw_pair)
-            wmat = 2.25 * wmat - 1.5 * square + 0.25 * cube
+            third = mm(split(square), both)
+            dcube = third[:, channels:] + mm(split(dsquare), w_pair)
+            wmat = 2.25 * wmat - 1.5 * square + 0.25 * third[:, :channels]
             dw = 2.25 * dw - 1.5 * dsquare + 0.25 * dcube
 
     root = jnp.sqrt(trace)
@@ -257,8 +268,9 @@
         raster = (tile_row * width + inner_col).astype(F32)
         pieces.append(jnp.where(raster < limit, both[r * wide : (r + 1) * wide], 0.0).astype(BF16))
     back_mapped = jnp.concatenate(pieces, axis=0)
-    back_hidden = dot(back_mapped, mixing_turned).astype(BF16)
-    back[...] = back_hidden.astype(F32).reshape(height + 2, wide, channels)
+    back[...] = dot(back_mapped, mixing_turned).astype(BF16)
+    copy = pltpu.make_async_copy(back, back_out, sem)
+    copy.start()
 
     depth = []
     for lane in range(0, channels, LANES):
@@ -267,7 +279,8 @@
         within = (column >= LEFT) & (column < LEFT + width)
 
         def body(i, sums, part=part, within=within):
-            own = jnp.where(within, back[i + 1, :, part], 0.0)
+            start = pl.multiple_of((i + 1) * wide, 16)
+            own = jnp.where(within, back[pl.ds(start, wide), part].astype(F32), 0.0)
             moved_own = [shifted(own, -1), own, shifted(own, 1)]
             feats = [ext[i + 1 + a, :, part] for a in range(3)]
             out = []
@@ -299,16 +312,21 @@
         sent[k, rp + rc : rp + rc + 8, :] = jnp.concatenate(
             [small[k * rd : (k + 1) * rd]] + pad, axis=0
         )
+    copy.wait()
 
 
 def spread_kernel(back, weights, gradient):
     height, width, channels = gradient.shape
+    wide = width + 2 * LEFT
     for lane in range(0, channels, LANES):
         part = slice(lane, lane + LANES)
-        taps = [weights[k // 3, k % 3 : k % 3 + 1, part].astype(F32) for k in range(9)]
+        taps = [weights[k : k + 1, part] for k in range(9)]
 
         def body(i, carry, part=part, taps=taps):
-            rows = [back[i + a, :, part] for a in range(3)]
+            rows = [
+                back[pl.ds(pl.multiple_of((i + a) * wide, 16), wide), part].astype(F32)
+                for a in range(3)
+            ]
             cols = [sum(rows[2 - a] * taps[3 * a + b] for a in range(3)) for b in range(3)]
             value = cols[1] + shifted(cols[0], -1) + shifted(cols[2], 1)
             gradient[i, :, part] = value[LEFT : LEFT + width].astype(BF16)
@@ -386,50 +404,54 @@
 
     up, down = edges(tile[:RIM], tile[height - RIM :], "gy")
 
-    def strip(start):
-        return jnp.concatenate([part[:, start : start + RIM] for part in (up, tile, down)], axis=0)
-
-    left, right = edges(strip(0), strip(width - RIM), "gx")
-
-    point_turned = point_weight.T
+    tile, low, high, weights, point_turned, toward = pl.pallas_call(
+        load_kernel,
+        out_shape=(
+            jax.ShapeDtypeStruct(tile.shape, BF16),
+            jax.ShapeDtypeStruct((height, RIM, channels), BF16),
+            jax.ShapeDtypeStruct((height, RIM, channels), BF16),
+            jax.ShapeDtypeStruct((9, channels), F32),
+            jax.ShapeDtypeStruct((channels, channels), BF16),
+            jax.ShapeDtypeStruct((channels, channels), F32),
+        ),
+        in_specs=[VMEM] * 4,
+        out_specs=(VMEM,) * 6,
+        compiler_params=SMALL,
+        name="load",
+    )(tile, depth_weight, point_weight, classifier)
+
+    def strip(own, start):
+        ends = [part[:, start : start + RIM] for part in (up, down)]
+        return jnp.concatenate([ends[0], own, ends[1]], axis=0)
+
+    left, right = edges(strip(low, 0), strip(high, width - RIM), "gx")
+
     count = valid_count.reshape(1)
     place = jnp.stack([lax.axis_index("gy"), lax.axis_index("gx")]).astype(jnp.int32)
     halo = (tile, up, down, left, right)
     chunks = -(-(channels + 3) // planes)
-
     pixels = (height + 2) * wide
     ext_shape = (height + 2 * RIM, wide, channels)
 
-    hidden, packed = pl.pallas_call(
+    mapped, packed, ext = pl.pallas_call(
         functools.partial(forward_kernel, planes),
         out_shape=(
             jax.ShapeDtypeStruct((pixels, channels), BF16),
             jax.ShapeDtypeStruct((planes, chunks + 1, LANES), F32),
+            jax.ShapeDtypeStruct(ext_shape, F32),
         ),
-        in_specs=[SMEM] + [VMEM] * 6,
-        out_specs=(VMEM, VMEM),
-        scratch_shapes=[pltpu.VMEM(ext_shape, F32), pltpu.VMEM((height * width, channels), BF16)],
+        in_specs=[SMEM] + [VMEM] * 7,
+        out_specs=(VMEM, VMEM, VMEM),
+        scratch_shapes=[
+            pltpu.VMEM((pixels, channels), BF16),
+            pltpu.VMEM((height * width, channels), BF16),
+        ],
         compiler_params=PARAMS,
         name="forward",
-    )(count, *halo, depth_weight)
+    )(count, *halo, weights, point_weight)
+    packed, place, labels = lax.optimization_barrier((packed, place, labels))
 
     packed = lax.all_to_all(packed, ("gy", "gx"), 0, 0)
-
-    mapped, ext, toward = pl.pallas_call(
-        prepare_kernel,
-        out_shape=(
-            jax.ShapeDtypeStruct((pixels, channels), BF16),
-            jax.ShapeDtypeStruct(ext_shape, F32),
-            jax.ShapeDtypeStruct((channels, channels), F32),
-        ),
-        in_specs=[VMEM] * 8,
-        out_specs=(VMEM, VMEM, VMEM),
-        compiler_params=PARAMS,
-        cost_estimate=pl.CostEstimate(
-            flops=2 * pixels * channels * channels, bytes_accessed=5 << 20, transcendentals=0
-        ),
-        name="prepare",
-    )(hidden, point_weight, *halo, classifier)
 
     packed = pl.pallas_call(
         plane_sum_kernel,
@@ -446,11 +468,12 @@
     back, sent = pl.pallas_call(
         functools.partial(cov_kernel, grid_y, grid_x, slides),
         out_shape=(
-            jax.ShapeDtypeStruct((height + 2, wide, channels), F32),
+            jax.ShapeDtypeStruct((pixels, channels), BF16),
             jax.ShapeDtypeStruct((slides, main + 8, channels), F32),
         ),
         in_specs=[SMEM, SMEM] + [VMEM] * 7,
-        out_specs=(VMEM, VMEM),
+        out_specs=(pl.BlockSpec(memory_space=pltpu.HBM), VMEM),
+        scratch_shapes=[pltpu.VMEM((pixels, channels), BF16), pltpu.SemaphoreType.DMA],
         compiler_params=PARAMS,
         name="covariance",
     )(place, labels, gathered, ext, mapped, toward, point_weight, point_turned, classifier)
@@ -466,7 +489,7 @@
             flops=20 * pixels * channels, bytes_accessed=4 << 20, transcendentals=0
         ),
         name="spread",
-    )(back, depth_weight)
+    )(back, weights)
     shares, spread = pl.pallas_call(
         functools.partial(slide_sum_kernel, rd),
         out_shape=(

time: 150 us -> 148 us (0.987)
  Pallas kernels: 18 us -> 15.7 us
  local copies, waits for them, and re-layouts: 10.3 us -> 8.15 us
    all_to_all x1, waiting for transfers between devices: 10.1 us -> 14.2 us  [per_device(): gathered = lax.all_to_all(packed, ('gy', 'gx'), 0, 0)]
    ppermute x2, waiting for transfers between devices: 2.85 us -> 0.01 us  [edges(): lax.ppermute(low_part, axis, backward)]
    pallas_call x1, Pallas kernels: 11.1 us -> 8.76 us  [per_device(): pl.pallas_call(functools.partial(cov_kernel, grid_y, grid_x, slides), out...]
    unnamed x33 -> x20, local copies, waits for them, and re-layouts: 8.45 us -> 7.22 us
  transfers between devices with their start and end apart: 6 -> 6, of which waited for: 4 -> 3; matrix products, arithmetic and copies ran while one was open for 1% -> 0% of each run, Pallas kernels for 2% -> 1%
where the time goes in v4:
time: 148 us; the launch traced here: 147 us
  blocking collectives  77.8 us (53%)
  starting transfers between devices  24.2 us (16%)
  waiting for transfers between devices  18.9 us (13%)
  Pallas kernels  15.7 us (11%)
  local copies, waits for them, and re-layouts  8.15 us (6%)
  between operations  2.09 us (1%)
    all_to_all x1, blocking collectives, per_device(): packed = lax.all_to_all(packed, ('gy', 'gx'), 0, 0)  38.6 us
    all_to_all x1, blocking collectives, per_device(): spread = lax.all_to_all(spread, ('gy', 'gx'), 0, 0)  21.1 us
    all_to_all x1, blocking collectives, per_device(): received = lax.all_to_all(sent, 'slide', 0, 0)  18.1 us
    all_to_all x1, waiting for transfers between devices, per_device(): gathered = lax.all_to_all(packed, ('gy', 'gx'), 0, 0)  14.2 us
    ppermute x2, starting transfers between devices, edges(): lax.ppermute(high_part, axis, forward)  9.44 us
    pallas_call x1, Pallas kernels, per_device(): pl.pallas_call(functools.partial(cov_kernel, grid_y, grid_x, slides), out...  8.76 us
    unnamed x20, local copies, waits for them, and re-layouts  7.22 us
    all_to_all x1, starting transfers between devices, per_device(): joined = lax.all_to_all(joined, 'slide', 0, 0)  6.26 us
  transfers between devices with their start and end apart: 6, of which 3 were waited for; matrix products, arithmetic and copies ran while one was open for 0% of the time, Pallas kernels for 1%

profile of v4, /device:TPU:1, one launch (start us, length us, event | category | flops | bytes accessed | tf_op | source)
XLA Modules:
  0.0 147.0 jit_solution(4608853031277752517)
XLA Ops:
  0.6 0.9 slice_bitcast_fusion
  1.6 1.3 collective-permute-start.1
  2.9 5.5 %collective-permute-start = (bf16[2,64,256]{2,1,0:T(8,128)(2,1)S(1)}, bf16[2,64,256]{2,1,0:T(8,128)(2,1)S(1)}, u32[]{:S(2)}, u32[]{:S(2)}) collective-permute-start(bf16[2,64,256]{2,1,0:T(8,128)(2,1)S(1)} %get-tuple-element.46), channel_id=1, source_target_pairs={{0,8},{8,16},{16,24},{24,32},{32,40},{40,48},{48,56},{56,64},{64,7... | collective-permute-start | bytes 196616 | tf_op jit(solution)/shard_map/ppermute | solution.py:403
  8.4 1.0 copy-done
  9.4 0.9 copy-done.2
  10.3 1.0 copy-done.4
  13.0 1.3 collective-permute-start.3
  14.3 4.0 %collective-permute-start.2 = (bf16[20,2,256]{2,1,0:T(2,128)(2,1)S(1)}, bf16[20,2,256]{2,1,0:T(2,128)(2,1)S(1)}, u32[]{:S(2)}, u32[]{:S(2)}) collective-permute-start(bf16[20,2,256]{2,1,0:T(2,128)(2,1)S(1)} %pad_maximum_fusion), channel_id=1, source_target_pairs={{0,1},{1,2},{2,3},{3,4},{4,5},{5,6},{6,7},{8,9},{9,10},{10,11},{11... | collective-permute-start | bytes 61448 | tf_op jit(solution)/shard_map/ppermute | solution.py:403
  19.2 2.2 %forward.1 = (bf16[1440,256]{1,0:T(8,128)(2,1)S(1)}, f32[96,4,128]{2,1,0:T(4,128)S(1)}, f32[20,80,256]{2,1,0:T(8,128)S(1)}) custom-call(s32[1]{0:T(128)} %bitcast.10.count, bf16[16,64,256]{2,1,0:T(8,128)(2,1)S(1)} %get-tuple-element.25.tile, bf16[2,64,256]{2,1,0:T(8,128)(2,1)S(1)} %collective-permute-done.up, ...), custom_call_target="tpu_custom_call" | custom-call | tf_op jit(solution)/shard_map/forward/pallas_call | solution.py:436
  21.4 0.9 copy-done.5
  22.3 38.6 %all_to_all.25.terms = f32[96,4,128]{2,1,0:T(4,128)S(1)} all-to-all(f32[96,4,128]{2,1,0:T(4,128)S(1)} %get-tuple-element.32), channel_id=1, replica_groups=mesh['slide'=8,'gy'=12,'gx'=8] {'gy','gx'}, dimensions={0} | all-to-all | bytes 393216 | tf_op jit(solution)/shard_map/all_to_all | solution.py:454
  60.8 0.8 plane_sum.1
  61.6 5.9 %all-to-all-start.1 = ((f32[96,4,128]{2,1,0:T(4,128)}), f32[96,4,128]{2,1,0:T(4,128)S(1)}, u32[]{:S(2)}, u32[]{:S(2)}) async-start(f32[96,4,128]{2,1,0:T(4,128)} %plane_sum.1), calls=%async_computation.1 | async-start | bytes 393216 | tf_op jit(solution)/shard_map/all_to_all | solution.py:464
  68.2 14.2 %all-to-all-done.1.gathered = f32[96,4,128]{2,1,0:T(4,128)S(1)} async-done(((f32[96,4,128]{2,1,0:T(4,128)}), f32[96,4,128]{2,1,0:T(4,128)S(1)}, u32[]{:S(2)}, u32[]{:S(2)}) %all-to-all-start.1) | async-done | bytes 196640 | tf_op jit(solution)/shard_map/all_to_all | solution.py:464
  82.4 1.1 copy-done.6
  83.6 0.9 copy-done.8
  84.5 8.8 %covariance.1 = (bf16[1440,256]{1,0:T(8,128)(2,1)S(1)}, f32[8,56,256]{2,1,0:T(8,128)S(1)}) custom-call(s32[2]{0:T(128)S(1)} %pad_add_fusion.place, s32[1]{0:T(128)S(6)} %copy.12.label, f32[96,4,128]{2,1,0:T(4,128)S(1)} %all-to-all-done.1.gathered, f32[20,80,256]{2,1,0:T(8,128)S(1)} %get-tuple-element.33.ext, bf16[1440,256]{1,0:T(8,128)(2,1)S(1)} %copy-done.6, ...), custom_call_target="tpu_custom_call" | custom-call | tf_op jit(solution)/shard_map/covariance/pallas_call | solution.py:468
  93.2 18.1 %all_to_all.26.terms = f32[8,56,256]{2,1,0:T(8,128)S(1)} all-to-all(f32[8,56,256]{2,1,0:T(8,128)S(1)} %get-tuple-element.37), channel_id=1, replica_groups=mesh['slide'=8,'gy'=12,'gx'=8] {'slide'}, dimensions={0} | all-to-all | bytes 917504 | tf_op jit(solution)/shard_map/all_to_all | solution.py:481
  111.4 21.1 %all_to_all.27.spread = f32[96,4,128]{2,1,0:T(4,128)S(1)} all-to-all(f32[96,4,128]{2,1,0:T(4,128)S(1)} %get-tuple-element.39), channel_id=1, replica_groups=mesh['slide'=8,'gy'=12,'gx'=8] {'gy','gx'}, dimensions={0} | all-to-all | bytes 393216 | tf_op jit(solution)/shard_map/all_to_all | solution.py:504
  132.5 0.8 join.1
  133.3 6.3 %all-to-all-start.4 = ((bf16[8,64,256]{2,1,0:T(8,128)(2,1)}), bf16[8,64,256]{2,1,0:T(8,128)(2,1)S(1)}, u32[]{:S(2)}, u32[]{:S(2)}) async-start(bf16[8,64,256]{2,1,0:T(8,128)(2,1)} %join.1), calls=%async_computation.4 | async-start | bytes 524288 | tf_op jit(solution)/shard_map/all_to_all | solution.py:513
  139.6 2.0 %spread.1 = bf16[16,64,256]{2,1,0:T(8,128)(2,1)} custom-call(bf16[1440,256]{1,0:T(8,128)(2,1)S(1)} %get-tuple-element.44.back, f32[9,256]{1,0:T(8,128)S(1)} %get-tuple-element.28.weights), custom_call_target="tpu_custom_call" | custom-call | flops 7372800 | bytes 4194304 | tf_op jit(solution)/shard_map/spread/pallas_call | solution.py:482
  141.5 4.6 %all-to-all-done.4.terms = bf16[8,64,256]{2,1,0:T(8,128)(2,1)S(1)} async-done(((bf16[8,64,256]{2,1,0:T(8,128)(2,1)}), bf16[8,64,256]{2,1,0:T(8,128)(2,1)S(1)}, u32[]{:S(2)}, u32[]{:S(2)}) %all-to-all-start.4) | async-done | bytes 262176 | tf_op jit(solution)/shard_map/all_to_all | solution.py:513
  146.1 0.9 finish.1
  (25 shorter events, 1.9 us)
Async XLA Ops:
  0.6 18.6 %copy-start.3 = (bf16[256,256]{1,0:T(8,128)(2,1)S(1)}, bf16[256,256]{1,0:T(8,128)(2,1)}, u32[]{:S(2)}) copy-start(bf16[256,256]{1,0:T(8,128)(2,1)} %point.5) | copy-start | bytes 393220
  1.6 11.3 %collective-permute-start.1 = (bf16[2,64,256]{2,1,0:T(8,128)(2,1)S(1)}, bf16[2,64,256]{2,1,0:T(8,128)(2,1)S(1)}, u32[]{:S(2)}, u32[]{:S(2)}) collective-permute-start(bf16[2,64,256]{2,1,0:T(8,128)(2,1)S(1)} %get-tuple-element.45), channel_id=1, source_target_pairs={{8,0},{16,8},{24,16},{32,24},{40,32},{48,40},{56,48},{64,56},{72,6... | collective-permute-start | bytes 196616 | tf_op jit(solution)/shard_map/ppermute | solution.py:403
  2.9 10.0 %collective-permute-start = (bf16[2,64,256]{2,1,0:T(8,128)(2,1)S(1)}, bf16[2,64,256]{2,1,0:T(8,128)(2,1)S(1)}, u32[]{:S(2)}, u32[]{:S(2)}) collective-permute-start(bf16[2,64,256]{2,1,0:T(8,128)(2,1)S(1)} %get-tuple-element.46), channel_id=1, source_target_pairs={{0,8},{8,16},{16,24},{24,32},{32,40},{40,48},{48,56},{56,64},{64,7... | collective-permute-start | bytes 196616 | tf_op jit(solution)/shard_map/ppermute | solution.py:403
  8.3 1.0 copy-start
  9.4 0.9 copy-start.2
  10.3 1.0 copy-start.4
  11.3 0.7 copy-start.9
  12.0 70.4 %copy-start.1 = (f32[2,256,256]{2,1,0:T(8,128)S(1)}, f32[2,256,256]{2,1,0:T(8,128)}, u32[]{:S(2)}) copy-start(f32[2,256,256]{2,1,0:T(8,128)} %classifier.3) | copy-start | bytes 1572868
  12.2 0.7 copy-start.7
  13.0 6.1 %collective-permute-start.3 = (bf16[20,2,256]{2,1,0:T(2,128)(2,1)S(1)}, bf16[20,2,256]{2,1,0:T(2,128)(2,1)S(1)}, u32[]{:S(2)}, u32[]{:S(2)}) collective-permute-start(bf16[20,2,256]{2,1,0:T(2,128)(2,1)S(1)} %pad_maximum_fusion.1), channel_id=1, source_target_pairs={{1,0},{2,1},{3,2},{4,3},{5,4},{6,5},{7,6},{9,8},{10,9},{11,10},{12... | collective-permute-start | bytes 61448 | tf_op jit(solution)/shard_map/ppermute | solution.py:403
  14.3 4.9 %collective-permute-start.2 = (bf16[20,2,256]{2,1,0:T(2,128)(2,1)S(1)}, bf16[20,2,256]{2,1,0:T(2,128)(2,1)S(1)}, u32[]{:S(2)}, u32[]{:S(2)}) collective-permute-start(bf16[20,2,256]{2,1,0:T(2,128)(2,1)S(1)} %pad_maximum_fusion), channel_id=1, source_target_pairs={{0,1},{1,2},{2,3},{3,4},{4,5},{5,6},{6,7},{8,9},{9,10},{10,11},{11... | collective-permute-start | bytes 61448 | tf_op jit(solution)/shard_map/ppermute | solution.py:403
  21.4 0.9 copy-start.5
  61.6 20.8 %all-to-all-start.1 = ((f32[96,4,128]{2,1,0:T(4,128)}), f32[96,4,128]{2,1,0:T(4,128)S(1)}, u32[]{:S(2)}, u32[]{:S(2)}) async-start(f32[96,4,128]{2,1,0:T(4,128)} %plane_sum.1), calls=%async_computation.1 | async-start | bytes 393216 | tf_op jit(solution)/shard_map/all_to_all | solution.py:464
  82.4 1.1 copy-start.6
  83.6 0.9 copy-start.8
  133.3 12.8 %all-to-all-start.4 = ((bf16[8,64,256]{2,1,0:T(8,128)(2,1)}), bf16[8,64,256]{2,1,0:T(8,128)(2,1)S(1)}, u32[]{:S(2)}, u32[]{:S(2)}) async-start(bf16[8,64,256]{2,1,0:T(8,128)(2,1)} %join.1), calls=%async_computation.4 | async-start | bytes 524288 | tf_op jit(solution)/shard_map/all_to_all | solution.py:513

commit v5 on v4

--- a/solution.py
+++ b/solution.py
@@ -14,6 +14,7 @@
 F32 = jnp.float32
 BF16 = jnp.bfloat16
 VMEM = pl.BlockSpec(memory_space=pltpu.VMEM)
+HBM = pl.BlockSpec(memory_space=pltpu.HBM)
 SMEM = pl.BlockSpec(memory_space=pltpu.SMEM)
 PARAMS = pltpu.CompilerParams(vmem_limit_bytes=16 * 1024 * 1024)
 SMALL = pltpu.CompilerParams(vmem_limit_bytes=4 * 1024 * 1024)
@@ -87,26 +88,35 @@
     ext[:, LEFT + width : LEFT + width + RIM, :] = right[...].astype(F32)
 
 
-def load_kernel(
-    tile, weights, point, classifier, tile_out, low, high, taps, turned, toward
-):
+def load_kernel(scalars, tile_in, tile, low, high, info):
     width = tile.shape[1]
-    tile_out[...] = tile[...]
-    low[...] = tile[:, :RIM, :]
-    high[...] = tile[:, width - RIM :, :]
+    tile[...] = tile_in[...]
+    low[...] = tile_in[:, :RIM, :]
+    high[...] = tile_in[:, width - RIM :, :]
+    row = iota(info.shape, 0)
+    value = jnp.zeros(info.shape, F32)
+    for k in range(4):
+        value = jnp.where(row == k, scalars[k].astype(F32), value)
+    info[...] = value
+
+
+def weights_kernel(edge, weights, point, classifier, taps, mixing, turned, classes, toward):
     taps[...] = jnp.concatenate([weights[a].astype(F32) for a in range(3)], axis=0)
+    mixing[...] = point[...]
     turned[...] = point[...].astype(F32).T.astype(BF16)
+    classes[...] = classifier[...]
     gap = classifier[0] - classifier[1]
     toward[...] = gap + gap.T
 
 
 def forward_kernel(
-    planes, count, tile, up, down, left, right, weights, point, mapped, packed, ext, hidden, inner
+    planes, info, tile, up, down, left, right, weights, point, mapped, packed, ext, hidden, inner
 ):
     height, width, channels = tile.shape
     wide = ext.shape[1]
     assemble(ext, tile, up, down, left, right)
-    valid = count[0]
+    valid = jnp.broadcast_to(info[0:1, :].astype(jnp.int32), (width, LANES))
+    order = iota((width, LANES), 0)
 
     for lane in range(0, channels, LANES):
         part = slice(lane, lane + LANES)
@@ -120,8 +130,7 @@
 
             @pl.when((r >= 1) & (r <= height))
             def _():
-                raster = (r - 1) * width + iota((width, LANES), 0)
-                kept = jnp.where(raster < valid, value[LEFT : LEFT + width], 0.0)
+                kept = jnp.where(order < valid - (r - 1) * width, value[LEFT : LEFT + width], 0.0)
                 start = pl.multiple_of((r - 1) * width, 16)
                 inner[pl.ds(start, width), part] = kept.astype(BF16)
 
@@ -145,16 +154,15 @@
     packed[:, chunks, :] = jnp.zeros((planes, LANES), F32)
 
 
-def plane_sum_kernel(count, terms, out):
+def plane_sum_kernel(info, terms, out):
     planes, rows, lanes = terms.shape
     summed = jnp.sum(terms[...], axis=0)
-    valid = jnp.full((rows, lanes), count[0].astype(F32))
-    summed = jnp.where(iota((rows, lanes), 0) == rows - 1, valid, summed)
+    summed = jnp.where(iota((rows, lanes), 0) == rows - 1, info[0:1, 0:1], summed)
     out[...] = jnp.broadcast_to(summed[None], out.shape)
 
 
 def cov_kernel(
-    grid_y, grid_x, slides, place, label, gathered, ext, mapped, toward_ref, point, point_turned,
+    grid_y, grid_x, slides, info, gathered, ext, mapped, toward_ref, point, point_turned,
     classifier, back_out, sent, back, sem,
 ):
     planes = grid_y * grid_x
@@ -222,7 +230,7 @@
     logit1 = total(classifier[1] * pooled)
     peak = jnp.maximum(logit0, logit1)
     lse = peak + jnp.log(jnp.exp(logit0 - peak) + jnp.exp(logit1 - peak))
-    is_zero = label[0] == 0
+    is_zero = info[1:2, 0:1] == 0.0
     slope = jnp.where(is_zero, -jnp.exp(logit1 - lse), jnp.exp(logit0 - lse)) * (1.0 / slides)
     loss = (lse - jnp.where(is_zero, logit0, logit1)) * (1.0 / slides)
 
@@ -241,13 +249,13 @@
     )
     offset = -mm(split(mean), sym_pair)[0:1]
 
-    row_id = iota((planes, LANES), 0)
+    row_id = iota((planes, LANES), 0).astype(F32)
     spots = []
     for dy_ in (-1, 0, 1):
         for dx_ in (-1, 0, 1):
-            near_y, near_x = place[0] + dy_, place[1] + dx_
+            near_y, near_x = info[2:3, 0:1] + dy_, info[3:4, 0:1] + dx_
             inside = (near_y >= 0) & (near_y < grid_y) & (near_x >= 0) & (near_x < grid_x)
-            spot = jnp.where(inside, near_y * grid_x + near_x, -1)
+            spot = jnp.where(inside, near_y * grid_x + near_x, -1.0)
             near = jnp.sum(jnp.where(row_id == spot, counts, 0.0), axis=0, keepdims=True)
             spots.append(near[:, 0:1])
 
@@ -403,31 +411,50 @@
         return lax.ppermute(high_part, axis, forward), lax.ppermute(low_part, axis, backward)
 
     up, down = edges(tile[:RIM], tile[height - RIM :], "gy")
-
-    tile, low, high, weights, point_turned, toward = pl.pallas_call(
+    strip_shape = jax.ShapeDtypeStruct((height, RIM, channels), BF16)
+    scalars = jnp.stack(
+        [
+            valid_count[0, 0, 0],
+            labels[0],
+            lax.axis_index("gy").astype(jnp.int32),
+            lax.axis_index("gx").astype(jnp.int32),
+        ]
+    )
+    tile, low, high, info = pl.pallas_call(
         load_kernel,
         out_shape=(
             jax.ShapeDtypeStruct(tile.shape, BF16),
-            jax.ShapeDtypeStruct((height, RIM, channels), BF16),
-            jax.ShapeDtypeStruct((height, RIM, channels), BF16),
-            jax.ShapeDtypeStruct((9, channels), F32),
-            jax.ShapeDtypeStruct((channels, channels), BF16),
-            jax.ShapeDtypeStruct((channels, channels), F32),
-        ),
-        in_specs=[VMEM] * 4,
-        out_specs=(VMEM,) * 6,
+            strip_shape,
+            strip_shape,
+            jax.ShapeDtypeStruct((8, LANES), F32),
+        ),
+        in_specs=[SMEM, VMEM],
+        out_specs=(VMEM,) * 4,
         compiler_params=SMALL,
         name="load",
-    )(tile, depth_weight, point_weight, classifier)
-
+    )(scalars, tile)
     def strip(own, start):
         ends = [part[:, start : start + RIM] for part in (up, down)]
         return jnp.concatenate([ends[0], own, ends[1]], axis=0)
 
-    left, right = edges(strip(low, 0), strip(high, width - RIM), "gx")
-
-    count = valid_count.reshape(1)
-    place = jnp.stack([lax.axis_index("gy"), lax.axis_index("gx")]).astype(jnp.int32)
+    low_strip, high_strip = strip(low, 0), strip(high, width - RIM)
+    left, right = edges(low_strip, high_strip, "gx")
+    square = (channels, channels)
+    weights, point, point_turned, classes, toward = pl.pallas_call(
+        weights_kernel,
+        out_shape=(
+            jax.ShapeDtypeStruct((9, channels), F32),
+            jax.ShapeDtypeStruct(square, BF16),
+            jax.ShapeDtypeStruct(square, BF16),
+            jax.ShapeDtypeStruct(classifier.shape, F32),
+            jax.ShapeDtypeStruct(square, F32),
+        ),
+        in_specs=[VMEM] * 4,
+        out_specs=(VMEM,) * 5,
+        compiler_params=SMALL,
+        name="weights",
+    )(low_strip, depth_weight, point_weight, classifier)
+
     halo = (tile, up, down, left, right)
     chunks = -(-(channels + 3) // planes)
     pixels = (height + 2) * wide
@@ -440,27 +467,26 @@
             jax.ShapeDtypeStruct((planes, chunks + 1, LANES), F32),
             jax.ShapeDtypeStruct(ext_shape, F32),
         ),
-        in_specs=[SMEM] + [VMEM] * 7,
-        out_specs=(VMEM, VMEM, VMEM),
+        in_specs=[VMEM] * 8,
+        out_specs=(VMEM,) * 3,
         scratch_shapes=[
             pltpu.VMEM((pixels, channels), BF16),
             pltpu.VMEM((height * width, channels), BF16),
         ],
         compiler_params=PARAMS,
         name="forward",
-    )(count, *halo, weights, point_weight)
-    packed, place, labels = lax.optimization_barrier((packed, place, labels))
+    )(info, *halo, weights, point)
 
     packed = lax.all_to_all(packed, ("gy", "gx"), 0, 0)
 
     packed = pl.pallas_call(
         plane_sum_kernel,
         out_shape=jax.ShapeDtypeStruct((planes, chunks + 1, LANES), F32),
-        in_specs=[SMEM, VMEM],
+        in_specs=[VMEM, VMEM],
         out_specs=VMEM,
         compiler_params=SMALL,
         name="plane_sum",
-    )(count, packed)
+    )(info, packed)
     gathered = lax.all_to_all(packed, ("gy", "gx"), 0, 0)
 
     rp, rd = channels // slides, 16 // slides
@@ -471,12 +497,12 @@
             jax.ShapeDtypeStruct((pixels, channels), BF16),
             jax.ShapeDtypeStruct((slides, main + 8, channels), F32),
         ),
-        in_specs=[SMEM, SMEM] + [VMEM] * 7,
-        out_specs=(pl.BlockSpec(memory_space=pltpu.HBM), VMEM),
+        in_specs=[VMEM] * 8,
+        out_specs=(HBM, VMEM),
         scratch_shapes=[pltpu.VMEM((pixels, channels), BF16), pltpu.SemaphoreType.DMA],
         compiler_params=PARAMS,
         name="covariance",
-    )(place, labels, gathered, ext, mapped, toward, point_weight, point_turned, classifier)
+    )(info, gathered, ext, mapped, toward, point, point_turned, classes)
 
     received = lax.all_to_all(sent, "slide", 0, 0)
     gradient = pl.pallas_call(
@@ -511,7 +537,7 @@
         name="join",
     )(shares, spread)
     joined = lax.all_to_all(joined, "slide", 0, 0)
-    loss, depth, point, classes = pl.pallas_call(
+    loss, depth, point_total, class_total = pl.pallas_call(
         finish_kernel,
         out_shape=(
             jax.ShapeDtypeStruct((1, 1), F32),
@@ -524,7 +550,7 @@
         compiler_params=SMALL,
         name="finish",
     )(joined)
-    return loss.reshape(()), depth, point, classes, gradient[None]
+    return loss.reshape(()), depth, point_total, class_total, gradient[None]
 
 
 def solution(mesh):

time: 148 us -> 143 us (0.966)
  blocking collectives: 77.8 us -> 97.6 us
  waiting for transfers between devices: 18.9 us -> 4.98 us
  starting transfers between devices: 24.2 us -> 17.5 us
  local copies, waits for them, and re-layouts: 8.15 us -> 4.57 us
    all_to_all x0 -> x1, blocking collectives: none -> 20.5 us  [per_device(): gathered = lax.all_to_all(packed, ('gy', 'gx'), 0, 0)]
    all_to_all x1 -> x0, waiting for transfers between devices: 14.2 us -> none  [per_device(): gathered = lax.all_to_all(packed, ('gy', 'gx'), 0, 0)]
    all_to_all x1 -> x0, starting transfers between devices: 5.94 us -> none  [per_device(): gathered = lax.all_to_all(packed, ('gy', 'gx'), 0, 0)]
    unnamed x20 -> x8, local copies, waits for them, and re-layouts: 7.22 us -> 3.67 us
  transfers between devices with their start and end apart: 6 -> 5, of which waited for: 3 -> 2; matrix products, arithmetic and copies ran while one was open for 0% -> 0% of each run, Pallas kernels for 1% -> 2%
where the time goes in v5:
time: 143 us; the launch traced here: 142 us
  blocking collectives  97.6 us (68%)
  starting transfers between devices  17.5 us (12%)
  Pallas kernels  15.1 us (11%)
  waiting for transfers between devices  4.98 us (3%)
  local copies, waits for them, and re-layouts  4.57 us (3%)
  between operations  2.07 us (1%)
    all_to_all x1, blocking collectives, per_device(): packed = lax.all_to_all(packed, ('gy', 'gx'), 0, 0)  38.6 us
    all_to_all x1, blocking collectives, per_device(): spread = lax.all_to_all(spread, ('gy', 'gx'), 0, 0)  21.1 us
    all_to_all x1, blocking collectives, per_device(): gathered = lax.all_to_all(packed, ('gy', 'gx'), 0, 0)  20.5 us
    all_to_all x1, blocking collectives, per_device(): received = lax.all_to_all(sent, 'slide', 0, 0)  17.4 us
    ppermute x2, starting transfers between devices, edges(): lax.ppermute(high_part, axis, forward)  8.66 us
    pallas_call x1, Pallas kernels, per_device(): pl.pallas_call(functools.partial(cov_kernel, grid_y, grid_x, slides), out...  8.28 us
    all_to_all x1, starting transfers between devices, per_device(): joined = lax.all_to_all(joined, 'slide', 0, 0)  6.26 us
    all_to_all x1, waiting for transfers between devices, per_device(): joined = lax.all_to_all(joined, 'slide', 0, 0)  4.57 us
  transfers between devices with their start and end apart: 5, of which 2 were waited for; matrix products, arithmetic and copies ran while one was open for 0% of the time, Pallas kernels for 2%

profile of v5, /device:TPU:1, one launch (start us, length us, event | category | flops | bytes accessed | tf_op | source)
XLA Modules:
  0.0 142.0 jit_solution(16835750165308645374)
XLA Ops:
  0.6 0.9 slice_bitcast_fusion
  1.5 1.3 collective-permute-start.1
  2.8 5.5 %collective-permute-start = (bf16[2,64,256]{2,1,0:T(8,128)(2,1)S(1)}, bf16[2,64,256]{2,1,0:T(8,128)(2,1)S(1)}, u32[]{:S(2)}, u32[]{:S(2)}) collective-permute-start(bf16[2,64,256]{2,1,0:T(8,128)(2,1)S(1)} %get-tuple-element.46), channel_id=1, source_target_pairs={{0,8},{8,16},{16,24},{24,32},{32,40},{40,48},{48,56},{56,64},{64,7... | collective-permute-start | bytes 196616 | tf_op jit(solution)/shard_map/ppermute | solution.py:411
  9.7 1.0 copy-done
  10.7 0.6 load.1
  11.4 3.2 %collective-permute-start.2 = (bf16[20,2,256]{2,1,0:T(2,128)(2,1)S(1)}, bf16[20,2,256]{2,1,0:T(2,128)(2,1)S(1)}, u32[]{:S(2)}, u32[]{:S(2)}) collective-permute-start(bf16[20,2,256]{2,1,0:T(2,128)(2,1)S(1)} %pad_maximum_fusion), channel_id=1, source_target_pairs={{0,1},{1,2},{2,3},{3,4},{4,5},{5,6},{6,7},{8,9},{9,10},{10,11},{11... | collective-permute-start | bytes 61448 | tf_op jit(solution)/shard_map/ppermute | solution.py:411
  14.7 1.3 collective-permute-start.3
  16.0 1.0 copy-done.1
  17.0 0.9 copy-done.2
  17.9 0.7 copy-done.3
  18.6 0.2 weights.2
  18.8 0.4 collective-permute-done.3.right
  19.2 2.2 %forward.1 = (bf16[1440,256]{1,0:T(8,128)(2,1)S(1)}, f32[96,4,128]{2,1,0:T(4,128)S(1)}, f32[20,80,256]{2,1,0:T(8,128)S(1)}) custom-call(f32[8,128]{1,0:T(8,128)S(1)} %get-tuple-element.25.info, bf16[16,64,256]{2,1,0:T(8,128)(2,1)S(1)} %get-tuple-element.26.tile, bf16[2,64,256]{2,1,0:T(8,128)(2,1)S(1)} %collective-permute-done.up, ...), custom_call_target="tpu_custom_call" | custom-call | tf_op jit(solution)/shard_map/forward/pallas_call | solution.py:463
  21.4 38.6 %all_to_all.25.terms = f32[96,4,128]{2,1,0:T(4,128)S(1)} all-to-all(f32[96,4,128]{2,1,0:T(4,128)S(1)} %get-tuple-element.31), channel_id=1, replica_groups=mesh['slide'=8,'gy'=12,'gx'=8] {'gy','gx'}, dimensions={0} | all-to-all | bytes 393216 | tf_op jit(solution)/shard_map/all_to_all | solution.py:480
  60.0 0.1 plane_sum.1
  60.1 20.5 %all_to_all.26.gathered = f32[96,4,128]{2,1,0:T(4,128)S(1)} all-to-all(f32[96,4,128]{2,1,0:T(4,128)S(1)} %plane_sum.1), channel_id=1, replica_groups=mesh['slide'=8,'gy'=12,'gx'=8] {'gy','gx'}, dimensions={0} | all-to-all | bytes 393216 | tf_op jit(solution)/shard_map/all_to_all | solution.py:490
  80.6 8.3 %covariance.1 = (bf16[1440,256]{1,0:T(8,128)(2,1)S(1)}, f32[8,56,256]{2,1,0:T(8,128)S(1)}) custom-call(f32[8,128]{1,0:T(8,128)S(1)} %get-tuple-element.25.info, f32[96,4,128]{2,1,0:T(4,128)S(1)} %all_to_all.26.gathered, f32[20,80,256]{2,1,0:T(8,128)S(1)} %get-tuple-element.32.ext, bf16[1440,256]{1,0:T(8,128)(2,1)S(1)} %get-tuple-element.33.mapped, ...), custom_call_target="tpu_custom_call" | custom-call | tf_op jit(solution)/shard_map/covariance/pallas_call | solution.py:494
  88.9 17.4 %all_to_all.27.terms = f32[8,56,256]{2,1,0:T(8,128)S(1)} all-to-all(f32[8,56,256]{2,1,0:T(8,128)S(1)} %get-tuple-element.37), channel_id=1, replica_groups=mesh['slide'=8,'gy'=12,'gx'=8] {'slide'}, dimensions={0} | all-to-all | bytes 917504 | tf_op jit(solution)/shard_map/all_to_all | solution.py:507
  106.4 21.1 %all_to_all.28.spread = f32[96,4,128]{2,1,0:T(4,128)S(1)} all-to-all(f32[96,4,128]{2,1,0:T(4,128)S(1)} %get-tuple-element.39), channel_id=1, replica_groups=mesh['slide'=8,'gy'=12,'gx'=8] {'gy','gx'}, dimensions={0} | all-to-all | bytes 393216 | tf_op jit(solution)/shard_map/all_to_all | solution.py:530
  127.5 0.8 join.1
  128.3 6.3 %all-to-all-start.4 = ((bf16[8,64,256]{2,1,0:T(8,128)(2,1)}), bf16[8,64,256]{2,1,0:T(8,128)(2,1)S(1)}, u32[]{:S(2)}, u32[]{:S(2)}) async-start(bf16[8,64,256]{2,1,0:T(8,128)(2,1)} %join.1), calls=%async_computation.4 | async-start | bytes 524288 | tf_op jit(solution)/shard_map/all_to_all | solution.py:539
  134.6 2.0 %spread.1 = bf16[16,64,256]{2,1,0:T(8,128)(2,1)} custom-call(bf16[1440,256]{1,0:T(8,128)(2,1)S(1)} %get-tuple-element.44.back, f32[9,256]{1,0:T(8,128)S(1)} %get-tuple-element.29.weights), custom_call_target="tpu_custom_call" | custom-call | flops 7372800 | bytes 4194304 | tf_op jit(solution)/shard_map/spread/pallas_call | solution.py:508
  136.5 4.6 %all-to-all-done.4.terms = bf16[8,64,256]{2,1,0:T(8,128)(2,1)S(1)} async-done(((bf16[8,64,256]{2,1,0:T(8,128)(2,1)}), bf16[8,64,256]{2,1,0:T(8,128)(2,1)S(1)}, u32[]{:S(2)}, u32[]{:S(2)}) %all-to-all-start.4) | async-done | bytes 262176 | tf_op jit(solution)/shard_map/all_to_all | solution.py:539
  141.1 0.9 finish.1
  (13 shorter events, 0.2 us)
Async XLA Ops:
  1.5 9.8 %collective-permute-start.1 = (bf16[2,64,256]{2,1,0:T(8,128)(2,1)S(1)}, bf16[2,64,256]{2,1,0:T(8,128)(2,1)S(1)}, u32[]{:S(2)}, u32[]{:S(2)}) collective-permute-start(bf16[2,64,256]{2,1,0:T(8,128)(2,1)S(1)} %get-tuple-element.45), channel_id=1, source_target_pairs={{8,0},{16,8},{24,16},{32,24},{40,32},{48,40},{56,48},{64,56},{72,6... | collective-permute-start | bytes 196616 | tf_op jit(solution)/shard_map/ppermute | solution.py:411
  2.8 8.5 %collective-permute-start = (bf16[2,64,256]{2,1,0:T(8,128)(2,1)S(1)}, bf16[2,64,256]{2,1,0:T(8,128)(2,1)S(1)}, u32[]{:S(2)}, u32[]{:S(2)}) collective-permute-start(bf16[2,64,256]{2,1,0:T(8,128)(2,1)S(1)} %get-tuple-element.46), channel_id=1, source_target_pairs={{0,8},{8,16},{16,24},{24,32},{32,40},{40,48},{48,56},{56,64},{64,7... | collective-permute-start | bytes 196616 | tf_op jit(solution)/shard_map/ppermute | solution.py:411
  9.7 1.0 copy-start
  11.4 7.4 %collective-permute-start.2 = (bf16[20,2,256]{2,1,0:T(2,128)(2,1)S(1)}, bf16[20,2,256]{2,1,0:T(2,128)(2,1)S(1)}, u32[]{:S(2)}, u32[]{:S(2)}) collective-permute-start(bf16[20,2,256]{2,1,0:T(2,128)(2,1)S(1)} %pad_maximum_fusion), channel_id=1, source_target_pairs={{0,1},{1,2},{2,3},{3,4},{4,5},{5,6},{6,7},{8,9},{9,10},{10,11},{11... | collective-permute-start | bytes 61448 | tf_op jit(solution)/shard_map/ppermute | solution.py:411
  14.7 4.5 %collective-permute-start.3 = (bf16[20,2,256]{2,1,0:T(2,128)(2,1)S(1)}, bf16[20,2,256]{2,1,0:T(2,128)(2,1)S(1)}, u32[]{:S(2)}, u32[]{:S(2)}) collective-permute-start(bf16[20,2,256]{2,1,0:T(2,128)(2,1)S(1)} %pad_maximum_fusion.1.edge), channel_id=1, source_target_pairs={{1,0},{2,1},{3,2},{4,3},{5,4},{6,5},{7,6},{9,8},{10,9},{11,10},{12... | collective-permute-start | bytes 61448 | tf_op jit(solution)/shard_map/ppermute | solution.py:411
  16.0 1.0 copy-start.1
  17.0 0.9 copy-start.2
  17.9 0.7 copy-start.3
  128.3 12.8 %all-to-all-start.4 = ((bf16[8,64,256]{2,1,0:T(8,128)(2,1)}), bf16[8,64,256]{2,1,0:T(8,128)(2,1)S(1)}, u32[]{:S(2)}, u32[]{:S(2)}) async-start(bf16[8,64,256]{2,1,0:T(8,128)(2,1)} %join.1), calls=%async_computation.4 | async-start | bytes 524288 | tf_op jit(solution)/shard_map/all_to_all | solution.py:539

commit v6 on v5

--- a/solution.py
+++ b/solution.py
@@ -88,19 +88,28 @@
     ext[:, LEFT + width : LEFT + width + RIM, :] = right[...].astype(F32)
 
 
-def load_kernel(scalars, tile_in, tile, low, high, info):
-    width = tile.shape[1]
+def load_kernel(count, label, tile_in, tile, bottom, low, high, info):
+    height, width, _ = tile.shape
     tile[...] = tile_in[...]
+    bottom[...] = tile_in[height - RIM :]
     low[...] = tile_in[:, :RIM, :]
     high[...] = tile_in[:, width - RIM :, :]
     row = iota(info.shape, 0)
     value = jnp.zeros(info.shape, F32)
-    for k in range(4):
-        value = jnp.where(row == k, scalars[k].astype(F32), value)
+    for k, scalar in enumerate(
+        (count[0], label[0], lax.axis_index("gy"), lax.axis_index("gx"), lax.axis_index("slide"))
+    ):
+        value = jnp.where(row == k, scalar.astype(jnp.int32).astype(F32), value)
     info[...] = value
 
 
-def weights_kernel(edge, weights, point, classifier, taps, mixing, turned, classes, toward):
+def weights_kernel(
+    up, own, down, weights, point, classifier, strip, taps, mixing, turned, classes, toward
+):
+    height, width = own.shape[0], up.shape[1]
+    strip[0:RIM] = up[:, width - RIM :, :]
+    strip[RIM : RIM + height] = own[...]
+    strip[RIM + height :] = down[:, width - RIM :, :]
     taps[...] = jnp.concatenate([weights[a].astype(F32) for a in range(3)], axis=0)
     mixing[...] = point[...]
     turned[...] = point[...].astype(F32).T.astype(BF16)
@@ -308,8 +317,7 @@
 
     upper, tri, diag = tri_pack(class_term)
     class_flat = jnp.concatenate([upper, tri], axis=0)
-    scale = 1.0 / planes
-    extra = jnp.concatenate([diag, jnp.broadcast_to(loss, (1, half))], axis=1) * scale
+    extra = jnp.concatenate([diag, jnp.broadcast_to(loss, (1, half))], axis=1)
     small = jnp.concatenate([depth, extra, jnp.zeros((6, channels), F32)], axis=0)
     rp, rc, rd = channels // slides, channels // slides // 2, 16 // slides
     pad = [jnp.zeros((8 - rd, channels), F32)] if rd < 8 else []
@@ -343,26 +351,26 @@
         lax.fori_loop(0, height, body, 0)
 
 
-def slide_sum_kernel(rd, terms, shares, spread):
+def slide_sum_kernel(rd, terms, shares, small, spread):
     slides, rows, channels = terms.shape
     main = rows - 8
     summed = terms[0]
     for k in range(1, slides):
         summed = summed + terms[k]
     shares[...] = summed[:main].astype(BF16)
-    tail = summed[main : main + rd]
+    tail = summed[main:]
+    small[...] = tail
     lines = jnp.concatenate(
         [tail[q : q + 1, p : p + LANES] for q in range(rd) for p in range(0, channels, LANES)],
         axis=0,
     )
-    spread[...] = jnp.broadcast_to(lines[None], spread.shape)
-
-
-def join_kernel(shares, spread, out):
+    spread[...] = jnp.broadcast_to(lines.astype(BF16)[None], spread.shape)
+
+
+def join_kernel(rd, info, shares, small, spread, out):
     slides, rows, channels = out.shape
-    summed = jnp.sum(spread[...], axis=0)
+    summed = jnp.sum(spread[...].astype(F32), axis=0)
     per = channels // LANES
-    rd = summed.shape[0] // per
     tail = jnp.concatenate(
         [
             jnp.concatenate([summed[per * q + p : per * q + p + 1] for p in range(per)], axis=1)
@@ -370,6 +378,8 @@
         ],
         axis=0,
     )
+    line = info[4:5, 0:1] * rd + iota((rd, channels), 0).astype(F32)
+    tail = jnp.where(line < 9, tail, small[:rd])
     high, low = split(tail)
     tail = jnp.concatenate([high, low, jnp.zeros((16 - 2 * rd, channels), BF16)], axis=0)
     for k in range(slides):
@@ -405,55 +415,52 @@
     height, width, channels = tile.shape
     wide = width + 2 * LEFT
 
-    def edges(low_part, high_part, axis):
-        forward = [(i, i + 1) for i in range(lax.axis_size(axis) - 1)]
-        backward = [(target, source) for source, target in forward]
-        return lax.ppermute(high_part, axis, forward), lax.ppermute(low_part, axis, backward)
-
-    up, down = edges(tile[:RIM], tile[height - RIM :], "gy")
-    strip_shape = jax.ShapeDtypeStruct((height, RIM, channels), BF16)
-    scalars = jnp.stack(
-        [
-            valid_count[0, 0, 0],
-            labels[0],
-            lax.axis_index("gy").astype(jnp.int32),
-            lax.axis_index("gx").astype(jnp.int32),
-        ]
-    )
-    tile, low, high, info = pl.pallas_call(
+    def upward(part, axis):
+        pairs = [(i, i + 1) for i in range(lax.axis_size(axis) - 1)]
+        return lax.ppermute(part, axis, pairs)
+
+    def downward(part, axis):
+        pairs = [(i + 1, i) for i in range(lax.axis_size(axis) - 1)]
+        return lax.ppermute(part, axis, pairs)
+
+    square = jax.ShapeDtypeStruct((channels, channels), BF16)
+    strip = jax.ShapeDtypeStruct((height, RIM, channels), BF16)
+    down = downward(tile[:RIM], "gy")
+    tile, bottom, low, high, info = pl.pallas_call(
         load_kernel,
         out_shape=(
             jax.ShapeDtypeStruct(tile.shape, BF16),
-            strip_shape,
-            strip_shape,
+            jax.ShapeDtypeStruct((RIM, width, channels), BF16),
+            strip,
+            strip,
             jax.ShapeDtypeStruct((8, LANES), F32),
         ),
-        in_specs=[SMEM, VMEM],
-        out_specs=(VMEM,) * 4,
+        in_specs=[SMEM, SMEM, VMEM],
+        out_specs=(VMEM,) * 5,
         compiler_params=SMALL,
         name="load",
-    )(scalars, tile)
-    def strip(own, start):
-        ends = [part[:, start : start + RIM] for part in (up, down)]
-        return jnp.concatenate([ends[0], own, ends[1]], axis=0)
-
-    low_strip, high_strip = strip(low, 0), strip(high, width - RIM)
-    left, right = edges(low_strip, high_strip, "gx")
-    square = (channels, channels)
-    weights, point, point_turned, classes, toward = pl.pallas_call(
+    )(valid_count.reshape(1), labels, tile)
+    up = upward(bottom, "gy")
+
+    right = downward(
+        jnp.concatenate([up[:, :RIM], low, down[:, :RIM]], axis=0), "gx"
+    )
+    strip, weights, point, point_turned, classes, toward = pl.pallas_call(
         weights_kernel,
         out_shape=(
+            jax.ShapeDtypeStruct((height + 2 * RIM, RIM, channels), BF16),
             jax.ShapeDtypeStruct((9, channels), F32),
-            jax.ShapeDtypeStruct(square, BF16),
-            jax.ShapeDtypeStruct(square, BF16),
+            square,
+            square,
             jax.ShapeDtypeStruct(classifier.shape, F32),
-            jax.ShapeDtypeStruct(square, F32),
-        ),
-        in_specs=[VMEM] * 4,
-        out_specs=(VMEM,) * 5,
+            jax.ShapeDtypeStruct((channels, channels), F32),
+        ),
+        in_specs=[VMEM] * 6,
+        out_specs=(VMEM,) * 6,
         compiler_params=SMALL,
         name="weights",
-    )(low_strip, depth_weight, point_weight, classifier)
+    )(up, high, down, depth_weight, point_weight, classifier)
+    left = upward(strip, "gx")
 
     halo = (tile, up, down, left, right)
     chunks = -(-(channels + 3) // planes)
@@ -516,26 +523,28 @@
         ),
         name="spread",
     )(back, weights)
-    shares, spread = pl.pallas_call(
+    shares, small, spread = pl.pallas_call(
         functools.partial(slide_sum_kernel, rd),
         out_shape=(
             jax.ShapeDtypeStruct((main, channels), BF16),
-            jax.ShapeDtypeStruct((planes, rd * channels // LANES, LANES), F32),
+            jax.ShapeDtypeStruct((8, channels), F32),
+            jax.ShapeDtypeStruct((planes, rd * channels // LANES, LANES), BF16),
         ),
         in_specs=[VMEM],
-        out_specs=(VMEM, VMEM),
+        out_specs=(VMEM, VMEM, VMEM),
         compiler_params=SMALL,
         name="slide_sum",
     )(received)
     spread = lax.all_to_all(spread, ("gy", "gx"), 0, 0)
+    spread, gradient = lax.optimization_barrier((spread, gradient))
     joined = pl.pallas_call(
-        join_kernel,
+        functools.partial(join_kernel, rd),
         out_shape=jax.ShapeDtypeStruct((slides, main + 16, channels), BF16),
-        in_specs=[VMEM, VMEM],
+        in_specs=[VMEM] * 4,
         out_specs=VMEM,
         compiler_params=SMALL,
         name="join",
-    )(shares, spread)
+    )(info, shares, small, spread)
     joined = lax.all_to_all(joined, "slide", 0, 0)
     loss, depth, point_total, class_total = pl.pallas_call(
         finish_kernel,

time: 143 us -> 143 us (level)
  waiting for transfers between devices: 4.98 us -> 13.7 us
  blocking collectives: 97.6 us -> 89.5 us
    all_to_all x1, blocking collectives: 21.1 us -> 11.3 us  [per_device(): joined = lax.all_to_all(joined, 'slide', 0, 0)]
    all_to_all x1, waiting for transfers between devices: 4.57 us -> 11.6 us  [per_device(): spread = lax.all_to_all(spread, ('gy', 'gx'), 0, 0)]
    ppermute x4, waiting for transfers between devices: 0.41 us -> 2.17 us  [the longest x2 2.17 us: upward(): return lax.ppermute(part, axis, pairs)]
    all_to_all x1, blocking collectives: 17.4 us -> 18.9 us  [per_device(): received = lax.all_to_all(sent, 'slide', 0, 0)]
  transfers between devices with their start and end apart: 5 -> 5, of which waited for: 2 -> 3; matrix products, arithmetic and copies ran while one was open for 0% -> 0% of each run, Pallas kernels for 2% -> 2%
where the time goes in v6:
time: 143 us; the launch traced here: 142 us
  blocking collectives  89.5 us (63%)
  starting transfers between devices  18 us (13%)
  Pallas kernels  14.5 us (10%)
  waiting for transfers between devices  13.7 us (10%)
  local copies, waits for them, and re-layouts  4.53 us (3%)
  between operations  2.04 us (1%)
    all_to_all x1, blocking collectives, per_device(): packed = lax.all_to_all(packed, ('gy', 'gx'), 0, 0)  39.2 us
    all_to_all x1, blocking collectives, per_device(): gathered = lax.all_to_all(packed, ('gy', 'gx'), 0, 0)  20.2 us
    all_to_all x1, blocking collectives, per_device(): received = lax.all_to_all(sent, 'slide', 0, 0)  18.9 us
    all_to_all x1, waiting for transfers between devices, per_device(): spread = lax.all_to_all(spread, ('gy', 'gx'), 0, 0)  11.6 us
    all_to_all x1, blocking collectives, per_device(): joined = lax.all_to_all(joined, 'slide', 0, 0)  11.3 us
    ppermute x2, starting transfers between devices, upward(): return lax.ppermute(part, axis, pairs)  9.44 us
    pallas_call x1, Pallas kernels, per_device(): pl.pallas_call(functools.partial(cov_kernel, grid_y, grid_x, slides), out...  8.28 us
    all_to_all x1, starting transfers between devices, per_device(): spread = lax.all_to_all(spread, ('gy', 'gx'), 0, 0)  5.94 us
  transfers between devices with their start and end apart: 5, of which 3 were waited for; matrix products, arithmetic and copies ran while one was open for 0% of the time, Pallas kernels for 2%

profile of v6, /device:TPU:1, one launch (start us, length us, event | category | flops | bytes accessed | tf_op | source)
XLA Modules:
  0.0 142.4 jit_solution(10320841762633858444)
XLA Ops:
  0.6 0.8 slice_bitcast_fusion
  1.5 1.3 collective-permute-start.1
  4.1 1.0 copy-done
  5.2 5.5 %collective-permute-start = (bf16[2,64,256]{2,1,0:T(8,128)(2,1)S(1)}, bf16[2,64,256]{2,1,0:T(8,128)(2,1)S(1)}, u32[]{:S(2)}, u32[]{:S(2)}) collective-permute-start(bf16[2,64,256]{2,1,0:T(8,128)(2,1)S(1)} %get-tuple-element.32), channel_id=1, source_target_pairs={{0,8},{8,16},{16,24},{24,32},{32,40},{40,48},{48,56},{56,64},{64,7... | collective-permute-start | bytes 196616 | tf_op jit(solution)/shard_map/ppermute | solution.py:420
  10.7 1.3 collective-permute-done.up
  12.0 1.3 collective-permute-start.3
  13.3 1.0 copy-done.1
  14.3 0.9 copy-done.2
  15.2 0.7 copy-done.3
  15.9 0.2 weights.2
  16.1 4.0 %collective-permute-start.2 = (bf16[20,2,256]{2,1,0:T(2,128)(2,1)S(1)}, bf16[20,2,256]{2,1,0:T(2,128)(2,1)S(1)}, u32[]{:S(2)}, u32[]{:S(2)}) collective-permute-start(bf16[20,2,256]{2,1,0:T(2,128)(2,1)S(1)} %get-tuple-element.34), channel_id=1, source_target_pairs={{0,1},{1,2},{2,3},{3,4},{4,5},{5,6},{6,7},{8,9},{9,10},{10,11},{11... | collective-permute-start | bytes 61448 | tf_op jit(solution)/shard_map/ppermute | solution.py:420
  20.1 0.9 collective-permute-done.2.left
  21.0 2.2 %forward.1 = (bf16[1440,256]{1,0:T(8,128)(2,1)S(1)}, f32[96,4,128]{2,1,0:T(4,128)S(1)}, f32[20,80,256]{2,1,0:T(8,128)S(1)}) custom-call(f32[8,128]{1,0:T(8,128)S(1)} %get-tuple-element.30.info, bf16[16,64,256]{2,1,0:T(8,128)(2,1)S(1)} %get-tuple-element.31.tile, bf16[2,64,256]{2,1,0:T(8,128)(2,1)S(1)} %collective-permute-done.up, ...), custom_call_target="tpu_custom_call" | custom-call | tf_op jit(solution)/shard_map/forward/pallas_call | solution.py:470
  23.2 39.2 %all_to_all.25.terms = f32[96,4,128]{2,1,0:T(4,128)S(1)} all-to-all(f32[96,4,128]{2,1,0:T(4,128)S(1)} %get-tuple-element.38), channel_id=1, replica_groups=mesh['slide'=8,'gy'=12,'gx'=8] {'gy','gx'}, dimensions={0} | all-to-all | bytes 393216 | tf_op jit(solution)/shard_map/all_to_all | solution.py:487
  62.4 0.1 plane_sum.1
  62.5 20.2 %all_to_all.26.gathered = f32[96,4,128]{2,1,0:T(4,128)S(1)} all-to-all(f32[96,4,128]{2,1,0:T(4,128)S(1)} %plane_sum.1), channel_id=1, replica_groups=mesh['slide'=8,'gy'=12,'gx'=8] {'gy','gx'}, dimensions={0} | all-to-all | bytes 393216 | tf_op jit(solution)/shard_map/all_to_all | solution.py:497
  82.7 8.3 %covariance.1 = (bf16[1440,256]{1,0:T(8,128)(2,1)S(1)}, f32[8,56,256]{2,1,0:T(8,128)S(1)}) custom-call(f32[8,128]{1,0:T(8,128)S(1)} %get-tuple-element.30.info, f32[96,4,128]{2,1,0:T(4,128)S(1)} %all_to_all.26.gathered, f32[20,80,256]{2,1,0:T(8,128)S(1)} %get-tuple-element.39.ext, bf16[1440,256]{1,0:T(8,128)(2,1)S(1)} %get-tuple-element.40.mapped, ...), custom_call_target="tpu_custom_call" | custom-call | tf_op jit(solution)/shard_map/covariance/pallas_call | solution.py:501
  91.0 18.9 %all_to_all.27.terms = f32[8,56,256]{2,1,0:T(8,128)S(1)} all-to-all(f32[8,56,256]{2,1,0:T(8,128)S(1)} %get-tuple-element.44), channel_id=1, replica_groups=mesh['slide'=8,'gy'=12,'gx'=8] {'slide'}, dimensions={0} | all-to-all | bytes 917504 | tf_op jit(solution)/shard_map/all_to_all | solution.py:514
  109.8 0.7 slide_sum.1
  110.5 5.9 %all-to-all-start.3 = ((bf16[96,4,128]{2,1,0:T(4,128)(2,1)}), bf16[96,4,128]{2,1,0:T(4,128)(2,1)S(1)}, u32[]{:S(2)}, u32[]{:S(2)}) async-start(bf16[96,4,128]{2,1,0:T(4,128)(2,1)} %get-tuple-element.47), calls=%async_computation.3 | async-start | bytes 196608 | tf_op jit(solution)/shard_map/all_to_all | solution.py:538
  116.5 2.0 %spread.1 = bf16[16,64,256]{2,1,0:T(8,128)(2,1)} custom-call(bf16[1440,256]{1,0:T(8,128)(2,1)S(1)} %get-tuple-element.48.back, f32[9,256]{1,0:T(8,128)S(1)} %get-tuple-element.36.weights), custom_call_target="tpu_custom_call" | custom-call | flops 7372800 | bytes 4194304 | tf_op jit(solution)/shard_map/spread/pallas_call | solution.py:515
  118.4 11.6 %all-to-all-done.3.spread = bf16[96,4,128]{2,1,0:T(4,128)(2,1)S(1)} async-done(((bf16[96,4,128]{2,1,0:T(4,128)(2,1)}), bf16[96,4,128]{2,1,0:T(4,128)(2,1)S(1)}, u32[]{:S(2)}, u32[]{:S(2)}) %all-to-all-start.3) | async-done | bytes 98336 | tf_op jit(solution)/shard_map/all_to_all | solution.py:538
  130.1 11.3 %all_to_all.28.terms = bf16[8,64,256]{2,1,0:T(8,128)(2,1)S(1)} all-to-all(bf16[8,64,256]{2,1,0:T(8,128)(2,1)S(1)} %join.1), channel_id=1, replica_groups=mesh['slide'=8,'gy'=12,'gx'=8] {'slide'}, dimensions={0} | all-to-all | bytes 524288 | tf_op jit(solution)/shard_map/all_to_all | solution.py:548
  141.4 0.9 finish.1
  (11 shorter events, 0.3 us)
Async XLA Ops:
  1.5 9.2 %collective-permute-start.1 = (bf16[2,64,256]{2,1,0:T(8,128)(2,1)S(1)}, bf16[2,64,256]{2,1,0:T(8,128)(2,1)S(1)}, u32[]{:S(2)}, u32[]{:S(2)}) collective-permute-start(bf16[2,64,256]{2,1,0:T(8,128)(2,1)S(1)} %slice_bitcast_fusion), channel_id=1, source_target_pairs={{8,0},{16,8},{24,16},{32,24},{40,32},{48,40},{56,48},{64,56},{72,6... | collective-permute-start | bytes 196616 | tf_op jit(solution)/shard_map/ppermute | solution.py:424
  4.1 1.0 copy-start
  5.2 6.8 %collective-permute-start = (bf16[2,64,256]{2,1,0:T(8,128)(2,1)S(1)}, bf16[2,64,256]{2,1,0:T(8,128)(2,1)S(1)}, u32[]{:S(2)}, u32[]{:S(2)}) collective-permute-start(bf16[2,64,256]{2,1,0:T(8,128)(2,1)S(1)} %get-tuple-element.32), channel_id=1, source_target_pairs={{0,8},{8,16},{16,24},{24,32},{32,40},{40,48},{48,56},{56,64},{64,7... | collective-permute-start | bytes 196616 | tf_op jit(solution)/shard_map/ppermute | solution.py:420
  12.0 8.1 %collective-permute-start.3 = (bf16[20,2,256]{2,1,0:T(2,128)(2,1)S(1)}, bf16[20,2,256]{2,1,0:T(2,128)(2,1)S(1)}, u32[]{:S(2)}, u32[]{:S(2)}) collective-permute-start(bf16[20,2,256]{2,1,0:T(2,128)(2,1)S(1)} %pad_maximum_fusion), channel_id=1, source_target_pairs={{1,0},{2,1},{3,2},{4,3},{5,4},{6,5},{7,6},{9,8},{10,9},{11,10},{12... | collective-permute-start | bytes 61448 | tf_op jit(solution)/shard_map/ppermute | solution.py:424
  13.3 1.0 copy-start.1
  14.3 0.9 copy-start.2
  15.2 0.7 copy-start.3
  16.1 4.9 %collective-permute-start.2 = (bf16[20,2,256]{2,1,0:T(2,128)(2,1)S(1)}, bf16[20,2,256]{2,1,0:T(2,128)(2,1)S(1)}, u32[]{:S(2)}, u32[]{:S(2)}) collective-permute-start(bf16[20,2,256]{2,1,0:T(2,128)(2,1)S(1)} %get-tuple-element.34), channel_id=1, source_target_pairs={{0,1},{1,2},{2,3},{3,4},{4,5},{5,6},{6,7},{8,9},{9,10},{10,11},{11... | collective-permute-start | bytes 61448 | tf_op jit(solution)/shard_map/ppermute | solution.py:420
  110.5 19.5 %all-to-all-start.3 = ((bf16[96,4,128]{2,1,0:T(4,128)(2,1)}), bf16[96,4,128]{2,1,0:T(4,128)(2,1)S(1)}, u32[]{:S(2)}, u32[]{:S(2)}) async-start(bf16[96,4,128]{2,1,0:T(4,128)(2,1)} %get-tuple-element.47), calls=%async_computation.3 | async-start | bytes 196608 | tf_op jit(solution)/shard_map/all_to_all | solution.py:538

commit v7 on v6

--- a/solution.py
+++ b/solution.py
@@ -88,34 +88,23 @@
     ext[:, LEFT + width : LEFT + width + RIM, :] = right[...].astype(F32)
 
 
-def load_kernel(count, label, tile_in, tile, bottom, low, high, info):
-    height, width, _ = tile.shape
+def load_kernel(tile_in, tile, low, high):
+    width = tile.shape[1]
     tile[...] = tile_in[...]
-    bottom[...] = tile_in[height - RIM :]
     low[...] = tile_in[:, :RIM, :]
     high[...] = tile_in[:, width - RIM :, :]
-    row = iota(info.shape, 0)
-    value = jnp.zeros(info.shape, F32)
-    for k, scalar in enumerate(
-        (count[0], label[0], lax.axis_index("gy"), lax.axis_index("gx"), lax.axis_index("slide"))
-    ):
-        value = jnp.where(row == k, scalar.astype(jnp.int32).astype(F32), value)
-    info[...] = value
-
-
-def weights_kernel(
-    up, own, down, weights, point, classifier, strip, taps, mixing, turned, classes, toward
-):
-    height, width = own.shape[0], up.shape[1]
-    strip[0:RIM] = up[:, width - RIM :, :]
-    strip[RIM : RIM + height] = own[...]
-    strip[RIM + height :] = down[:, width - RIM :, :]
+
+
+def weights_kernel(count, label, strip, weights, point, taps, mixing, turned, info):
     taps[...] = jnp.concatenate([weights[a].astype(F32) for a in range(3)], axis=0)
     mixing[...] = point[...]
     turned[...] = point[...].astype(F32).T.astype(BF16)
-    classes[...] = classifier[...]
-    gap = classifier[0] - classifier[1]
-    toward[...] = gap + gap.T
+    row = iota(info.shape, 0)
+    value = jnp.zeros(info.shape, F32)
+    scalars = [count[0], label[0]] + [lax.axis_index(axis) for axis in ("gy", "gx", "slide")]
+    for k, scalar in enumerate(scalars):
+        value = jnp.where(row == k, scalar.astype(jnp.int32).astype(F32), value)
+    info[...] = value
 
 
 def forward_kernel(
@@ -150,13 +139,15 @@
     kept = inner[...]
     gram = lax.dot_general(kept, kept, (((0,), (0,)), ((), ())), preferred_element_type=F32)
     mapped[...] = dot(hidden[...], point[...]).astype(BF16)
-    sums = jnp.sum(kept.astype(F32), axis=0, keepdims=True)
+    ones = jnp.ones((16, height * width), BF16)
+    sums = dot(ones, kept)[0:1]
+    first = dot(ones, dot(kept, point[...]).astype(BF16))[0:1]
     upper, both, diag = tri_pack(gram)
     chunks = packed.shape[1] - 1
-    spare = chunks * planes - 2 * LANES - 3
+    lines = [line[:, p : p + LANES] for line in (sums, first) for p in range(0, channels, LANES)]
+    spare = chunks * planes - 2 * LANES - 1 - len(lines)
     flat = jnp.concatenate(
-        [upper, both, diag, sums[:, :LANES], sums[:, LANES:], jnp.zeros((spare, LANES), F32)],
-        axis=0,
+        [upper, both, diag] + lines + [jnp.zeros((spare, LANES), F32)], axis=0
     )
     for q in range(chunks):
         packed[:, q, :] = flat[q * planes : (q + 1) * planes]
@@ -171,8 +162,8 @@
 
 
 def cov_kernel(
-    grid_y, grid_x, slides, info, gathered, ext, mapped, toward_ref, point, point_turned,
-    classifier, back_out, sent, back, sem,
+    grid_y, grid_x, slides, info, gathered, ext, mapped, point, point_turned, classes,
+    back_out, sent, back, classifier, sems,
 ):
     planes = grid_y * grid_x
     wide, channels = ext.shape[1:]
@@ -180,6 +171,8 @@
     half = channels // 2
     chunks = gathered.shape[1] - 1
 
+    fetch = pltpu.make_async_copy(classes, classifier, sems.at[0])
+    fetch.start()
     flat = jnp.concatenate([gathered[:, q, :] for q in range(chunks)], axis=0)
     counts = gathered[:, chunks, :]
     inverse = 1.0 / jnp.sum(counts, axis=0, keepdims=True)[:, 0:1]
@@ -187,6 +180,9 @@
     sums = jnp.concatenate(
         [flat[2 * half + 1 : 2 * half + 2], flat[2 * half + 2 : 2 * half + 3]], axis=1
     )
+    mapped_sum = jnp.concatenate(
+        [flat[2 * half + 3 : 2 * half + 4], flat[2 * half + 4 : 2 * half + 5]], axis=1
+    )
     center = sums * inverse
     spread = jnp.broadcast_to(center, (channels, channels))
     moment = gram * inverse - spread * spread.T
@@ -206,7 +202,9 @@
     trace = total(jnp.where(eye, sigma, 0.0))
     start = sigma * (1.0 / trace)
 
-    toward = toward_ref[...]
+    fetch.wait()
+    toward = classifier[0] - classifier[1]
+    toward = toward + toward.T
     wmat, ymat, dw, dy = start, start, toward, toward
     for step in range(ITERS):
         w_pair, dw_pair = split(wmat), split(dw)
@@ -252,10 +250,7 @@
 
     symmetric = slant * inverse
     sym_pair = split(symmetric)
-    center_pair = split(jnp.broadcast_to(center, (8, channels)))
-    mean = dot(
-        jnp.concatenate(center_pair, axis=1), jnp.concatenate([mixing, mixing], axis=0)
-    )
+    mean = jnp.broadcast_to(mapped_sum * inverse, (8, channels))
     offset = -mm(split(mean), sym_pair)[0:1]
 
     row_id = iota((planes, LANES), 0).astype(F32)
@@ -286,7 +281,7 @@
         pieces.append(jnp.where(raster < limit, both[r * wide : (r + 1) * wide], 0.0).astype(BF16))
     back_mapped = jnp.concatenate(pieces, axis=0)
     back[...] = dot(back_mapped, mixing_turned).astype(BF16)
-    copy = pltpu.make_async_copy(back, back_out, sem)
+    copy = pltpu.make_async_copy(back, back_out, sems.at[1])
     copy.start()
 
     depth = []
@@ -425,45 +420,37 @@
 
     square = jax.ShapeDtypeStruct((channels, channels), BF16)
     strip = jax.ShapeDtypeStruct((height, RIM, channels), BF16)
-    down = downward(tile[:RIM], "gy")
-    tile, bottom, low, high, info = pl.pallas_call(
+    up, down = upward(tile[height - RIM :], "gy"), downward(tile[:RIM], "gy")
+    tile, low, high = pl.pallas_call(
         load_kernel,
-        out_shape=(
-            jax.ShapeDtypeStruct(tile.shape, BF16),
-            jax.ShapeDtypeStruct((RIM, width, channels), BF16),
-            strip,
-            strip,
-            jax.ShapeDtypeStruct((8, LANES), F32),
-        ),
-        in_specs=[SMEM, SMEM, VMEM],
-        out_specs=(VMEM,) * 5,
+        out_shape=(jax.ShapeDtypeStruct(tile.shape, BF16), strip, strip),
+        in_specs=[VMEM],
+        out_specs=(VMEM,) * 3,
         compiler_params=SMALL,
         name="load",
-    )(valid_count.reshape(1), labels, tile)
-    up = upward(bottom, "gy")
-
-    right = downward(
-        jnp.concatenate([up[:, :RIM], low, down[:, :RIM]], axis=0), "gx"
-    )
-    strip, weights, point, point_turned, classes, toward = pl.pallas_call(
+    )(tile)
+
+    low_strip = jnp.concatenate([up[:, :RIM], low, down[:, :RIM]], axis=0)
+    high_strip = jnp.concatenate(
+        [up[:, width - RIM :], high, down[:, width - RIM :]], axis=0
+    )
+    left, right = upward(high_strip, "gx"), downward(low_strip, "gx")
+    weights, point, point_turned, info = pl.pallas_call(
         weights_kernel,
         out_shape=(
-            jax.ShapeDtypeStruct((height + 2 * RIM, RIM, channels), BF16),
             jax.ShapeDtypeStruct((9, channels), F32),
             square,
             square,
-            jax.ShapeDtypeStruct(classifier.shape, F32),
-            jax.ShapeDtypeStruct((channels, channels), F32),
+            jax.ShapeDtypeStruct((8, LANES), F32),
         ),
-        in_specs=[VMEM] * 6,
-        out_specs=(VMEM,) * 6,
+        in_specs=[SMEM, SMEM] + [VMEM] * 3,
+        out_specs=(VMEM,) * 4,
         compiler_params=SMALL,
         name="weights",
-    )(up, high, down, depth_weight, point_weight, classifier)
-    left = upward(strip, "gx")
+    )(valid_count.reshape(1), labels, low_strip, depth_weight, point_weight)
 
     halo = (tile, up, down, left, right)
-    chunks = -(-(channels + 3) // planes)
+    chunks = -(-(channels + 5) // planes)
     pixels = (height + 2) * wide
     ext_shape = (height + 2 * RIM, wide, channels)
 
@@ -504,12 +491,16 @@
             jax.ShapeDtypeStruct((pixels, channels), BF16),
             jax.ShapeDtypeStruct((slides, main + 8, channels), F32),
         ),
-        in_specs=[VMEM] * 8,
+        in_specs=[VMEM] * 6 + [HBM],
         out_specs=(HBM, VMEM),
-        scratch_shapes=[pltpu.VMEM((pixels, channels), BF16), pltpu.SemaphoreType.DMA],
+        scratch_shapes=[
+            pltpu.VMEM((pixels, channels), BF16),
+            pltpu.VMEM(classifier.shape, F32),
+            pltpu.SemaphoreType.DMA((2,)),
+        ],
         compiler_params=PARAMS,
         name="covariance",
-    )(info, gathered, ext, mapped, toward, point, point_turned, classes)
+    )(info, gathered, ext, mapped, point, point_turned, classifier)
 
     received = lax.all_to_all(sent, "slide", 0, 0)
     gradient = pl.pallas_call(

time: 143 us -> 140 us (0.979)
  blocking collectives: 89.5 us -> 87.4 us
    ppermute x2, waiting for transfers between devices: 0.01 us -> 3.43 us  [downward(): return lax.ppermute(part, axis, pairs)]
    ppermute x2, waiting for transfers between devices: 2.17 us -> 0.01 us  [upward(): return lax.ppermute(part, axis, pairs)]
where the time goes in v7:
time: 140 us; the launch traced here: 139 us
  blocking collectives  87.4 us (62%)
  starting transfers between devices  16.6 us (12%)
  waiting for transfers between devices  15 us (11%)
  Pallas kernels  14.7 us (10%)
  local copies, waits for them, and re-layouts  3.53 us (3%)
  between operations  2.04 us (1%)
    all_to_all x1, blocking collectives, per_device(): packed = lax.all_to_all(packed, ('gy', 'gx'), 0, 0)  37.8 us
    all_to_all x1, blocking collectives, per_device(): gathered = lax.all_to_all(packed, ('gy', 'gx'), 0, 0)  20.1 us
    all_to_all x1, blocking collectives, per_device(): received = lax.all_to_all(sent, 'slide', 0, 0)  18.1 us
    all_to_all x1, waiting for transfers between devices, per_device(): spread = lax.all_to_all(spread, ('gy', 'gx'), 0, 0)  11.6 us
    all_to_all x1, blocking collectives, per_device(): joined = lax.all_to_all(joined, 'slide', 0, 0)  11.3 us
    pallas_call x1, Pallas kernels, per_device(): pl.pallas_call(functools.partial(cov_kernel, grid_y, grid_x, slides), out...  8.09 us
    ppermute x2, starting transfers between devices, upward(): return lax.ppermute(part, axis, pairs)  8.03 us
    all_to_all x1, starting transfers between devices, per_device(): spread = lax.all_to_all(spread, ('gy', 'gx'), 0, 0)  5.94 us
  transfers between devices with their start and end apart: 5, of which 3 were waited for; matrix products, arithmetic and copies ran while one was open for 0% of the time, Pallas kernels for 2%

profile of v7, /device:TPU:1, one launch (start us, length us, event | category | flops | bytes accessed | tf_op | source)
XLA Modules:
  0.0 139.2 jit_solution(11329184341513775184)
XLA Ops:
  0.6 0.9 slice_bitcast_fusion.1
  1.5 4.8 %collective-permute-start = (bf16[2,64,256]{2,1,0:T(8,128)(2,1)S(1)}, bf16[2,64,256]{2,1,0:T(8,128)(2,1)S(1)}, u32[]{:S(2)}, u32[]{:S(2)}) collective-permute-start(bf16[2,64,256]{2,1,0:T(8,128)(2,1)S(1)} %get-tuple-element.47), channel_id=1, source_target_pairs={{0,8},{8,16},{16,24},{24,32},{32,40},{40,48},{48,56},{56,64},{64,7... | collective-permute-start | bytes 196616 | tf_op jit(solution)/shard_map/ppermute | solution.py:415
  6.4 1.3 collective-permute-start.1
  7.7 1.0 copy-done
  8.8 3.2 %collective-permute-done.1.down = bf16[2,64,256]{2,1,0:T(8,128)(2,1)S(1)} collective-permute-done((bf16[2,64,256]{2,1,0:T(8,128)(2,1)S(1)}, bf16[2,64,256]{2,1,0:T(8,128)(2,1)S(1)}, u32[]{:S(2)}, u32[]{:S(2)}) %collective-permute-start.1) | collective-permute-done | bytes 65568 | tf_op jit(solution)/shard_map/ppermute | solution.py:419
  12.1 3.2 %collective-permute-start.2 = (bf16[20,2,256]{2,1,0:T(2,128)(2,1)S(1)}, bf16[20,2,256]{2,1,0:T(2,128)(2,1)S(1)}, u32[]{:S(2)}, u32[]{:S(2)}) collective-permute-start(bf16[20,2,256]{2,1,0:T(2,128)(2,1)S(1)} %pad_maximum_fusion.1), channel_id=1, source_target_pairs={{0,1},{1,2},{2,3},{3,4},{4,5},{5,6},{6,7},{8,9},{9,10},{10,11},{11... | collective-permute-start | bytes 61448 | tf_op jit(solution)/shard_map/ppermute | solution.py:415
  15.3 1.3 collective-permute-start.3
  17.9 0.9 copy-done.2
  18.8 0.7 copy-done.3
  19.5 0.1 weights.2
  19.6 0.2 collective-permute-done.3.right
  19.8 2.6 %forward.1 = (bf16[1440,256]{1,0:T(8,128)(2,1)S(1)}, f32[96,4,128]{2,1,0:T(4,128)S(1)}, f32[20,80,256]{2,1,0:T(8,128)S(1)}) custom-call(f32[8,128]{1,0:T(8,128)S(1)} %get-tuple-element.27.info, bf16[16,64,256]{2,1,0:T(8,128)(2,1)S(1)} %get-tuple-element.28.tile, bf16[2,64,256]{2,1,0:T(8,128)(2,1)S(1)} %collective-permute-done.up, ...), custom_call_target="tpu_custom_call" | custom-call | tf_op jit(solution)/shard_map/forward/pallas_call | solution.py:457
  22.4 37.8 %all_to_all.25.terms = f32[96,4,128]{2,1,0:T(4,128)S(1)} all-to-all(f32[96,4,128]{2,1,0:T(4,128)S(1)} %get-tuple-element.32), channel_id=1, replica_groups=mesh['slide'=8,'gy'=12,'gx'=8] {'gy','gx'}, dimensions={0} | all-to-all | bytes 393216 | tf_op jit(solution)/shard_map/all_to_all | solution.py:474
  60.2 0.1 plane_sum.1
  60.4 20.1 %all_to_all.26.gathered = f32[96,4,128]{2,1,0:T(4,128)S(1)} all-to-all(f32[96,4,128]{2,1,0:T(4,128)S(1)} %plane_sum.1), channel_id=1, replica_groups=mesh['slide'=8,'gy'=12,'gx'=8] {'gy','gx'}, dimensions={0} | all-to-all | bytes 393216 | tf_op jit(solution)/shard_map/all_to_all | solution.py:484
  80.5 8.1 %covariance.1 = (bf16[1440,256]{1,0:T(8,128)(2,1)S(1)}, f32[8,56,256]{2,1,0:T(8,128)S(1)}) custom-call(f32[8,128]{1,0:T(8,128)S(1)} %get-tuple-element.27.info, f32[96,4,128]{2,1,0:T(4,128)S(1)} %all_to_all.26.gathered, f32[20,80,256]{2,1,0:T(8,128)S(1)} %get-tuple-element.33.ext, bf16[1440,256]{1,0:T(8,128)(2,1)S(1)} %get-tuple-element.34.mapped, ...), custom_call_target="tpu_custom_call" | custom-call | tf_op jit(solution)/shard_map/covariance/pallas_call | solution.py:488
  88.6 18.1 %all_to_all.27.terms = f32[8,56,256]{2,1,0:T(8,128)S(1)} all-to-all(f32[8,56,256]{2,1,0:T(8,128)S(1)} %get-tuple-element.36), channel_id=1, replica_groups=mesh['slide'=8,'gy'=12,'gx'=8] {'slide'}, dimensions={0} | all-to-all | bytes 917504 | tf_op jit(solution)/shard_map/all_to_all | solution.py:505
  106.7 0.7 slide_sum.1
  107.4 5.9 %all-to-all-start.3 = ((bf16[96,4,128]{2,1,0:T(4,128)(2,1)}), bf16[96,4,128]{2,1,0:T(4,128)(2,1)S(1)}, u32[]{:S(2)}, u32[]{:S(2)}) async-start(bf16[96,4,128]{2,1,0:T(4,128)(2,1)} %get-tuple-element.39), calls=%async_computation.3 | async-start | bytes 196608 | tf_op jit(solution)/shard_map/all_to_all | solution.py:529
  113.3 2.0 %spread.1 = bf16[16,64,256]{2,1,0:T(8,128)(2,1)} custom-call(bf16[1440,256]{1,0:T(8,128)(2,1)S(1)} %get-tuple-element.40.back, f32[9,256]{1,0:T(8,128)S(1)} %get-tuple-element.30.weights), custom_call_target="tpu_custom_call" | custom-call | flops 7372800 | bytes 4194304 | tf_op jit(solution)/shard_map/spread/pallas_call | solution.py:506
  115.3 11.6 %all-to-all-done.3.spread = bf16[96,4,128]{2,1,0:T(4,128)(2,1)S(1)} async-done(((bf16[96,4,128]{2,1,0:T(4,128)(2,1)}), bf16[96,4,128]{2,1,0:T(4,128)(2,1)S(1)}, u32[]{:S(2)}, u32[]{:S(2)}) %all-to-all-start.3) | async-done | bytes 98336 | tf_op jit(solution)/shard_map/all_to_all | solution.py:529
  126.9 0.1 join.1
  127.0 11.3 %all_to_all.28.terms = bf16[8,64,256]{2,1,0:T(8,128)(2,1)S(1)} all-to-all(bf16[8,64,256]{2,1,0:T(8,128)(2,1)S(1)} %join.1), channel_id=1, replica_groups=mesh['slide'=8,'gy'=12,'gx'=8] {'slide'}, dimensions={0} | all-to-all | bytes 524288 | tf_op jit(solution)/shard_map/all_to_all | solution.py:539
  138.3 0.9 finish.1
  (12 shorter events, 0.2 us)
Async XLA Ops:
  1.5 7.3 %collective-permute-start = (bf16[2,64,256]{2,1,0:T(8,128)(2,1)S(1)}, bf16[2,64,256]{2,1,0:T(8,128)(2,1)S(1)}, u32[]{:S(2)}, u32[]{:S(2)}) collective-permute-start(bf16[2,64,256]{2,1,0:T(8,128)(2,1)S(1)} %get-tuple-element.47), channel_id=1, source_target_pairs={{0,8},{8,16},{16,24},{24,32},{32,40},{40,48},{48,56},{56,64},{64,7... | collective-permute-start | bytes 196616 | tf_op jit(solution)/shard_map/ppermute | solution.py:415
  6.4 5.6 %collective-permute-start.1 = (bf16[2,64,256]{2,1,0:T(8,128)(2,1)S(1)}, bf16[2,64,256]{2,1,0:T(8,128)(2,1)S(1)}, u32[]{:S(2)}, u32[]{:S(2)}) collective-permute-start(bf16[2,64,256]{2,1,0:T(8,128)(2,1)S(1)} %get-tuple-element.48), channel_id=1, source_target_pairs={{8,0},{16,8},{24,16},{32,24},{40,32},{48,40},{56,48},{64,56},{72,6... | collective-permute-start | bytes 196616 | tf_op jit(solution)/shard_map/ppermute | solution.py:419
  7.7 1.0 copy-start
  8.7 71.8 %copy-start.1 = (f32[2,256,256]{2,1,0:T(8,128)S(1)}, f32[2,256,256]{2,1,0:T(8,128)}, u32[]{:S(2)}) copy-start(f32[2,256,256]{2,1,0:T(8,128)} %classes.1) | copy-start | bytes 1572868
  12.1 7.6 %collective-permute-start.2 = (bf16[20,2,256]{2,1,0:T(2,128)(2,1)S(1)}, bf16[20,2,256]{2,1,0:T(2,128)(2,1)S(1)}, u32[]{:S(2)}, u32[]{:S(2)}) collective-permute-start(bf16[20,2,256]{2,1,0:T(2,128)(2,1)S(1)} %pad_maximum_fusion.1), channel_id=1, source_target_pairs={{0,1},{1,2},{2,3},{3,4},{4,5},{5,6},{6,7},{8,9},{9,10},{10,11},{11... | collective-permute-start | bytes 61448 | tf_op jit(solution)/shard_map/ppermute | solution.py:415
  15.3 4.5 %collective-permute-start.3 = (bf16[20,2,256]{2,1,0:T(2,128)(2,1)S(1)}, bf16[20,2,256]{2,1,0:T(2,128)(2,1)S(1)}, u32[]{:S(2)}, u32[]{:S(2)}) collective-permute-start(bf16[20,2,256]{2,1,0:T(2,128)(2,1)S(1)} %pad_maximum_fusion.strip), channel_id=1, source_target_pairs={{1,0},{2,1},{3,2},{4,3},{5,4},{6,5},{7,6},{9,8},{10,9},{11,10},{12... | collective-permute-start | bytes 61448 | tf_op jit(solution)/shard_map/ppermute | solution.py:419
  17.9 0.9 copy-start.2
  18.8 0.7 copy-start.3
  107.4 19.5 %all-to-all-start.3 = ((bf16[96,4,128]{2,1,0:T(4,128)(2,1)}), bf16[96,4,128]{2,1,0:T(4,128)(2,1)S(1)}, u32[]{:S(2)}, u32[]{:S(2)}) async-start(bf16[96,4,128]{2,1,0:T(4,128)(2,1)} %get-tuple-element.39), calls=%async_computation.3 | async-start | bytes 196608 | tf_op jit(solution)/shard_map/all_to_all | solution.py:529

commit v8 on v7

--- a/solution.py
+++ b/solution.py
@@ -15,7 +15,6 @@
 BF16 = jnp.bfloat16
 VMEM = pl.BlockSpec(memory_space=pltpu.VMEM)
 HBM = pl.BlockSpec(memory_space=pltpu.HBM)
-SMEM = pl.BlockSpec(memory_space=pltpu.SMEM)
 PARAMS = pltpu.CompilerParams(vmem_limit_bytes=16 * 1024 * 1024)
 SMALL = pltpu.CompilerParams(vmem_limit_bytes=4 * 1024 * 1024)
 
@@ -95,20 +94,20 @@
     high[...] = tile_in[:, width - RIM :, :]
 
 
-def weights_kernel(count, label, strip, weights, point, taps, mixing, turned, info):
+def weights_kernel(scalars, strip, weights, point, taps, mixing, turned, info):
     taps[...] = jnp.concatenate([weights[a].astype(F32) for a in range(3)], axis=0)
     mixing[...] = point[...]
     turned[...] = point[...].astype(F32).T.astype(BF16)
     row = iota(info.shape, 0)
-    value = jnp.zeros(info.shape, F32)
-    scalars = [count[0], label[0]] + [lax.axis_index(axis) for axis in ("gy", "gx", "slide")]
-    for k, scalar in enumerate(scalars):
-        value = jnp.where(row == k, scalar.astype(jnp.int32).astype(F32), value)
+    value = scalars[...]
+    for k, axis in enumerate(("gy", "gx", "slide")):
+        position = lax.axis_index(axis).astype(jnp.int32).astype(F32)
+        value = jnp.where(row == k + 2, position, value)
     info[...] = value
 
 
 def forward_kernel(
-    planes, info, tile, up, down, left, right, weights, point, mapped, packed, ext, hidden, inner
+    planes, grid_x, info, tile, up, down, left, right, weights, point, mapped, packed, ext, hidden, inner
 ):
     height, width, channels = tile.shape
     wide = ext.shape[1]
@@ -134,7 +133,7 @@
 
             return carry
 
-        lax.fori_loop(0, height + 2, body, 0)
+        lax.fori_loop(0, height + 2, body, 0, unroll=2)
 
     kept = inner[...]
     gram = lax.dot_general(kept, kept, (((0,), (0,)), ((), ())), preferred_element_type=F32)
@@ -143,22 +142,20 @@
     sums = dot(ones, kept)[0:1]
     first = dot(ones, dot(kept, point[...]).astype(BF16))[0:1]
     upper, both, diag = tri_pack(gram)
-    chunks = packed.shape[1] - 1
+    chunks = packed.shape[2] // LANES
     lines = [line[:, p : p + LANES] for line in (sums, first) for p in range(0, channels, LANES)]
+    spot = info[2:3, :] * grid_x + info[3:4, :]
+    lines.append(jnp.where(iota((1, LANES), 1).astype(F32) == spot, info[0:1, :], 0.0))
     spare = chunks * planes - 2 * LANES - 1 - len(lines)
     flat = jnp.concatenate(
         [upper, both, diag] + lines + [jnp.zeros((spare, LANES), F32)], axis=0
     )
     for q in range(chunks):
-        packed[:, q, :] = flat[q * planes : (q + 1) * planes]
-    packed[:, chunks, :] = jnp.zeros((planes, LANES), F32)
-
-
-def plane_sum_kernel(info, terms, out):
-    planes, rows, lanes = terms.shape
-    summed = jnp.sum(terms[...], axis=0)
-    summed = jnp.where(iota((rows, lanes), 0) == rows - 1, info[0:1, 0:1], summed)
-    out[...] = jnp.broadcast_to(summed[None], out.shape)
+        packed[:, 0, q * LANES : (q + 1) * LANES] = flat[q * planes : (q + 1) * planes]
+
+
+def plane_sum_kernel(terms, out):
+    out[...] = jnp.broadcast_to(jnp.sum(terms[...], axis=0, keepdims=True), out.shape)
 
 
 def cov_kernel(
@@ -169,13 +166,15 @@
     wide, channels = ext.shape[1:]
     height, width = ext.shape[0] - 2 * RIM, wide - 2 * LEFT
     half = channels // 2
-    chunks = gathered.shape[1] - 1
+    chunks = gathered.shape[2] // LANES
 
     fetch = pltpu.make_async_copy(classes, classifier, sems.at[0])
     fetch.start()
-    flat = jnp.concatenate([gathered[:, q, :] for q in range(chunks)], axis=0)
-    counts = gathered[:, chunks, :]
-    inverse = 1.0 / jnp.sum(counts, axis=0, keepdims=True)[:, 0:1]
+    flat = jnp.concatenate(
+        [gathered[:, 0, q * LANES : (q + 1) * LANES] for q in range(chunks)], axis=0
+    )
+    counts = flat[2 * half + 5 : 2 * half + 6]
+    inverse = 1.0 / jnp.sum(counts, axis=1, keepdims=True)
     gram = tri_unpack(flat[:half], flat[half : 2 * half], flat[2 * half : 2 * half + 1])
     sums = jnp.concatenate(
         [flat[2 * half + 1 : 2 * half + 2], flat[2 * half + 2 : 2 * half + 3]], axis=1
@@ -253,15 +252,15 @@
     mean = jnp.broadcast_to(mapped_sum * inverse, (8, channels))
     offset = -mm(split(mean), sym_pair)[0:1]
 
-    row_id = iota((planes, LANES), 0).astype(F32)
+    place = iota((1, LANES), 1).astype(F32)
     spots = []
     for dy_ in (-1, 0, 1):
         for dx_ in (-1, 0, 1):
             near_y, near_x = info[2:3, 0:1] + dy_, info[3:4, 0:1] + dx_
             inside = (near_y >= 0) & (near_y < grid_y) & (near_x >= 0) & (near_x < grid_x)
             spot = jnp.where(inside, near_y * grid_x + near_x, -1.0)
-            near = jnp.sum(jnp.where(row_id == spot, counts, 0.0), axis=0, keepdims=True)
-            spots.append(near[:, 0:1])
+            near = jnp.where(place == spot, counts, 0.0)
+            spots.append(jnp.sum(near, axis=1, keepdims=True))
 
     both = dot(mapped[...], sym_pair[0]) + dot(mapped[...], sym_pair[1]) + offset
     lane_col = iota((wide, channels), 0) - LEFT
@@ -303,7 +302,7 @@
             return tuple(out)
 
         sums = lax.fori_loop(
-            0, height, body, tuple(jnp.zeros((8, LANES), F32) for _ in range(9))
+            0, height, body, tuple(jnp.zeros((8, LANES), F32) for _ in range(9)), unroll=2
         )
         depth.append(
             jnp.concatenate([jnp.sum(s, axis=0, keepdims=True) for s in sums], axis=0)
@@ -343,7 +342,7 @@
             gradient[i, :, part] = value[LEFT : LEFT + width].astype(BF16)
             return carry
 
-        lax.fori_loop(0, height, body, 0)
+        lax.fori_loop(0, height, body, 0, unroll=2)
 
 
 def slide_sum_kernel(rd, terms, shares, small, spread):
@@ -435,6 +434,7 @@
         [up[:, width - RIM :], high, down[:, width - RIM :]], axis=0
     )
     left, right = upward(high_strip, "gx"), downward(low_strip, "gx")
+    scalars = jnp.where(iota((8, LANES), 0) == 0, valid_count[0, 0, 0], labels[0]).astype(F32)
     weights, point, point_turned, info = pl.pallas_call(
         weights_kernel,
         out_shape=(
@@ -443,22 +443,22 @@
             square,
             jax.ShapeDtypeStruct((8, LANES), F32),
         ),
-        in_specs=[SMEM, SMEM] + [VMEM] * 3,
+        in_specs=[VMEM] * 4,
         out_specs=(VMEM,) * 4,
         compiler_params=SMALL,
         name="weights",
-    )(valid_count.reshape(1), labels, low_strip, depth_weight, point_weight)
+    )(scalars, low_strip, depth_weight, point_weight)
 
     halo = (tile, up, down, left, right)
-    chunks = -(-(channels + 5) // planes)
+    chunks = -(-(channels + 6) // planes)
     pixels = (height + 2) * wide
     ext_shape = (height + 2 * RIM, wide, channels)
 
     mapped, packed, ext = pl.pallas_call(
-        functools.partial(forward_kernel, planes),
+        functools.partial(forward_kernel, planes, grid_x),
         out_shape=(
             jax.ShapeDtypeStruct((pixels, channels), BF16),
-            jax.ShapeDtypeStruct((planes, chunks + 1, LANES), F32),
+            jax.ShapeDtypeStruct((planes, 1, chunks * LANES), F32),
             jax.ShapeDtypeStruct(ext_shape, F32),
         ),
         in_specs=[VMEM] * 8,
@@ -475,12 +475,12 @@
 
     packed = pl.pallas_call(
         plane_sum_kernel,
-        out_shape=jax.ShapeDtypeStruct((planes, chunks + 1, LANES), F32),
-        in_specs=[VMEM, VMEM],
+        out_shape=jax.ShapeDtypeStruct((planes, 1, chunks * LANES), F32),
+        in_specs=[VMEM],
         out_specs=VMEM,
         compiler_params=SMALL,
         name="plane_sum",
-    )(info, packed)
+    )(packed)
     gathered = lax.all_to_all(packed, ("gy", "gx"), 0, 0)
 
     rp, rd = channels // slides, 16 // slides

time: 140 us -> 137 us (0.979)
  blocking collectives: 87.4 us -> 85.3 us
    all_to_all x1, blocking collectives: 37.8 us -> 36 us  [per_device(): packed = lax.all_to_all(packed, ('gy', 'gx'), 0, 0)]
  transfers between devices with their start and end apart: 5 -> 5, of which waited for: 3 -> 3; matrix products, arithmetic and copies ran while one was open for 0% -> 0% of each run, Pallas kernels for 2% -> 1%
where the time goes in v8:
time: 137 us
  blocking collectives  85.3 us (62%)
  starting transfers between devices  16.6 us (12%)
  waiting for transfers between devices  15 us (11%)
  Pallas kernels  14.2 us (10%)
  local copies, waits for them, and re-layouts  3.61 us (3%)
  between operations  2.05 us (1%)
    all_to_all x1, blocking collectives, per_device(): packed = lax.all_to_all(packed, ('gy', 'gx'), 0, 0)  36 us
    all_to_all x1, blocking collectives, per_device(): gathered = lax.all_to_all(packed, ('gy', 'gx'), 0, 0)  19.5 us
    all_to_all x1, blocking collectives, per_device(): received = lax.all_to_all(sent, 'slide', 0, 0)  18.5 us
    all_to_all x1, waiting for transfers between devices, per_device(): spread = lax.all_to_all(spread, ('gy', 'gx'), 0, 0)  11.7 us
    all_to_all x1, blocking collectives, per_device(): joined = lax.all_to_all(joined, 'slide', 0, 0)  11.3 us
    ppermute x2, starting transfers between devices, upward(): return lax.ppermute(part, axis, pairs)  8.03 us
    pallas_call x1, Pallas kernels, per_device(): pl.pallas_call(functools.partial(cov_kernel, grid_y, grid_x, slides), out...  7.9 us
    all_to_all x1, starting transfers between devices, per_device(): spread = lax.all_to_all(spread, ('gy', 'gx'), 0, 0)  5.94 us
  transfers between devices with their start and end apart: 5, of which 3 were waited for; matrix products, arithmetic and copies ran while one was open for 0% of the time, Pallas kernels for 1%

profile of v8, /device:TPU:1, one launch (start us, length us, event | category | flops | bytes accessed | tf_op | source)
XLA Modules:
  0.0 136.9 jit_solution(6367126440813033632)
XLA Ops:
  0.6 0.9 slice_bitcast_fusion.1
  1.5 4.8 %collective-permute-start = (bf16[2,64,256]{2,1,0:T(8,128)(2,1)S(1)}, bf16[2,64,256]{2,1,0:T(8,128)(2,1)S(1)}, u32[]{:S(2)}, u32[]{:S(2)}) collective-permute-start(bf16[2,64,256]{2,1,0:T(8,128)(2,1)S(1)} %get-tuple-element.47), channel_id=1, source_target_pairs={{0,8},{8,16},{16,24},{24,32},{32,40},{40,48},{48,56},{56,64},{64,7... | collective-permute-start | bytes 196616 | tf_op jit(solution)/shard_map/ppermute | solution.py:414
  6.4 1.3 collective-permute-start.1
  9.0 1.0 copy-done
  10.1 1.9 %collective-permute-done.1.down = bf16[2,64,256]{2,1,0:T(8,128)(2,1)S(1)} collective-permute-done((bf16[2,64,256]{2,1,0:T(8,128)(2,1)S(1)}, bf16[2,64,256]{2,1,0:T(8,128)(2,1)S(1)}, u32[]{:S(2)}, u32[]{:S(2)}) %collective-permute-start.1) | collective-permute-done | bytes 65568 | tf_op jit(solution)/shard_map/ppermute | solution.py:418
  12.1 3.2 %collective-permute-start.2 = (bf16[20,2,256]{2,1,0:T(2,128)(2,1)S(1)}, bf16[20,2,256]{2,1,0:T(2,128)(2,1)S(1)}, u32[]{:S(2)}, u32[]{:S(2)}) collective-permute-start(bf16[20,2,256]{2,1,0:T(2,128)(2,1)S(1)} %pad_maximum_fusion.1), channel_id=1, source_target_pairs={{0,1},{1,2},{2,3},{3,4},{4,5},{5,6},{6,7},{8,9},{9,10},{10,11},{11... | collective-permute-start | bytes 61448 | tf_op jit(solution)/shard_map/ppermute | solution.py:414
  15.3 1.3 collective-permute-start.3
  16.7 0.9 copy-done.2
  17.6 0.7 copy-done.3
  18.3 0.1 weights.2
  18.4 1.4 %collective-permute-done.3.right = bf16[20,2,256]{2,1,0:T(2,128)(2,1)S(1)} collective-permute-done((bf16[20,2,256]{2,1,0:T(2,128)(2,1)S(1)}, bf16[20,2,256]{2,1,0:T(2,128)(2,1)S(1)}, u32[]{:S(2)}, u32[]{:S(2)}) %collective-permute-start.3) | collective-permute-done | bytes 20512 | tf_op jit(solution)/shard_map/ppermute | solution.py:418
  19.8 2.4 %forward.1 = (bf16[1440,256]{1,0:T(8,128)(2,1)S(1)}, f32[96,1,384]{2,1,0:T(1,128)S(1)}, f32[20,80,256]{2,1,0:T(8,128)S(1)}) custom-call(f32[8,128]{1,0:T(8,128)S(1)} %get-tuple-element.27.info, bf16[16,64,256]{2,1,0:T(8,128)(2,1)S(1)} %get-tuple-element.28.tile, bf16[2,64,256]{2,1,0:T(8,128)(2,1)S(1)} %collective-permute-done.up, ...), custom_call_target="tpu_custom_call" | custom-call | tf_op jit(solution)/shard_map/forward/pallas_call | solution.py:457
  22.3 36.0 %all_to_all.25.terms = f32[96,1,384]{2,1,0:T(1,128)S(1)} all-to-all(f32[96,1,384]{2,1,0:T(1,128)S(1)} %get-tuple-element.32), channel_id=1, replica_groups=mesh['slide'=8,'gy'=12,'gx'=8] {'gy','gx'}, dimensions={0} | all-to-all | bytes 294912 | tf_op jit(solution)/shard_map/all_to_all | solution.py:474
  58.3 0.2 plane_sum.1
  58.4 19.5 %all_to_all.26.gathered = f32[96,1,384]{2,1,0:T(1,128)S(1)} all-to-all(f32[96,1,384]{2,1,0:T(1,128)S(1)} %plane_sum.1), channel_id=1, replica_groups=mesh['slide'=8,'gy'=12,'gx'=8] {'gy','gx'}, dimensions={0} | all-to-all | bytes 294912 | tf_op jit(solution)/shard_map/all_to_all | solution.py:484
  78.0 7.9 %covariance.1 = (bf16[1440,256]{1,0:T(8,128)(2,1)S(1)}, f32[8,56,256]{2,1,0:T(8,128)S(1)}) custom-call(f32[8,128]{1,0:T(8,128)S(1)} %get-tuple-element.27.info, f32[96,1,384]{2,1,0:T(1,128)S(1)} %all_to_all.26.gathered, f32[20,80,256]{2,1,0:T(8,128)S(1)} %get-tuple-element.33.ext, bf16[1440,256]{1,0:T(8,128)(2,1)S(1)} %get-tuple-element.34.mapped, ...), custom_call_target="tpu_custom_call" | custom-call | tf_op jit(solution)/shard_map/covariance/pallas_call | solution.py:488
  85.9 18.5 %all_to_all.27.terms = f32[8,56,256]{2,1,0:T(8,128)S(1)} all-to-all(f32[8,56,256]{2,1,0:T(8,128)S(1)} %get-tuple-element.36), channel_id=1, replica_groups=mesh['slide'=8,'gy'=12,'gx'=8] {'slide'}, dimensions={0} | all-to-all | bytes 917504 | tf_op jit(solution)/shard_map/all_to_all | solution.py:505
  104.3 0.7 slide_sum.1
  105.0 5.9 %all-to-all-start.3 = ((bf16[96,4,128]{2,1,0:T(4,128)(2,1)}), bf16[96,4,128]{2,1,0:T(4,128)(2,1)S(1)}, u32[]{:S(2)}, u32[]{:S(2)}) async-start(bf16[96,4,128]{2,1,0:T(4,128)(2,1)} %get-tuple-element.39), calls=%async_computation.3 | async-start | bytes 196608 | tf_op jit(solution)/shard_map/all_to_all | solution.py:529
  111.0 1.8 %spread.1 = bf16[16,64,256]{2,1,0:T(8,128)(2,1)} custom-call(bf16[1440,256]{1,0:T(8,128)(2,1)S(1)} %get-tuple-element.40.back, f32[9,256]{1,0:T(8,128)S(1)} %get-tuple-element.30.weights), custom_call_target="tpu_custom_call" | custom-call | flops 7372800 | bytes 4194304 | tf_op jit(solution)/shard_map/spread/pallas_call | solution.py:506
  112.8 11.7 %all-to-all-done.3.spread = bf16[96,4,128]{2,1,0:T(4,128)(2,1)S(1)} async-done(((bf16[96,4,128]{2,1,0:T(4,128)(2,1)}), bf16[96,4,128]{2,1,0:T(4,128)(2,1)S(1)}, u32[]{:S(2)}, u32[]{:S(2)}) %all-to-all-start.3) | async-done | bytes 98336 | tf_op jit(solution)/shard_map/all_to_all | solution.py:529
  124.5 0.1 join.1
  124.6 11.3 %all_to_all.28.terms = bf16[8,64,256]{2,1,0:T(8,128)(2,1)S(1)} all-to-all(bf16[8,64,256]{2,1,0:T(8,128)(2,1)S(1)} %join.1), channel_id=1, replica_groups=mesh['slide'=8,'gy'=12,'gx'=8] {'slide'}, dimensions={0} | all-to-all | bytes 524288 | tf_op jit(solution)/shard_map/all_to_all | solution.py:539
  135.9 0.9 finish.1
  (14 shorter events, 0.2 us)
Async XLA Ops:
  1.5 8.5 %collective-permute-start = (bf16[2,64,256]{2,1,0:T(8,128)(2,1)S(1)}, bf16[2,64,256]{2,1,0:T(8,128)(2,1)S(1)}, u32[]{:S(2)}, u32[]{:S(2)}) collective-permute-start(bf16[2,64,256]{2,1,0:T(8,128)(2,1)S(1)} %get-tuple-element.47), channel_id=1, source_target_pairs={{0,8},{8,16},{16,24},{24,32},{32,40},{40,48},{48,56},{56,64},{64,7... | collective-permute-start | bytes 196616 | tf_op jit(solution)/shard_map/ppermute | solution.py:414
  6.4 5.6 %collective-permute-start.1 = (bf16[2,64,256]{2,1,0:T(8,128)(2,1)S(1)}, bf16[2,64,256]{2,1,0:T(8,128)(2,1)S(1)}, u32[]{:S(2)}, u32[]{:S(2)}) collective-permute-start(bf16[2,64,256]{2,1,0:T(8,128)(2,1)S(1)} %get-tuple-element.48), channel_id=1, source_target_pairs={{8,0},{16,8},{24,16},{32,24},{40,32},{48,40},{56,48},{64,56},{72,6... | collective-permute-start | bytes 196616 | tf_op jit(solution)/shard_map/ppermute | solution.py:418
  8.9 1.0 copy-start
  10.0 68.0 %copy-start.1 = (f32[2,256,256]{2,1,0:T(8,128)S(1)}, f32[2,256,256]{2,1,0:T(8,128)}, u32[]{:S(2)}) copy-start(f32[2,256,256]{2,1,0:T(8,128)} %classes.1) | copy-start | bytes 1572868
  12.1 6.3 %collective-permute-start.2 = (bf16[20,2,256]{2,1,0:T(2,128)(2,1)S(1)}, bf16[20,2,256]{2,1,0:T(2,128)(2,1)S(1)}, u32[]{:S(2)}, u32[]{:S(2)}) collective-permute-start(bf16[20,2,256]{2,1,0:T(2,128)(2,1)S(1)} %pad_maximum_fusion.1), channel_id=1, source_target_pairs={{0,1},{1,2},{2,3},{3,4},{4,5},{5,6},{6,7},{8,9},{9,10},{10,11},{11... | collective-permute-start | bytes 61448 | tf_op jit(solution)/shard_map/ppermute | solution.py:414
  15.3 4.5 %collective-permute-start.3 = (bf16[20,2,256]{2,1,0:T(2,128)(2,1)S(1)}, bf16[20,2,256]{2,1,0:T(2,128)(2,1)S(1)}, u32[]{:S(2)}, u32[]{:S(2)}) collective-permute-start(bf16[20,2,256]{2,1,0:T(2,128)(2,1)S(1)} %pad_maximum_fusion.strip), channel_id=1, source_target_pairs={{1,0},{2,1},{3,2},{4,3},{5,4},{6,5},{7,6},{9,8},{10,9},{11,10},{12... | collective-permute-start | bytes 61448 | tf_op jit(solution)/shard_map/ppermute | solution.py:418
  16.7 0.9 copy-start.2
  17.6 0.7 copy-start.3
  105.0 19.5 %all-to-all-start.3 = ((bf16[96,4,128]{2,1,0:T(4,128)(2,1)}), bf16[96,4,128]{2,1,0:T(4,128)(2,1)S(1)}, u32[]{:S(2)}, u32[]{:S(2)}) async-start(bf16[96,4,128]{2,1,0:T(4,128)(2,1)} %get-tuple-element.39), calls=%async_computation.3 | async-start | bytes 196608 | tf_op jit(solution)/shard_map/all_to_all | solution.py:529

commit v9 on v8

--- a/solution.py
+++ b/solution.py
@@ -87,14 +87,13 @@
     ext[:, LEFT + width : LEFT + width + RIM, :] = right[...].astype(F32)
 
 
-def load_kernel(tile_in, tile, low, high):
+def load_kernel(
+    scalars, tile_in, weights, point, tile, low, high, taps, mixing, turned, info
+):
     width = tile.shape[1]
     tile[...] = tile_in[...]
     low[...] = tile_in[:, :RIM, :]
     high[...] = tile_in[:, width - RIM :, :]
-
-
-def weights_kernel(scalars, strip, weights, point, taps, mixing, turned, info):
     taps[...] = jnp.concatenate([weights[a].astype(F32) for a in range(3)], axis=0)
     mixing[...] = point[...]
     turned[...] = point[...].astype(F32).T.astype(BF16)
@@ -196,7 +195,6 @@
         jnp.concatenate([mixing_turned, mixing_turned], axis=1),
         jnp.concatenate(moved_pair, axis=0),
     )
-    sigma = 0.5 * (sigma + sigma.T)
     eye = iota((channels, channels), 0) == iota((channels, channels), 1)
     trace = total(jnp.where(eye, sigma, 0.0))
     start = sigma * (1.0 / trace)
@@ -242,10 +240,8 @@
 
     level = 0.5 * total(toward * ymat) - total(dy * start)
     slant = (dy + jnp.where(eye, level, 0.0)) * (slope / root)
-    slant = 0.5 * (slant + slant.T)
     point_term = mm(moved_pair, split(slant))
     class_term = slope * pooled
-    class_term = 0.5 * (class_term + class_term.T)
 
     symmetric = slant * inverse
     sym_pair = split(symmetric)
@@ -420,34 +416,29 @@
     square = jax.ShapeDtypeStruct((channels, channels), BF16)
     strip = jax.ShapeDtypeStruct((height, RIM, channels), BF16)
     up, down = upward(tile[height - RIM :], "gy"), downward(tile[:RIM], "gy")
-    tile, low, high = pl.pallas_call(
+    scalars = jnp.where(iota((8, LANES), 0) == 0, valid_count[0, 0, 0], labels[0]).astype(F32)
+    tile, low, high, weights, point, point_turned, info = pl.pallas_call(
         load_kernel,
-        out_shape=(jax.ShapeDtypeStruct(tile.shape, BF16), strip, strip),
-        in_specs=[VMEM],
-        out_specs=(VMEM,) * 3,
-        compiler_params=SMALL,
-        name="load",
-    )(tile)
-
-    low_strip = jnp.concatenate([up[:, :RIM], low, down[:, :RIM]], axis=0)
-    high_strip = jnp.concatenate(
-        [up[:, width - RIM :], high, down[:, width - RIM :]], axis=0
-    )
-    left, right = upward(high_strip, "gx"), downward(low_strip, "gx")
-    scalars = jnp.where(iota((8, LANES), 0) == 0, valid_count[0, 0, 0], labels[0]).astype(F32)
-    weights, point, point_turned, info = pl.pallas_call(
-        weights_kernel,
         out_shape=(
+            jax.ShapeDtypeStruct(tile.shape, BF16),
+            strip,
+            strip,
             jax.ShapeDtypeStruct((9, channels), F32),
             square,
             square,
             jax.ShapeDtypeStruct((8, LANES), F32),
         ),
         in_specs=[VMEM] * 4,
-        out_specs=(VMEM,) * 4,
+        out_specs=(VMEM,) * 7,
         compiler_params=SMALL,
-        name="weights",
-    )(scalars, low_strip, depth_weight, point_weight)
+        name="load",
+    )(scalars, tile, depth_weight, point_weight)
+
+    low_strip = jnp.concatenate([up[:, :RIM], low, down[:, :RIM]], axis=0)
+    high_strip = jnp.concatenate(
+        [up[:, width - RIM :], high, down[:, width - RIM :]], axis=0
+    )
+    left, right = upward(high_strip, "gx"), downward(low_strip, "gx")
 
     halo = (tile, up, down, left, right)
     chunks = -(-(channels + 6) // planes)

time: 137 us -> 138 us (level)
  waiting for transfers between devices: 15 us -> 12.6 us
  blocking collectives: 85.3 us -> 86.9 us
  starting transfers between devices: 16.6 us -> 18 us
    ppermute x2, waiting for transfers between devices: 3.35 us -> 0.01 us  [downward(): return lax.ppermute(part, axis, pairs)]
    all_to_all x1, blocking collectives: 36 us -> 38 us  [per_device(): packed = lax.all_to_all(packed, ('gy', 'gx'), 0, 0)]
    ppermute x2, starting transfers between devices: 8.03 us -> 9.44 us  [upward(): return lax.ppermute(part, axis, pairs)]
  transfers between devices with their start and end apart: 5 -> 5, of which waited for: 3 -> 2; matrix products, arithmetic and copies ran while one was open for 0% -> 0% of each run, Pallas kernels for 1% -> 1%
where the time goes in v9:
time: 138 us; the launch traced here: 137 us
  blocking collectives  86.9 us (63%)
  starting transfers between devices  18 us (13%)
  Pallas kernels  13.9 us (10%)
  waiting for transfers between devices  12.6 us (9%)
  local copies, waits for them, and re-layouts  3.61 us (3%)
  between operations  2.05 us (1%)
    all_to_all x1, blocking collectives, per_device(): packed = lax.all_to_all(packed, ('gy', 'gx'), 0, 0)  38 us
    all_to_all x1, blocking collectives, per_device(): gathered = lax.all_to_all(packed, ('gy', 'gx'), 0, 0)  19.6 us
    all_to_all x1, blocking collectives, per_device(): received = lax.all_to_all(sent, 'slide', 0, 0)  18 us
    all_to_all x1, waiting for transfers between devices, per_device(): spread = lax.all_to_all(spread, ('gy', 'gx'), 0, 0)  11.7 us
    all_to_all x1, blocking collectives, per_device(): joined = lax.all_to_all(joined, 'slide', 0, 0)  11.3 us
    ppermute x2, starting transfers between devices, upward(): return lax.ppermute(part, axis, pairs)  9.44 us
    pallas_call x1, Pallas kernels, per_device(): pl.pallas_call(functools.partial(cov_kernel, grid_y, grid_x, slides), out...  7.69 us
    all_to_all x1, starting transfers between devices, per_device(): spread = lax.all_to_all(spread, ('gy', 'gx'), 0, 0)  5.94 us
  transfers between devices with their start and end apart: 5, of which 2 were waited for; matrix products, arithmetic and copies ran while one was open for 0% of the time, Pallas kernels for 1%

profile of v9, /device:TPU:1, one launch (start us, length us, event | category | flops | bytes accessed | tf_op | source)
XLA Modules:
  0.0 137.1 jit_solution(13765630184494159820)
XLA Ops:
  0.6 0.9 slice_bitcast_fusion
  1.5 1.3 collective-permute-start.1
  2.8 5.5 %collective-permute-start = (bf16[2,64,256]{2,1,0:T(8,128)(2,1)S(1)}, bf16[2,64,256]{2,1,0:T(8,128)(2,1)S(1)}, u32[]{:S(2)}, u32[]{:S(2)}) collective-permute-start(bf16[2,64,256]{2,1,0:T(8,128)(2,1)S(1)} %get-tuple-element.48), channel_id=1, source_target_pairs={{0,8},{8,16},{16,24},{24,32},{32,40},{40,48},{48,56},{56,64},{64,7... | collective-permute-start | bytes 196616 | tf_op jit(solution)/shard_map/ppermute | solution.py:410
  9.6 0.1 iota.7.scalars
  9.7 1.0 copy-done
  10.7 0.9 copy-done.2
  11.6 0.7 copy-done.3
  12.3 0.1 load.1
  12.5 1.3 collective-permute-start.3
  13.8 4.0 %collective-permute-start.2 = (bf16[20,2,256]{2,1,0:T(2,128)(2,1)S(1)}, bf16[20,2,256]{2,1,0:T(2,128)(2,1)S(1)}, u32[]{:S(2)}, u32[]{:S(2)}) collective-permute-start(bf16[20,2,256]{2,1,0:T(2,128)(2,1)S(1)} %pad_maximum_fusion), channel_id=1, source_target_pairs={{0,1},{1,2},{2,3},{3,4},{4,5},{5,6},{6,7},{8,9},{9,10},{10,11},{11... | collective-permute-start | bytes 61448 | tf_op jit(solution)/shard_map/ppermute | solution.py:410
  17.8 0.9 collective-permute-done.2.left
  18.7 2.4 %forward.1 = (bf16[1440,256]{1,0:T(8,128)(2,1)S(1)}, f32[96,1,384]{2,1,0:T(1,128)S(1)}, f32[20,80,256]{2,1,0:T(8,128)S(1)}) custom-call(f32[8,128]{1,0:T(8,128)S(1)} %get-tuple-element.26.info, bf16[16,64,256]{2,1,0:T(8,128)(2,1)S(1)} %get-tuple-element.27.tile, bf16[2,64,256]{2,1,0:T(8,128)(2,1)S(1)} %collective-permute-done.up, ...), custom_call_target="tpu_custom_call" | custom-call | tf_op jit(solution)/shard_map/forward/pallas_call | solution.py:448
  21.2 38.0 %all_to_all.25.terms = f32[96,1,384]{2,1,0:T(1,128)S(1)} all-to-all(f32[96,1,384]{2,1,0:T(1,128)S(1)} %get-tuple-element.32), channel_id=1, replica_groups=mesh['slide'=8,'gy'=12,'gx'=8] {'gy','gx'}, dimensions={0} | all-to-all | bytes 294912 | tf_op jit(solution)/shard_map/all_to_all | solution.py:465
  59.1 0.2 plane_sum.1
  59.3 19.6 %all_to_all.26.gathered = f32[96,1,384]{2,1,0:T(1,128)S(1)} all-to-all(f32[96,1,384]{2,1,0:T(1,128)S(1)} %plane_sum.1), channel_id=1, replica_groups=mesh['slide'=8,'gy'=12,'gx'=8] {'gy','gx'}, dimensions={0} | all-to-all | bytes 294912 | tf_op jit(solution)/shard_map/all_to_all | solution.py:475
  78.9 7.7 %covariance.1 = (bf16[1440,256]{1,0:T(8,128)(2,1)S(1)}, f32[8,56,256]{2,1,0:T(8,128)S(1)}) custom-call(f32[8,128]{1,0:T(8,128)S(1)} %get-tuple-element.26.info, f32[96,1,384]{2,1,0:T(1,128)S(1)} %all_to_all.26.gathered, f32[20,80,256]{2,1,0:T(8,128)S(1)} %get-tuple-element.33.ext, bf16[1440,256]{1,0:T(8,128)(2,1)S(1)} %get-tuple-element.34.mapped, ...), custom_call_target="tpu_custom_call" | custom-call | tf_op jit(solution)/shard_map/covariance/pallas_call | solution.py:479
  86.6 18.0 %all_to_all.27.terms = f32[8,56,256]{2,1,0:T(8,128)S(1)} all-to-all(f32[8,56,256]{2,1,0:T(8,128)S(1)} %get-tuple-element.36), channel_id=1, replica_groups=mesh['slide'=8,'gy'=12,'gx'=8] {'slide'}, dimensions={0} | all-to-all | bytes 917504 | tf_op jit(solution)/shard_map/all_to_all | solution.py:496
  104.6 0.7 slide_sum.1
  105.3 5.9 %all-to-all-start.3 = ((bf16[96,4,128]{2,1,0:T(4,128)(2,1)}), bf16[96,4,128]{2,1,0:T(4,128)(2,1)S(1)}, u32[]{:S(2)}, u32[]{:S(2)}) async-start(bf16[96,4,128]{2,1,0:T(4,128)(2,1)} %get-tuple-element.39), calls=%async_computation.3 | async-start | bytes 196608 | tf_op jit(solution)/shard_map/all_to_all | solution.py:520
  111.2 1.8 %spread.1 = bf16[16,64,256]{2,1,0:T(8,128)(2,1)} custom-call(bf16[1440,256]{1,0:T(8,128)(2,1)S(1)} %get-tuple-element.40.back, f32[9,256]{1,0:T(8,128)S(1)} %get-tuple-element.30.weights), custom_call_target="tpu_custom_call" | custom-call | flops 7372800 | bytes 4194304 | tf_op jit(solution)/shard_map/spread/pallas_call | solution.py:497
  113.1 11.7 %all-to-all-done.3.spread = bf16[96,4,128]{2,1,0:T(4,128)(2,1)S(1)} async-done(((bf16[96,4,128]{2,1,0:T(4,128)(2,1)}), bf16[96,4,128]{2,1,0:T(4,128)(2,1)S(1)}, u32[]{:S(2)}, u32[]{:S(2)}) %all-to-all-start.3) | async-done | bytes 98336 | tf_op jit(solution)/shard_map/all_to_all | solution.py:520
  124.7 0.1 join.1
  124.9 11.3 %all_to_all.28.terms = bf16[8,64,256]{2,1,0:T(8,128)(2,1)S(1)} all-to-all(bf16[8,64,256]{2,1,0:T(8,128)(2,1)S(1)} %join.1), channel_id=1, replica_groups=mesh['slide'=8,'gy'=12,'gx'=8] {'slide'}, dimensions={0} | all-to-all | bytes 524288 | tf_op jit(solution)/shard_map/all_to_all | solution.py:530
  136.2 0.9 finish.1
  (13 shorter events, 0.1 us)
Async XLA Ops:
  1.5 10.9 %collective-permute-start.1 = (bf16[2,64,256]{2,1,0:T(8,128)(2,1)S(1)}, bf16[2,64,256]{2,1,0:T(8,128)(2,1)S(1)}, u32[]{:S(2)}, u32[]{:S(2)}) collective-permute-start(bf16[2,64,256]{2,1,0:T(8,128)(2,1)S(1)} %get-tuple-element.47), channel_id=1, source_target_pairs={{8,0},{16,8},{24,16},{32,24},{40,32},{48,40},{56,48},{64,56},{72,6... | collective-permute-start | bytes 196616 | tf_op jit(solution)/shard_map/ppermute | solution.py:414
  2.8 9.6 %collective-permute-start = (bf16[2,64,256]{2,1,0:T(8,128)(2,1)S(1)}, bf16[2,64,256]{2,1,0:T(8,128)(2,1)S(1)}, u32[]{:S(2)}, u32[]{:S(2)}) collective-permute-start(bf16[2,64,256]{2,1,0:T(8,128)(2,1)S(1)} %get-tuple-element.48), channel_id=1, source_target_pairs={{0,8},{8,16},{16,24},{24,32},{32,40},{40,48},{48,56},{56,64},{64,7... | collective-permute-start | bytes 196616 | tf_op jit(solution)/shard_map/ppermute | solution.py:410
  9.7 1.0 copy-start
  10.7 0.9 copy-start.2
  11.6 0.7 copy-start.3
  12.3 66.6 %copy-start.1 = (f32[2,256,256]{2,1,0:T(8,128)S(1)}, f32[2,256,256]{2,1,0:T(8,128)}, u32[]{:S(2)}) copy-start(f32[2,256,256]{2,1,0:T(8,128)} %classes.1) | copy-start | bytes 1572868
  12.5 5.3 %collective-permute-start.3 = (bf16[20,2,256]{2,1,0:T(2,128)(2,1)S(1)}, bf16[20,2,256]{2,1,0:T(2,128)(2,1)S(1)}, u32[]{:S(2)}, u32[]{:S(2)}) collective-permute-start(bf16[20,2,256]{2,1,0:T(2,128)(2,1)S(1)} %pad_maximum_fusion.1), channel_id=1, source_target_pairs={{1,0},{2,1},{3,2},{4,3},{5,4},{6,5},{7,6},{9,8},{10,9},{11,10},{12... | collective-permute-start | bytes 61448 | tf_op jit(solution)/shard_map/ppermute | solution.py:414
  13.8 4.9 %collective-permute-start.2 = (bf16[20,2,256]{2,1,0:T(2,128)(2,1)S(1)}, bf16[20,2,256]{2,1,0:T(2,128)(2,1)S(1)}, u32[]{:S(2)}, u32[]{:S(2)}) collective-permute-start(bf16[20,2,256]{2,1,0:T(2,128)(2,1)S(1)} %pad_maximum_fusion), channel_id=1, source_target_pairs={{0,1},{1,2},{2,3},{3,4},{4,5},{5,6},{6,7},{8,9},{9,10},{10,11},{11... | collective-permute-start | bytes 61448 | tf_op jit(solution)/shard_map/ppermute | solution.py:410
  105.3 19.5 %all-to-all-start.3 = ((bf16[96,4,128]{2,1,0:T(4,128)(2,1)}), bf16[96,4,128]{2,1,0:T(4,128)(2,1)S(1)}, u32[]{:S(2)}, u32[]{:S(2)}) async-start(bf16[96,4,128]{2,1,0:T(4,128)(2,1)} %get-tuple-element.39), calls=%async_computation.3 | async-start | bytes 196608 | tf_op jit(solution)/shard_map/all_to_all | solution.py:520

commit v10 on v9

--- a/solution.py
+++ b/solution.py
@@ -14,6 +14,7 @@
 F32 = jnp.float32
 BF16 = jnp.bfloat16
 VMEM = pl.BlockSpec(memory_space=pltpu.VMEM)
+SMEM = pl.BlockSpec(memory_space=pltpu.SMEM)
 HBM = pl.BlockSpec(memory_space=pltpu.HBM)
 PARAMS = pltpu.CompilerParams(vmem_limit_bytes=16 * 1024 * 1024)
 SMALL = pltpu.CompilerParams(vmem_limit_bytes=4 * 1024 * 1024)
@@ -88,7 +89,7 @@
 
 
 def load_kernel(
-    scalars, tile_in, weights, point, tile, low, high, taps, mixing, turned, info
+    tile_in, weights, point, tile, low, high, taps, mixing, turned
 ):
     width = tile.shape[1]
     tile[...] = tile_in[...]
@@ -97,11 +98,14 @@
     taps[...] = jnp.concatenate([weights[a].astype(F32) for a in range(3)], axis=0)
     mixing[...] = point[...]
     turned[...] = point[...].astype(F32).T.astype(BF16)
+
+
+def info_kernel(count, label, strip, info):
     row = iota(info.shape, 0)
-    value = scalars[...]
-    for k, axis in enumerate(("gy", "gx", "slide")):
-        position = lax.axis_index(axis).astype(jnp.int32).astype(F32)
-        value = jnp.where(row == k + 2, position, value)
+    value = jnp.zeros(info.shape, F32)
+    scalars = [count[0], label[0]] + [lax.axis_index(axis) for axis in ("gy", "gx", "slide")]
+    for k, scalar in enumerate(scalars):
+        value = jnp.where(row == k, scalar.astype(jnp.int32).astype(F32), value)
     info[...] = value
 
 
@@ -416,8 +420,7 @@
     square = jax.ShapeDtypeStruct((channels, channels), BF16)
     strip = jax.ShapeDtypeStruct((height, RIM, channels), BF16)
     up, down = upward(tile[height - RIM :], "gy"), downward(tile[:RIM], "gy")
-    scalars = jnp.where(iota((8, LANES), 0) == 0, valid_count[0, 0, 0], labels[0]).astype(F32)
-    tile, low, high, weights, point, point_turned, info = pl.pallas_call(
+    tile, low, high, weights, point, point_turned = pl.pallas_call(
         load_kernel,
         out_shape=(
             jax.ShapeDtypeStruct(tile.shape, BF16),
@@ -426,19 +429,26 @@
             jax.ShapeDtypeStruct((9, channels), F32),
             square,
             square,
-            jax.ShapeDtypeStruct((8, LANES), F32),
         ),
-        in_specs=[VMEM] * 4,
-        out_specs=(VMEM,) * 7,
+        in_specs=[VMEM] * 3,
+        out_specs=(VMEM,) * 6,
         compiler_params=SMALL,
         name="load",
-    )(scalars, tile, depth_weight, point_weight)
+    )(tile, depth_weight, point_weight)
 
     low_strip = jnp.concatenate([up[:, :RIM], low, down[:, :RIM]], axis=0)
     high_strip = jnp.concatenate(
         [up[:, width - RIM :], high, down[:, width - RIM :]], axis=0
     )
     left, right = upward(high_strip, "gx"), downward(low_strip, "gx")
+    info = pl.pallas_call(
+        info_kernel,
+        out_shape=jax.ShapeDtypeStruct((8, LANES), F32),
+        in_specs=[SMEM, SMEM, VMEM],
+        out_specs=VMEM,
+        compiler_params=SMALL,
+        name="info",
+    )(valid_count.reshape(1), labels, low_strip)
 
     halo = (tile, up, down, left, right)
     chunks = -(-(channels + 6) // planes)

time: 138 us -> 137 us (level)
  waiting for transfers between devices: 12.6 us -> 15.2 us
  blocking collectives: 86.9 us -> 85.3 us
  starting transfers between devices: 18 us -> 16.6 us
    ppermute x2, waiting for transfers between devices: 0.01 us -> 3.47 us  [downward(): return lax.ppermute(part, axis, pairs)]
    all_to_all x1, blocking collectives: 38 us -> 35.6 us  [per_device(): packed = lax.all_to_all(packed, ('gy', 'gx'), 0, 0)]
    ppermute x2, starting transfers between devices: 9.44 us -> 8.03 us  [upward(): return lax.ppermute(part, axis, pairs)]
  transfers between devices with their start and end apart: 5 -> 5, of which waited for: 2 -> 3; matrix products, arithmetic and copies ran while one was open for 0% -> 0% of each run, Pallas kernels for 1% -> 1%
where the time goes in v10:
time: 137 us
  blocking collectives  85.3 us (62%)
  starting transfers between devices  16.6 us (12%)
  waiting for transfers between devices  15.2 us (11%)
  Pallas kernels  14 us (10%)
  local copies, waits for them, and re-layouts  3.53 us (3%)
  between operations  2.04 us (1%)
    all_to_all x1, blocking collectives, per_device(): packed = lax.all_to_all(packed, ('gy', 'gx'), 0, 0)  35.6 us
    all_to_all x1, blocking collectives, per_device(): gathered = lax.all_to_all(packed, ('gy', 'gx'), 0, 0)  19.6 us
    all_to_all x1, blocking collectives, per_device(): received = lax.all_to_all(sent, 'slide', 0, 0)  18.8 us
    all_to_all x1, waiting for transfers between devices, per_device(): spread = lax.all_to_all(spread, ('gy', 'gx'), 0, 0)  11.7 us
    all_to_all x1, blocking collectives, per_device(): joined = lax.all_to_all(joined, 'slide', 0, 0)  11.3 us
    ppermute x2, starting transfers between devices, upward(): return lax.ppermute(part, axis, pairs)  8.03 us
    pallas_call x1, Pallas kernels, per_device(): pl.pallas_call(functools.partial(cov_kernel, grid_y, grid_x, slides), out...  7.69 us
    all_to_all x1, starting transfers between devices, per_device(): spread = lax.all_to_all(spread, ('gy', 'gx'), 0, 0)  5.94 us
  transfers between devices with their start and end apart: 5, of which 3 were waited for; matrix products, arithmetic and copies ran while one was open for 0% of the time, Pallas kernels for 1%

profile of v10, /device:TPU:1, one launch (start us, length us, event | category | flops | bytes accessed | tf_op | source)
XLA Modules:
  0.0 136.7 jit_solution(7824771614943958283)
XLA Ops:
  0.6 0.9 slice_bitcast_fusion.1
  1.5 4.8 %collective-permute-start = (bf16[2,64,256]{2,1,0:T(8,128)(2,1)S(1)}, bf16[2,64,256]{2,1,0:T(8,128)(2,1)S(1)}, u32[]{:S(2)}, u32[]{:S(2)}) collective-permute-start(bf16[2,64,256]{2,1,0:T(8,128)(2,1)S(1)} %get-tuple-element.45), channel_id=1, source_target_pairs={{0,8},{8,16},{16,24},{24,32},{32,40},{40,48},{48,56},{56,64},{64,7... | collective-permute-start | bytes 196616 | tf_op jit(solution)/shard_map/ppermute | solution.py:414
  6.4 1.3 collective-permute-start.1
  7.7 1.0 copy-done
  8.7 0.9 copy-done.2
  9.6 0.7 copy-done.3
  10.3 0.1 load.1
  10.4 1.6 %collective-permute-done.1.down = bf16[2,64,256]{2,1,0:T(8,128)(2,1)S(1)} collective-permute-done((bf16[2,64,256]{2,1,0:T(8,128)(2,1)S(1)}, bf16[2,64,256]{2,1,0:T(8,128)(2,1)S(1)}, u32[]{:S(2)}, u32[]{:S(2)}) %collective-permute-start.1) | collective-permute-done | bytes 65568 | tf_op jit(solution)/shard_map/ppermute | solution.py:418
  12.1 3.2 %collective-permute-start.2 = (bf16[20,2,256]{2,1,0:T(2,128)(2,1)S(1)}, bf16[20,2,256]{2,1,0:T(2,128)(2,1)S(1)}, u32[]{:S(2)}, u32[]{:S(2)}) collective-permute-start(bf16[20,2,256]{2,1,0:T(2,128)(2,1)S(1)} %pad_maximum_fusion.1), channel_id=1, source_target_pairs={{0,1},{1,2},{2,3},{3,4},{4,5},{5,6},{6,7},{8,9},{9,10},{10,11},{11... | collective-permute-start | bytes 61448 | tf_op jit(solution)/shard_map/ppermute | solution.py:414
  15.3 1.3 collective-permute-start.3
  17.9 1.9 %collective-permute-done.3.right = bf16[20,2,256]{2,1,0:T(2,128)(2,1)S(1)} collective-permute-done((bf16[20,2,256]{2,1,0:T(2,128)(2,1)S(1)}, bf16[20,2,256]{2,1,0:T(2,128)(2,1)S(1)}, u32[]{:S(2)}, u32[]{:S(2)}) %collective-permute-start.3) | collective-permute-done | bytes 20512 | tf_op jit(solution)/shard_map/ppermute | solution.py:418
  19.8 2.4 %forward.1 = (bf16[1440,256]{1,0:T(8,128)(2,1)S(1)}, f32[96,1,384]{2,1,0:T(1,128)S(1)}, f32[20,80,256]{2,1,0:T(8,128)S(1)}) custom-call(f32[8,128]{1,0:T(8,128)S(1)} %info.1, bf16[16,64,256]{2,1,0:T(8,128)(2,1)S(1)} %get-tuple-element.26.tile, bf16[2,64,256]{2,1,0:T(8,128)(2,1)S(1)} %collective-permute-done.up, ...), custom_call_target="tpu_custom_call" | custom-call | tf_op jit(solution)/shard_map/forward/pallas_call | solution.py:458
  22.3 35.6 %all_to_all.25.terms = f32[96,1,384]{2,1,0:T(1,128)S(1)} all-to-all(f32[96,1,384]{2,1,0:T(1,128)S(1)} %get-tuple-element.30), channel_id=1, replica_groups=mesh['slide'=8,'gy'=12,'gx'=8] {'gy','gx'}, dimensions={0} | all-to-all | bytes 294912 | tf_op jit(solution)/shard_map/all_to_all | solution.py:475
  57.9 0.2 plane_sum.1
  58.0 19.6 %all_to_all.26.gathered = f32[96,1,384]{2,1,0:T(1,128)S(1)} all-to-all(f32[96,1,384]{2,1,0:T(1,128)S(1)} %plane_sum.1), channel_id=1, replica_groups=mesh['slide'=8,'gy'=12,'gx'=8] {'gy','gx'}, dimensions={0} | all-to-all | bytes 294912 | tf_op jit(solution)/shard_map/all_to_all | solution.py:485
  77.6 7.7 %covariance.1 = (bf16[1440,256]{1,0:T(8,128)(2,1)S(1)}, f32[8,56,256]{2,1,0:T(8,128)S(1)}) custom-call(f32[8,128]{1,0:T(8,128)S(1)} %info.1, f32[96,1,384]{2,1,0:T(1,128)S(1)} %all_to_all.26.gathered, f32[20,80,256]{2,1,0:T(8,128)S(1)} %get-tuple-element.31.ext, bf16[1440,256]{1,0:T(8,128)(2,1)S(1)} %get-tuple-element.32.mapped, ...), custom_call_target="tpu_custom_call" | custom-call | tf_op jit(solution)/shard_map/covariance/pallas_call | solution.py:489
  85.3 18.8 %all_to_all.27.terms = f32[8,56,256]{2,1,0:T(8,128)S(1)} all-to-all(f32[8,56,256]{2,1,0:T(8,128)S(1)} %get-tuple-element.34), channel_id=1, replica_groups=mesh['slide'=8,'gy'=12,'gx'=8] {'slide'}, dimensions={0} | all-to-all | bytes 917504 | tf_op jit(solution)/shard_map/all_to_all | solution.py:506
  104.2 0.7 slide_sum.1
  104.8 5.9 %all-to-all-start.3 = ((bf16[96,4,128]{2,1,0:T(4,128)(2,1)}), bf16[96,4,128]{2,1,0:T(4,128)(2,1)S(1)}, u32[]{:S(2)}, u32[]{:S(2)}) async-start(bf16[96,4,128]{2,1,0:T(4,128)(2,1)} %get-tuple-element.37), calls=%async_computation.3 | async-start | bytes 196608 | tf_op jit(solution)/shard_map/all_to_all | solution.py:530
  110.8 1.8 %spread.1 = bf16[16,64,256]{2,1,0:T(8,128)(2,1)} custom-call(bf16[1440,256]{1,0:T(8,128)(2,1)S(1)} %get-tuple-element.38.back, f32[9,256]{1,0:T(8,128)S(1)} %get-tuple-element.28.weights), custom_call_target="tpu_custom_call" | custom-call | flops 7372800 | bytes 4194304 | tf_op jit(solution)/shard_map/spread/pallas_call | solution.py:507
  112.6 11.7 %all-to-all-done.3.spread = bf16[96,4,128]{2,1,0:T(4,128)(2,1)S(1)} async-done(((bf16[96,4,128]{2,1,0:T(4,128)(2,1)}), bf16[96,4,128]{2,1,0:T(4,128)(2,1)S(1)}, u32[]{:S(2)}, u32[]{:S(2)}) %all-to-all-start.3) | async-done | bytes 98336 | tf_op jit(solution)/shard_map/all_to_all | solution.py:530
  124.3 0.1 join.1
  124.4 11.3 %all_to_all.28.terms = bf16[8,64,256]{2,1,0:T(8,128)(2,1)S(1)} all-to-all(bf16[8,64,256]{2,1,0:T(8,128)(2,1)S(1)} %join.1), channel_id=1, replica_groups=mesh['slide'=8,'gy'=12,'gx'=8] {'slide'}, dimensions={0} | all-to-all | bytes 524288 | tf_op jit(solution)/shard_map/all_to_all | solution.py:540
  135.7 0.9 finish.1
  (12 shorter events, 0.1 us)
Async XLA Ops:
  1.5 8.9 %collective-permute-start = (bf16[2,64,256]{2,1,0:T(8,128)(2,1)S(1)}, bf16[2,64,256]{2,1,0:T(8,128)(2,1)S(1)}, u32[]{:S(2)}, u32[]{:S(2)}) collective-permute-start(bf16[2,64,256]{2,1,0:T(8,128)(2,1)S(1)} %get-tuple-element.45), channel_id=1, source_target_pairs={{0,8},{8,16},{16,24},{24,32},{32,40},{40,48},{48,56},{56,64},{64,7... | collective-permute-start | bytes 196616 | tf_op jit(solution)/shard_map/ppermute | solution.py:414
  6.4 5.6 %collective-permute-start.1 = (bf16[2,64,256]{2,1,0:T(8,128)(2,1)S(1)}, bf16[2,64,256]{2,1,0:T(8,128)(2,1)S(1)}, u32[]{:S(2)}, u32[]{:S(2)}) collective-permute-start(bf16[2,64,256]{2,1,0:T(8,128)(2,1)S(1)} %get-tuple-element.46), channel_id=1, source_target_pairs={{8,0},{16,8},{24,16},{32,24},{40,32},{48,40},{56,48},{64,56},{72,6... | collective-permute-start | bytes 196616 | tf_op jit(solution)/shard_map/ppermute | solution.py:418
  7.7 1.0 copy-start
  8.7 0.9 copy-start.2
  9.6 0.7 copy-start.3
  10.3 67.3 %copy-start.1 = (f32[2,256,256]{2,1,0:T(8,128)S(1)}, f32[2,256,256]{2,1,0:T(8,128)}, u32[]{:S(2)}) copy-start(f32[2,256,256]{2,1,0:T(8,128)} %classes.1) | copy-start | bytes 1572868
  12.1 5.9 %collective-permute-start.2 = (bf16[20,2,256]{2,1,0:T(2,128)(2,1)S(1)}, bf16[20,2,256]{2,1,0:T(2,128)(2,1)S(1)}, u32[]{:S(2)}, u32[]{:S(2)}) collective-permute-start(bf16[20,2,256]{2,1,0:T(2,128)(2,1)S(1)} %pad_maximum_fusion.1), channel_id=1, source_target_pairs={{0,1},{1,2},{2,3},{3,4},{4,5},{5,6},{6,7},{8,9},{9,10},{10,11},{11... | collective-permute-start | bytes 61448 | tf_op jit(solution)/shard_map/ppermute | solution.py:414
  15.3 4.5 %collective-permute-start.3 = (bf16[20,2,256]{2,1,0:T(2,128)(2,1)S(1)}, bf16[20,2,256]{2,1,0:T(2,128)(2,1)S(1)}, u32[]{:S(2)}, u32[]{:S(2)}) collective-permute-start(bf16[20,2,256]{2,1,0:T(2,128)(2,1)S(1)} %pad_maximum_fusion.strip), channel_id=1, source_target_pairs={{1,0},{2,1},{3,2},{4,3},{5,4},{6,5},{7,6},{9,8},{10,9},{11,10},{12... | collective-permute-start | bytes 61448 | tf_op jit(solution)/shard_map/ppermute | solution.py:418
  104.8 19.5 %all-to-all-start.3 = ((bf16[96,4,128]{2,1,0:T(4,128)(2,1)}), bf16[96,4,128]{2,1,0:T(4,128)(2,1)S(1)}, u32[]{:S(2)}, u32[]{:S(2)}) async-start(bf16[96,4,128]{2,1,0:T(4,128)(2,1)} %get-tuple-element.37), calls=%async_computation.3 | async-start | bytes 196608 | tf_op jit(solution)/shard_map/all_to_all | solution.py:530
